TPU v7x, 32 devices: a whole 2x2x4 slice. The times are simulated.
32 devices in a mesh: pipe: 2 (over x), expert: 16 (over z, y, core).
Axes of the slice: x: 2, y: 2, z: 4, core: 2. Of those that a mesh axis runs over, the one named last changes fastest.
Arguments:
- inputs: bfloat16 [2, 2048, 2048], P('pipe', 'expert'), may hold values from -6 to 6
- out_grads: bfloat16 [2, 2048, 2048], P('pipe', 'expert'), may hold values from -6 to 6
- expert_ids: int32 [2, 2048, 8], P('pipe', 'expert'), may hold values from 0 to 127, all different within a row
- gate_values: float32 [2, 2048, 8], P('pipe', 'expert'), may hold values from 0.2 to 1
- w_gate: bfloat16 [2, 2048, 4096], P('pipe', None, 'expert'), may hold values from -0.125 to 0.125
- w_up: bfloat16 [2, 2048, 4096], P('pipe', None, 'expert'), may hold values from -0.125 to 0.125
- w_down: bfloat16 [2, 4096, 2048], P('pipe', 'expert'), may hold values from -0.1875 to 0.1875
Outputs:
- prev_grads: bfloat16 [2, 2048, 2048], P('pipe', 'expert')
- gate_grads: float32 [2, 2048, 8], P('pipe', 'expert')
Inputs may be any that keep to these rules, and one draw needn't show every extreme that they name: `expert_ids`: each token names 8 different experts.
All inputs are finite; a program needn't handle non-finite values.
Results may differ from a plain program's by a relative error of at most 0.0057.
Values may be sent and summed in bfloat16 or wider, within the bound.
No kernel may reach another device: no remote copies, remote signals or barrier semaphores. Data moves between devices by JAX's collectives and lax.ppermute only.
A program may use at most 64 MiB of HBM per device.

v0:
```python
import jax
import jax.numpy as jnp
from jax import lax
from jax.sharding import PartitionSpec as P

SLICES = 4
CAP = 12


def shifted(block, axis, distance):
    devices = range(lax.axis_size(axis))
    route = [((i - distance) % len(devices), i) for i in devices]
    return lax.ppermute(block, axis, route)


def expert_grads(rows_in, rows_grad, gate_cols, up_cols, down_rows):
    gate_pre = jnp.dot(rows_in, gate_cols, preferred_element_type=jnp.float32)
    up_pre = jnp.dot(rows_in, up_cols, preferred_element_type=jnp.float32)
    sig = jax.nn.sigmoid(gate_pre)
    act = gate_pre * sig
    hidden = act * up_pre
    dhidden = lax.dot_general(
        rows_grad, down_rows, (((1,), (1,)), ((), ())), preferred_element_type=jnp.float32
    )
    gate_part = jnp.sum(hidden * dhidden, axis=1)
    d_gate_pre = (dhidden * up_pre * sig * (1.0 + gate_pre * (1.0 - sig))).astype(jnp.bfloat16)
    d_up_pre = (dhidden * act).astype(jnp.bfloat16)
    back = lax.dot_general(
        d_gate_pre, gate_cols, (((1,), (1,)), ((), ())), preferred_element_type=jnp.float32
    )
    back = back + lax.dot_general(
        d_up_pre, up_cols, (((1,), (1,)), ((), ())), preferred_element_type=jnp.float32
    )
    return (back, gate_part)


def send_back(back, gate_part):
    return (
        lax.all_to_all(back, "expert", split_axis=0, concat_axis=0, tiled=True),
        lax.all_to_all(gate_part, "expert", split_axis=0, concat_axis=0, tiled=True),
    )


def per_device(inputs, out_grads, expert_ids, gate_values, w_gate, w_up, w_down):
    devices_axis = lax.axis_size("expert")
    flight = devices_axis // SLICES
    tokens = inputs[0]
    grads = out_grads[0]
    ids = expert_ids[0]
    gates = gate_values[0]
    gate_cols = w_gate[0]
    up_cols = w_up[0]
    down_rows = w_down[0]
    count = tokens.shape[0]
    width = tokens.shape[1]
    experts_here = jnp.arange(flight, dtype=jnp.int32)
    match = ids[:, :, None] == experts_here[None, None, :]
    routed = jnp.sum(match.astype(jnp.int32), axis=1)
    weight_te = jnp.sum(jnp.where(match, gates[:, :, None], jnp.float32(0.0)), axis=1)
    before = jnp.cumsum(routed, axis=0) - routed
    kept = (routed > 0) & (before < CAP)
    slots = jnp.arange(CAP, dtype=jnp.int32)
    place = kept.T[:, None, :] & (before.T[:, None, :] == slots[None, :, None])
    place_bf = place.astype(jnp.bfloat16)
    send_x = jnp.einsum("ect,td->ecd", place_bf, tokens, preferred_element_type=jnp.float32).astype(
        jnp.bfloat16
    )
    send_g = jnp.einsum("ect,td->ecd", place_bf, grads, preferred_element_type=jnp.float32).astype(
        jnp.bfloat16
    )
    send_x = jnp.broadcast_to(send_x[:, None], (flight, SLICES, CAP, width)).reshape(
        devices_axis, CAP, width
    )
    send_g = jnp.broadcast_to(send_g[:, None], (flight, SLICES, CAP, width)).reshape(
        devices_axis, CAP, width
    )
    rows_in = lax.all_to_all(send_x, "expert", split_axis=0, concat_axis=0, tiled=True)
    rows_grad = lax.all_to_all(send_g, "expert", split_axis=0, concat_axis=0, tiled=True)
    lead = rows_in.shape[0]
    items = rows_in.shape[1]
    back, part = expert_grads(
        rows_in.reshape(lead * items, width),
        rows_grad.reshape(lead * items, width),
        gate_cols,
        up_cols,
        down_rows,
    )
    back_bf = back.astype(jnp.bfloat16).reshape(lead, items, width)
    part_bf = part.astype(jnp.bfloat16).reshape(lead, items)
    received, gate_back = send_back(back_bf, part_bf)
    total = jnp.sum(received.astype(jnp.float32).reshape(flight, SLICES, CAP, width), axis=1)
    gsum = jnp.sum(gate_back.astype(jnp.float32).reshape(flight, SLICES, CAP), axis=1)
    place_f = place.astype(jnp.float32)
    mix = jnp.transpose(place_f * weight_te.T[:, None, :], (2, 0, 1)).reshape(count, flight * CAP)
    moe = jnp.dot(
        mix,
        total.reshape(flight * CAP, width),
        precision=lax.Precision.HIGHEST,
        preferred_element_type=jnp.float32,
    )
    moe_bf = moe.astype(jnp.bfloat16)
    d_gate_te = jnp.einsum("ect,ec->te", place_f, gsum, precision=lax.Precision.HIGHEST)
    d_gates = jnp.sum(jnp.where(match, d_gate_te[:, None, :], jnp.float32(0.0)), axis=2)
    arrived = shifted(moe_bf, "pipe", -1)
    return (arrived[None], d_gates[None])


def solution(mesh):
    return jax.shard_map(
        per_device,
        mesh=mesh,
        in_specs=(
            P("pipe", "expert", None),
            P("pipe", "expert", None),
            P("pipe", "expert", None),
            P("pipe", "expert", None),
            P("pipe", None, "expert"),
            P("pipe", None, "expert"),
            P("pipe", "expert", None),
        ),
        out_specs=(P("pipe", "expert", None), P("pipe", "expert", None)),
        check_vma=False,
    )
```

profile of v0, /device:TPU:0, one launch (start us, length us, event | category | flops | bytes accessed | tf_op | source)
XLA Modules:
  0.0 126.3 jit_solution(15318237555433640698)
XLA Ops:
  0.6 0.8 convert_reduce_fusion.1
  1.8 1.3 %convolution_convert_fusion = bf16[4,12,2048]{2,1,0:T(8,128)(2,1)S(1)} fusion(bf16[1,128,2048]{2,1,0:T(8,128)(2,1)} %param.7, s32[4,128]{1,0:T(4,128)S(1)} %bitcast.54, pred[4,128]{1,0:T(4,128)(4,1)S(1)} %bitcast_and_fusion), kind=kOutput, calls=%fused_computation.4 | convolution fusion | flops 25276416 | bytes 723456 | tf_op jit(solution)/shard_map/ect,td->ecd/dot_general | solution.py:65
  3.1 1.1 broadcast_in_dim.52
  4.2 7.4 %all-to-all-start.1 = ((bf16[16,12,2048]{2,1,0:T(8,128)(2,1)}), bf16[16,12,2048]{2,1,0:T(8,128)(2,1)S(1)}, u32[]{:S(2)}, u32[]{:S(2)}) async-start(bf16[16,12,2048]{2,1,0:T(8,128)(2,1)} %bitcast.10), calls=%async_computation.1 | async-start | bytes 2097152 | tf_op jit(solution)/shard_map/all_to_all | solution.py:77
  11.8 22.7 %all-to-all-done.1 = bf16[16,12,2048]{2,1,0:T(8,128)(2,1)S(1)} async-done(((bf16[16,12,2048]{2,1,0:T(8,128)(2,1)}), bf16[16,12,2048]{2,1,0:T(8,128)(2,1)S(1)}, u32[]{:S(2)}, u32[]{:S(2)}) %all-to-all-start.1) | async-done | bytes 786464 | tf_op jit(solution)/shard_map/all_to_all | solution.py:77
  34.6 1.2 broadcast_in_dim.51
  35.7 6.9 %all-to-all-start = ((bf16[16,12,2048]{2,1,0:T(8,128)(2,1)}), bf16[16,12,2048]{2,1,0:T(8,128)(2,1)}, u32[]{:S(2)}, u32[]{:S(2)}) async-start(bf16[16,12,2048]{2,1,0:T(8,128)(2,1)} %bitcast.6), calls=%async_computation | async-start | bytes 2097152 | tf_op jit(solution)/shard_map/all_to_all | solution.py:78
  43.2 0.8 copy-done.1
  44.5 21.2 %all-to-all-done = bf16[16,12,2048]{2,1,0:T(8,128)(2,1)} async-done(((bf16[16,12,2048]{2,1,0:T(8,128)(2,1)}), bf16[16,12,2048]{2,1,0:T(8,128)(2,1)}, u32[]{:S(2)}, u32[]{:S(2)}) %all-to-all-start) | async-done | bytes 786464 | tf_op jit(solution)/shard_map/all_to_all | solution.py:78
  65.6 1.3 %reshape.55 = bf16[192,2048]{1,0:T(8,128)(2,1)S(1)} reshape(bf16[16,12,2048]{2,1,0:T(8,128)(2,1)} %all-to-all-done) | data formatting | bytes 1572864 | tf_op jit(solution)/shard_map/reshape | solution.py:83
  66.9 1.8 %multiply_reduce_fusion = (bf16[192]{0:T(256)(128)(2,1)S(1)}, f32[192,256]{1,0:T(8,128)S(1)}) fusion(f32[192,256]{1,0:T(8,128)S(1)} %fusion.7, f32[192,256]{1,0:T(8,128)S(1)} %fusion.4, bf16[192,2048]{1,0:T(8,128)(2,1)S(1)} %reshape.55, bf16[1,256,2048]{2,1,0:T(8,128)(2,1)} %param.13), kind=kOutput, calls=%fused_computation.18 | convolution fusion | flops 201670464 | bytes 2425216 | tf_op jit(solution)/shard_map/dot_general | solution.py:22
  68.8 0.5 fusion.2
  69.3 0.7 convert_element_type.61
  70.0 6.9 %all-to-all-start.3 = ((bf16[16,1,12]{2,1,0:T(2,128)(2,1)}), bf16[16,1,12]{2,1,0:T(2,128)(2,1)S(1)}, u32[]{:S(2)}, u32[]{:S(2)}) async-start(bf16[16,1,12]{2,1,0:T(2,128)(2,1)} %convert_element_type.61), calls=%async_computation.3 | async-start | bytes 16384 | tf_op jit(solution)/shard_map/all_to_all | solution.py:40
  76.9 1.9 %fusion = bf16[192,2048]{1,0:T(8,128)(2,1)S(1)} fusion(f32[192,2048]{1,0:T(8,128)S(1)} %fusion.2, bf16[1,2048,256]{2,1,0:T(8,128)(2,1)} %param.12, f32[192,256]{1,0:T(8,128)} %copy-done.3, f32[192,256]{1,0:T(8,128)} %copy-done.2), kind=kOutput, calls=%fused_computation.1 | convolution fusion | flops 202407936 | bytes 3801088 | tf_op jit(solution)/shard_map/dot_general | solution.py:31
  78.8 1.2 reshape.58
  80.0 3.3 %all-to-all-done.3 = bf16[16,1,12]{2,1,0:T(2,128)(2,1)S(1)} async-done(((bf16[16,1,12]{2,1,0:T(2,128)(2,1)}), bf16[16,1,12]{2,1,0:T(2,128)(2,1)S(1)}, u32[]{:S(2)}, u32[]{:S(2)}) %all-to-all-start.3) | async-done | bytes 416 | tf_op jit(solution)/shard_map/all_to_all | solution.py:40
  83.3 3.7 %all-to-all-start.2 = ((bf16[16,12,2048]{2,1,0:T(8,128)(2,1)}), bf16[16,12,2048]{2,1,0:T(8,128)(2,1)S(1)}, u32[]{:S(2)}, u32[]{:S(2)}) async-start(bf16[16,12,2048]{2,1,0:T(8,128)(2,1)} %reshape.58), calls=%async_computation.2 | async-start | bytes 2097152 | tf_op jit(solution)/shard_map/all_to_all | solution.py:39
  87.1 0.6 select_reduce_fusion
  87.7 22.1 %all-to-all-done.2 = bf16[16,12,2048]{2,1,0:T(8,128)(2,1)S(1)} async-done(((bf16[16,12,2048]{2,1,0:T(8,128)(2,1)}), bf16[16,12,2048]{2,1,0:T(8,128)(2,1)S(1)}, u32[]{:S(2)}, u32[]{:S(2)}) %all-to-all-start.2) | async-done | bytes 786464 | tf_op jit(solution)/shard_map/all_to_all | solution.py:39
  110.0 1.0 fusion.1
  111.1 1.6 %collective-permute-start = (bf16[128,2048]{1,0:T(8,128)(2,1)S(1)}, bf16[128,2048]{1,0:T(8,128)(2,1)S(1)}, u32[]{:S(2)}, u32[]{:S(2)}) collective-permute-start(bf16[128,2048]{1,0:T(8,128)(2,1)S(1)} %fusion.1), channel_id=1, source_target_pairs={{16,0},{0,16},{17,1},{1,17},{18,2},{2,18},{19,3},{3,19},{20,4},{4,... | collective-permute-start | bytes 1572872 | tf_op jit(solution)/shard_map/ppermute | solution.py:13
  112.6 12.9 %collective-permute-done = bf16[128,2048]{1,0:T(8,128)(2,1)S(1)} collective-permute-done((bf16[128,2048]{1,0:T(8,128)(2,1)S(1)}, bf16[128,2048]{1,0:T(8,128)(2,1)S(1)}, u32[]{:S(2)}, u32[]{:S(2)}) %collective-permute-start) | collective-permute-done | bytes 524320 | tf_op jit(solution)/shard_map/ppermute | solution.py:13
  125.5 0.8 copy.42
  (26 shorter events, 1.9 us)
Async XLA Ops:
  0.6 42.2 %copy-start = (bf16[1,2048,256]{2,1,0:T(8,128)(2,1)S(1)}, bf16[1,2048,256]{2,1,0:T(8,128)(2,1)}, u32[]{:S(2)}) copy-start(bf16[1,2048,256]{2,1,0:T(8,128)(2,1)} %param.11) | copy-start | bytes 3145732
  3.1 8.5 %copy-start.4 = (bf16[1,128,2048]{2,1,0:T(8,128)(2,1)S(1)}, bf16[1,128,2048]{2,1,0:T(8,128)(2,1)}, u32[]{:S(2)}) copy-start(bf16[1,128,2048]{2,1,0:T(8,128)(2,1)} %param.8) | copy-start | bytes 1572868
  4.2 30.3 %all-to-all-start.1 = ((bf16[16,12,2048]{2,1,0:T(8,128)(2,1)}), bf16[16,12,2048]{2,1,0:T(8,128)(2,1)S(1)}, u32[]{:S(2)}, u32[]{:S(2)}) async-start(bf16[16,12,2048]{2,1,0:T(8,128)(2,1)} %bitcast.10), calls=%async_computation.1 | async-start | bytes 2097152 | tf_op jit(solution)/shard_map/all_to_all | solution.py:77
  35.7 29.9 %all-to-all-start = ((bf16[16,12,2048]{2,1,0:T(8,128)(2,1)}), bf16[16,12,2048]{2,1,0:T(8,128)(2,1)}, u32[]{:S(2)}, u32[]{:S(2)}) async-start(bf16[16,12,2048]{2,1,0:T(8,128)(2,1)} %bitcast.6), calls=%async_computation | async-start | bytes 2097152 | tf_op jit(solution)/shard_map/all_to_all | solution.py:78
  42.8 1.2 copy-start.1
  44.1 24.7 %copy-start.2 = (f32[192,256]{1,0:T(8,128)}, f32[192,256]{1,0:T(8,128)S(1)}, u32[]{:S(2)}) copy-start(f32[192,256]{1,0:T(8,128)S(1)} %fusion.4) | copy-start | bytes 589828
  68.8 1.2 copy-start.3
  70.0 13.3 %all-to-all-start.3 = ((bf16[16,1,12]{2,1,0:T(2,128)(2,1)}), bf16[16,1,12]{2,1,0:T(2,128)(2,1)S(1)}, u32[]{:S(2)}, u32[]{:S(2)}) async-start(bf16[16,1,12]{2,1,0:T(2,128)(2,1)} %convert_element_type.61), calls=%async_computation.3 | async-start | bytes 16384 | tf_op jit(solution)/shard_map/all_to_all | solution.py:40
  78.8 8.3 %copy-start.5 = (s32[1,128,8]{1,2,0:T(8,128)S(1)}, s32[1,128,8]{1,2,0:T(8,128)}, u32[]{:S(2)}) copy-start(s32[1,128,8]{1,2,0:T(8,128)} %param.9) | copy-start | bytes 12292
  78.8 8.3 %copy-start.6 = (f32[1,128,8]{1,2,0:T(8,128)S(1)}, f32[1,128,8]{1,2,0:T(8,128)}, u32[]{:S(2)}) copy-start(f32[1,128,8]{1,2,0:T(8,128)} %param.10) | copy-start | bytes 12292
  83.3 26.6 %all-to-all-start.2 = ((bf16[16,12,2048]{2,1,0:T(8,128)(2,1)}), bf16[16,12,2048]{2,1,0:T(8,128)(2,1)S(1)}, u32[]{:S(2)}, u32[]{:S(2)}) async-start(bf16[16,12,2048]{2,1,0:T(8,128)(2,1)} %reshape.58), calls=%async_computation.2 | async-start | bytes 2097152 | tf_op jit(solution)/shard_map/all_to_all | solution.py:39
  111.1 14.5 %collective-permute-start = (bf16[128,2048]{1,0:T(8,128)(2,1)S(1)}, bf16[128,2048]{1,0:T(8,128)(2,1)S(1)}, u32[]{:S(2)}, u32[]{:S(2)}) collective-permute-start(bf16[128,2048]{1,0:T(8,128)(2,1)S(1)} %fusion.1), channel_id=1, source_target_pairs={{16,0},{0,16},{17,1},{1,17},{18,2},{2,18},{19,3},{3,19},{20,4},{4,... | collective-permute-start | bytes 1572872 | tf_op jit(solution)/shard_map/ppermute | solution.py:13
where the time goes:
time: 127 us; the launch traced here: 126 us
  waiting for transfers between devices  82.2 us (65%)
  starting transfers between devices  26.4 us (21%)
  matrix products  7.7 us (6%)
  local copies, waits for them, and re-layouts  7.45 us (6%)
  other arithmetic  1.81 us (1%)
    all_to_all x1, waiting for transfers between devices, per_device(): lax.all_to_all(send_x, 'expert', split_axis=0, concat_axis=0, tiled=True)  22.7 us
    all_to_all x1, waiting for transfers between devices, send_back(): lax.all_to_all(back, 'expert', split_axis=0, concat_axis=0, tiled=True)  22.1 us
    all_to_all x1, waiting for transfers between devices, per_device(): lax.all_to_all(send_g, 'expert', split_axis=0, concat_axis=0, tiled=True)  21.2 us
    ppermute x1, waiting for transfers between devices, shifted(): return lax.ppermute(block, axis, route)  12.9 us
    all_to_all x1, starting transfers between devices, per_device(): lax.all_to_all(send_x, 'expert', split_axis=0, concat_axis=0, tiled=True)  7.38 us
    all_to_all x1, starting transfers between devices, per_device(): lax.all_to_all(send_g, 'expert', split_axis=0, concat_axis=0, tiled=True)  6.91 us
    all_to_all x1, starting transfers between devices, send_back(): lax.all_to_all(gate_part, 'expert', split_axis=0, concat_axis=0, tiled=True)  6.87 us
    all_to_all x1, starting transfers between devices, send_back(): lax.all_to_all(back, 'expert', split_axis=0, concat_axis=0, tiled=True)  3.65 us
  transfers between devices with their start and end apart: 5, of which 5 were waited for; matrix products, arithmetic and copies ran while one was open for 4% of the time, Pallas kernels for 0%

commit v1 on v0

v1 whole, which is shorter than its diff:
```python
import functools

import jax
import jax.numpy as jnp
from jax import lax
from jax.experimental import pallas as pl
from jax.experimental.pallas import tpu as pltpu
from jax.sharding import PartitionSpec as P

SLICES = 4
CAP = 12
PAD = 16
LANES = 128
BF = jnp.bfloat16
F32 = jnp.float32
PARAMS = pltpu.CompilerParams(vmem_limit_bytes=40 * 1024 * 1024)


def select_kernel(flight, ids_ref, gates_ref, x_ref, g_ref, *outs):
    blocks, mix_ref, place_ref = outs[:flight], outs[flight], outs[flight + 1]
    own = lax.axis_index("expert") // SLICES
    ids = ids_ref[...]
    gates = gates_ref[...]
    count = ids.shape[1]
    routed, weight = [], []
    for s in range(flight):
        match = ids == (own ^ s)
        routed.append(jnp.sum(jnp.where(match, 1.0, 0.0), axis=0, keepdims=True))
        weight.append(jnp.sum(jnp.where(match, gates, 0.0), axis=0, keepdims=True))
    fill = [jnp.zeros((1, count), F32)] * (-flight % 8)
    table = jnp.concatenate(routed + fill, axis=0)
    earlier = lax.broadcasted_iota(jnp.int32, (count, count), 0) < lax.broadcasted_iota(
        jnp.int32, (count, count), 1
    )
    rank = jnp.dot(
        table.astype(BF), jnp.where(earlier, 1.0, 0.0).astype(BF), preferred_element_type=F32
    )
    key = jnp.where((table > 0.0) & (rank < float(CAP)), rank, -1.0)
    row = lax.broadcasted_iota(jnp.int32, (2 * CAP, count), 0)
    is_x = row < CAP
    slot = jnp.where(is_x, row, row - CAP).astype(F32)
    slot16 = lax.broadcasted_iota(jnp.int32, (PAD, count), 0)
    slot16 = jnp.where(slot16 < CAP, slot16, -2).astype(F32)
    picks_x, picks_g = [], []
    for s in range(flight):
        hit = key[s : s + 1] == slot
        picks_x.append(jnp.where(hit & is_x, 1.0, 0.0))
        picks_g.append(jnp.where(hit & ~is_x, 1.0, 0.0))
        at = jnp.where(key[s : s + 1] == slot16, 1.0, 0.0)
        place_ref[s * PAD : (s + 1) * PAD] = at
        mix_ref[s * PAD : (s + 1) * PAD] = at * weight[s]
    pick_x = jnp.concatenate(picks_x, axis=0).astype(BF)
    pick_g = jnp.concatenate(picks_g, axis=0).astype(BF)
    rows = jnp.dot(pick_x, x_ref[...], preferred_element_type=F32)
    rows = rows + jnp.dot(pick_g, g_ref[...], preferred_element_type=F32)
    rows = rows.astype(BF)
    for s in range(flight):
        blocks[s][...] = rows[s * 2 * CAP : (s + 1) * 2 * CAP]


def experts_kernel(count, *refs):
    blocks, weights, outs = refs[:count], refs[count : count + 6], refs[count + 6 :]
    x = jnp.concatenate([b[:CAP] for b in blocks], axis=0)
    g = jnp.concatenate([b[CAP:] for b in blocks], axis=0)
    width = x.shape[1]
    nt = (((1,), (1,)), ((), ()))
    part = jnp.zeros((x.shape[0], 1), F32)
    lefts, rights = [], []
    for half in range(2):
        wg, wu, wd = weights[3 * half : 3 * half + 3]
        a = jnp.dot(x, wg[...], preferred_element_type=F32)
        u = jnp.dot(x, wu[...], preferred_element_type=F32)
        dh = lax.dot_general(g, wd[...], nt, preferred_element_type=F32)
        sig = jax.nn.sigmoid(a)
        act = a * sig
        part = part + jnp.sum(act * u * dh, axis=1, keepdims=True)
        lefts += [
            (dh * u * sig * (1.0 + a * (1.0 - sig))).astype(BF),
            (dh * act).astype(BF),
        ]
        rights += [wg, wu]
    part_hi = part.astype(BF).astype(F32)
    lane = lax.broadcasted_iota(jnp.int32, (x.shape[0], LANES), 1)
    tail = jnp.where(lane == 0, part_hi, jnp.where(lane == 1, part - part_hi, 0.0))
    main = width * CAP // PAD
    step = width - main
    pieces = []
    for c in range(0, width, step):
        total = lax.dot_general(lefts[0], rights[0][c : c + step, :], nt, preferred_element_type=F32)
        for left, right in zip(lefts[1:], rights[1:]):
            total = total + lax.dot_general(left, right[c : c + step, :], nt, preferred_element_type=F32)
        pieces.append(total)
    last = pieces[-1]
    extra = PAD - CAP
    for i in range(count):
        base = i * CAP
        for j, piece in enumerate(pieces[:-1]):
            under = last[base + extra * j : base + extra * (j + 1)]
            both = jnp.concatenate([piece[base : base + CAP], under], axis=0)
            outs[i][:, j * step : (j + 1) * step] = both.astype(BF)
        both = jnp.concatenate([tail[base : base + CAP], jnp.zeros((extra, LANES), F32)], axis=0)
        outs[i][:, main:] = both.astype(BF)


def tails_kernel(flight, *refs):
    blocks, out_ref = refs[:-1], refs[-1]
    for s in range(flight):
        tail = blocks[s][...].astype(F32) + blocks[s + flight][...].astype(F32)
        out_ref[s * PAD : (s + 1) * PAD] = tail


def split(value):
    high = value.astype(BF)
    return high, (value - high.astype(F32)).astype(BF)


def mix_kernel(flight, *refs):
    blocks, mix_ref, out_ref = refs[: 2 * flight], refs[2 * flight], refs[2 * flight + 1]
    width = out_ref.shape[1]
    main = width * CAP // PAD
    step = width - main
    extra = PAD - CAP
    tn = (((0,), (0,)), ((), ()))
    mix_hi, mix_lo = split(mix_ref[...])
    left = jnp.concatenate([mix_hi, mix_hi, mix_lo], axis=0)

    def blend(rows):
        high, low = split(rows)
        right = jnp.concatenate([high, low, high], axis=0)
        return lax.dot_general(left, right, tn, preferred_element_type=F32).astype(BF)

    lasts = []
    for j in range(main // step):
        cols = pl.ds(j * step, step)
        rows = jnp.concatenate(
            [
                blocks[s][:, cols].astype(F32) + blocks[s + flight][:, cols].astype(F32)
                for s in range(flight)
            ],
            axis=0,
        )
        out_ref[:, j * step : (j + 1) * step] = blend(rows)
        lasts.append([rows[s * PAD + CAP : (s + 1) * PAD] for s in range(flight)])
    zero = jnp.zeros((extra, step), F32)
    rows = jnp.concatenate(
        [piece for s in range(flight) for piece in [l[s] for l in lasts] + [zero]], axis=0
    )
    out_ref[:, main:] = blend(rows)


def gates_kernel(flight, ids_ref, place_ref, tail_ref, out_ref):
    own = lax.axis_index("expert") // SLICES
    ids = ids_ref[...]
    total = jnp.zeros(ids.shape, F32)
    for s in range(flight):
        q = jnp.sum(tail_ref[s * PAD : (s + 1) * PAD], axis=1, keepdims=True)
        back = jnp.sum(place_ref[s * PAD : (s + 1) * PAD] * q, axis=0, keepdims=True)
        total = total + jnp.where(ids == (own ^ s), back, 0.0)
    out_ref[...] = total


def moved(value, sections, devices, stage, flip, bits):
    route = []
    for p in range(sections):
        for e in range(devices):
            route.append((p * devices + e, (p + flip) % sections * devices + (e ^ bits)))
    return lax.ppermute(value, stage, route)


def per_device(inputs, out_grads, expert_ids, gate_values, w_gate, w_up, w_down):
    devices = lax.axis_size("expert")
    sections = lax.axis_size("pipe")
    flight = devices // SLICES
    count, width = inputs.shape[1:]
    axes = ("pipe", "expert")
    go = functools.partial(moved, sections=sections, devices=devices, stage=axes)
    own_weights = [w_gate[0], w_up[0], w_down[0]]
    near_weights = [go(w, flip=0, bits=1) for w in own_weights]
    ids = expert_ids[0].T
    gates = gate_values[0].T
    *blocks, mix, place = pl.pallas_call(
        functools.partial(select_kernel, flight),
        out_shape=[jax.ShapeDtypeStruct((2 * CAP, width), BF)] * flight
        + [jax.ShapeDtypeStruct((flight * PAD, count), F32)] * 2,
        compiler_params=PARAMS,
        name="select",
    )(ids, gates, inputs[0], out_grads[0])
    rows = [blocks[0]] + [go(blocks[s], flip=0, bits=SLICES * s) for s in range(1, flight)]
    rows = rows + [go(r, flip=0, bits=2) for r in rows]
    mix = go(mix, flip=-1, bits=0)
    main = width * CAP // PAD
    parts = pl.pallas_call(
        functools.partial(experts_kernel, 2 * flight),
        out_shape=[jax.ShapeDtypeStruct((PAD, main + LANES), BF)] * (2 * flight),
        compiler_params=PARAMS,
        name="experts",
    )(*rows, *own_weights, *near_weights)
    home = [
        go(parts[t * flight + s], flip=-1, bits=SLICES * s + 2 * t)
        for t in range(2)
        for s in range(flight)
    ]
    tails = pl.pallas_call(
        functools.partial(tails_kernel, flight),
        out_shape=jax.ShapeDtypeStruct((flight * PAD, LANES), F32),
        compiler_params=PARAMS,
        name="tails",
    )(*[h[:, main:] for h in home])
    tails = go(tails, flip=1, bits=0)
    moe = pl.pallas_call(
        functools.partial(mix_kernel, flight),
        out_shape=jax.ShapeDtypeStruct((count, width), BF),
        compiler_params=PARAMS,
        name="mix",
    )(*home, mix)
    d_gates = pl.pallas_call(
        functools.partial(gates_kernel, flight),
        out_shape=jax.ShapeDtypeStruct(ids.shape, F32),
        compiler_params=PARAMS,
        name="gates",
    )(ids, place, tails)
    return (moe[None], d_gates.T[None])


def solution(mesh):
    return jax.shard_map(
        per_device,
        mesh=mesh,
        in_specs=(
            P("pipe", "expert", None),
            P("pipe", "expert", None),
            P("pipe", "expert", None),
            P("pipe", "expert", None),
            P("pipe", None, "expert"),
            P("pipe", None, "expert"),
            P("pipe", "expert", None),
        ),
        out_specs=(P("pipe", "expert", None), P("pipe", "expert", None)),
        check_vma=False,
    )
```

time: 127 us -> 61.9 us (0.49)
  waiting for transfers between devices: 82.2 us -> 15 us
  starting transfers between devices: 26.4 us -> 34.8 us
  matrix products: 7.7 us -> 0 us
  Pallas kernels: 0 us -> 5.18 us
  other arithmetic: 1.81 us -> 0 us
  local copies, waits for them, and re-layouts: 7.45 us -> 5.92 us
    all_to_all x4 -> x0, waiting for transfers between devices: 69.2 us -> none  [the longest x1 22.7 us: per_device(): lax.all_to_all(send_x, 'expert', split_axis=0, concat_axis=0, tiled=True)]
    ppermute x1 -> x20, starting transfers between devices: 1.56 us -> 34.8 us  [moved(): return lax.ppermute(value, stage, route)]
    all_to_all x4 -> x0, starting transfers between devices: 24.8 us -> none  [the longest x1 7.38 us: per_device(): lax.all_to_all(send_x, 'expert', split_axis=0, concat_axis=0, tiled=True)]
    dot_general x9 -> x0, matrix products: 7.7 us -> none  [the longest x1 1.94 us: expert_grads(): lax.dot_general(d_up_pre, up_cols, (((1,), (1,)), ((), ())), preferred_el...]
    pallas_call x0 -> x5, Pallas kernels: none -> 5.18 us  [the longest x1 2.86 us: per_device(): pl.pallas_call(functools.partial(experts_kernel, 2 * flight), out_shape=[...]
    unnamed x15 -> x16, local copies, waits for them, and re-layouts: 1.67 us -> 5.91 us
    reshape x3 -> x0, local copies, waits for them, and re-layouts: 2.65 us -> none  [the longest x1 1.31 us: per_device(): rows_grad.reshape(lead * items, width)]
    broadcast_in_dim x2 -> x0, local copies, waits for them, and re-layouts: 2.27 us -> none  [the longest x1 1.16 us: per_device(): jnp.broadcast_to(send_g[:, None], (flight, SLICES, CAP, width))]
  transfers between devices with their start and end apart: 5 -> 20, of which waited for: 5 -> 9; matrix products, arithmetic and copies ran while one was open for 4% -> 0% of each run, Pallas kernels for 0% -> 3%
where the time goes in v1:
time: 61.9 us; the launch traced here: 61.6 us
  starting transfers between devices  34.8 us (56%)
  waiting for transfers between devices  15 us (24%)
  local copies, waits for them, and re-layouts  5.92 us (10%)
  Pallas kernels  5.18 us (8%)
  between operations  0.72 us (1%)
    ppermute x20, starting transfers between devices, moved(): return lax.ppermute(value, stage, route)  34.8 us
    ppermute x20, waiting for transfers between devices, moved(): return lax.ppermute(value, stage, route)  15 us
    unnamed x16, local copies, waits for them, and re-layouts  5.91 us
    pallas_call x1, Pallas kernels, per_device(): pl.pallas_call(functools.partial(experts_kernel, 2 * flight), out_shape=[...  2.86 us
  transfers between devices with their start and end apart: 20, of which 9 were waited for; matrix products, arithmetic and copies ran while one was open for 0% of the time, Pallas kernels for 3%

profile of v1, /device:TPU:0, one launch (start us, length us, event | category | flops | bytes accessed | tf_op | source)
XLA Modules:
  0.0 61.6 jit_solution(16017184468356844232)
XLA Ops:
  5.6 2.7 %collective-permute-start = (bf16[24,2048]{1,0:T(8,128)(2,1)S(1)}, bf16[24,2048]{1,0:T(8,128)(2,1)S(1)}, u32[]{:S(2)}, u32[]{:S(2)}) collective-permute-start(bf16[24,2048]{1,0:T(8,128)(2,1)S(1)} %get-tuple-element.17), channel_id=1, source_target_pairs={{0,4},{1,5},{2,6},{3,7},{4,0},{5,1},{6,2},{7,3},{8,12},{9,13},{10,... | collective-permute-start | bytes 294920 | tf_op jit(solution)/shard_map/ppermute | solution.py:167
  8.3 2.6 %collective-permute-start.1 = (bf16[24,2048]{1,0:T(8,128)(2,1)S(1)}, bf16[24,2048]{1,0:T(8,128)(2,1)S(1)}, u32[]{:S(2)}, u32[]{:S(2)}) collective-permute-start(bf16[24,2048]{1,0:T(8,128)(2,1)S(1)} %get-tuple-element.18), channel_id=1, source_target_pairs={{0,8},{1,9},{2,10},{3,11},{4,12},{5,13},{6,14},{7,15},{8,0},{9,1},... | collective-permute-start | bytes 294920 | tf_op jit(solution)/shard_map/ppermute | solution.py:167
  11.7 4.8 %collective-permute-start.2 = (bf16[24,2048]{1,0:T(8,128)(2,1)S(1)}, bf16[24,2048]{1,0:T(8,128)(2,1)S(1)}, u32[]{:S(2)}, u32[]{:S(2)}) collective-permute-start(bf16[24,2048]{1,0:T(8,128)(2,1)S(1)} %get-tuple-element.19), channel_id=1, source_target_pairs={{0,12},{1,13},{2,14},{3,15},{4,8},{5,9},{6,10},{7,11},{8,4},{9,5},... | collective-permute-start | bytes 294920 | tf_op jit(solution)/shard_map/ppermute | solution.py:167
  16.6 1.5 %collective-permute-start.3 = (bf16[24,2048]{1,0:T(8,128)(2,1)S(1)}, bf16[24,2048]{1,0:T(8,128)(2,1)S(1)}, u32[]{:S(2)}, u32[]{:S(2)}) collective-permute-start(bf16[24,2048]{1,0:T(8,128)(2,1)S(1)} %get-tuple-element.16.refs_0_), channel_id=1, source_target_pairs={{0,2},{1,3},{2,0},{3,1},{4,6},{5,7},{6,4},{7,5},{8,10},{9,11},{10,... | collective-permute-start | bytes 294920 | tf_op jit(solution)/shard_map/ppermute | solution.py:167
  18.1 1.2 %collective-permute-done.2.refs_3_ = bf16[24,2048]{1,0:T(8,128)(2,1)S(1)} collective-permute-done((bf16[24,2048]{1,0:T(8,128)(2,1)S(1)}, bf16[24,2048]{1,0:T(8,128)(2,1)S(1)}, u32[]{:S(2)}, u32[]{:S(2)}) %collective-permute-start.2) | collective-permute-done | bytes 98336 | tf_op jit(solution)/shard_map/ppermute | solution.py:167
  19.3 1.5 %collective-permute-start.4 = (bf16[24,2048]{1,0:T(8,128)(2,1)S(1)}, bf16[24,2048]{1,0:T(8,128)(2,1)S(1)}, u32[]{:S(2)}, u32[]{:S(2)}) collective-permute-start(bf16[24,2048]{1,0:T(8,128)(2,1)S(1)} %collective-permute-done.refs_1_), channel_id=1, source_target_pairs={{0,2},{1,3},{2,0},{3,1},{4,6},{5,7},{6,4},{7,5},{8,10},{9,11},{10,... | collective-permute-start | bytes 294920 | tf_op jit(solution)/shard_map/ppermute | solution.py:167
  21.4 1.5 %collective-permute-start.5 = (bf16[24,2048]{1,0:T(8,128)(2,1)S(1)}, bf16[24,2048]{1,0:T(8,128)(2,1)S(1)}, u32[]{:S(2)}, u32[]{:S(2)}) collective-permute-start(bf16[24,2048]{1,0:T(8,128)(2,1)S(1)} %collective-permute-done.1.refs_2_), channel_id=1, source_target_pairs={{0,2},{1,3},{2,0},{3,1},{4,6},{5,7},{6,4},{7,5},{8,10},{9,11},{10,... | collective-permute-start | bytes 294920 | tf_op jit(solution)/shard_map/ppermute | solution.py:167
  23.0 1.4 %collective-permute-done.4.refs_5_ = bf16[24,2048]{1,0:T(8,128)(2,1)S(1)} collective-permute-done((bf16[24,2048]{1,0:T(8,128)(2,1)S(1)}, bf16[24,2048]{1,0:T(8,128)(2,1)S(1)}, u32[]{:S(2)}, u32[]{:S(2)}) %collective-permute-start.4) | collective-permute-done | bytes 98336 | tf_op jit(solution)/shard_map/ppermute | solution.py:167
  24.4 1.5 %collective-permute-start.6 = (bf16[24,2048]{1,0:T(8,128)(2,1)S(1)}, bf16[24,2048]{1,0:T(8,128)(2,1)S(1)}, u32[]{:S(2)}, u32[]{:S(2)}) collective-permute-start(bf16[24,2048]{1,0:T(8,128)(2,1)S(1)} %collective-permute-done.2.refs_3_), channel_id=1, source_target_pairs={{0,2},{1,3},{2,0},{3,1},{4,6},{5,7},{6,4},{7,5},{8,10},{9,11},{10,... | collective-permute-start | bytes 294920 | tf_op jit(solution)/shard_map/ppermute | solution.py:167
  26.8 2.2 %collective-permute-done.6.refs_7_ = bf16[24,2048]{1,0:T(8,128)(2,1)S(1)} collective-permute-done((bf16[24,2048]{1,0:T(8,128)(2,1)S(1)}, bf16[24,2048]{1,0:T(8,128)(2,1)S(1)}, u32[]{:S(2)}, u32[]{:S(2)}) %collective-permute-start.6) | collective-permute-done | bytes 98336 | tf_op jit(solution)/shard_map/ppermute | solution.py:167
  29.0 1.2 %copy-done.1 = bf16[1,2048,256]{2,1,0:T(8,128)(2,1)S(1)} copy-done((bf16[1,2048,256]{2,1,0:T(8,128)(2,1)S(1)}, bf16[1,2048,256]{2,1,0:T(8,128)(2,1)}, u32[]{:S(2)}) %copy-start.1) | copy-done | bytes 1048600
  30.2 1.2 %copy-done.2 = bf16[1,256,2048]{2,1,0:T(8,128)(2,1)S(1)} copy-done((bf16[1,256,2048]{2,1,0:T(8,128)(2,1)S(1)}, bf16[1,256,2048]{2,1,0:T(8,128)(2,1)}, u32[]{:S(2)}) %copy-start.2) | copy-done | bytes 1048600
  31.4 2.9 %experts.1 = (bf16[16,1664]{1,0:T(8,128)(2,1)S(1)}, bf16[16,1664]{1,0:T(8,128)(2,1)S(1)}, bf16[16,1664]{1,0:T(8,128)(2,1)S(1)}, bf16[16,1664]{1,0:T(8,128)(2,1)S...) custom-call(bf16[24,2048]{1,0:T(8,128)(2,1)S(1)} %get-tuple-element., ...), custom_call_target="tpu_custom_call" | custom-call | tf_op jit(solution)/shard_map/experts/pallas_call | solution.py:192
  34.3 1.6 %collective-permute-start.10 = (bf16[16,1664]{1,0:T(8,128)(2,1)S(1)}, bf16[16,1664]{1,0:T(8,128)(2,1)S(1)}, u32[]{:S(2)}, u32[]{:S(2)}) collective-permute-start(bf16[16,1664]{1,0:T(8,128)(2,1)S(1)} %get-tuple-element.20), channel_id=1, source_target_pairs={{0,16},{1,17},{2,18},{3,19},{4,20},{5,21},{6,22},{7,23},{8,24},{9,... | collective-permute-start | bytes 159752 | tf_op jit(solution)/shard_map/ppermute | solution.py:167
  35.9 2.2 %collective-permute-start.11 = (bf16[16,1664]{1,0:T(8,128)(2,1)S(1)}, bf16[16,1664]{1,0:T(8,128)(2,1)S(1)}, u32[]{:S(2)}, u32[]{:S(2)}) collective-permute-start(bf16[16,1664]{1,0:T(8,128)(2,1)S(1)} %get-tuple-element.21), channel_id=1, source_target_pairs={{0,20},{1,21},{2,22},{3,23},{4,16},{5,17},{6,18},{7,19},{8,28},{9,... | collective-permute-start | bytes 159752 | tf_op jit(solution)/shard_map/ppermute | solution.py:167
  38.0 2.6 %collective-permute-start.12 = (bf16[16,1664]{1,0:T(8,128)(2,1)S(1)}, bf16[16,1664]{1,0:T(8,128)(2,1)S(1)}, u32[]{:S(2)}, u32[]{:S(2)}) collective-permute-start(bf16[16,1664]{1,0:T(8,128)(2,1)S(1)} %get-tuple-element.22), channel_id=1, source_target_pairs={{0,24},{1,25},{2,26},{3,27},{4,28},{5,29},{6,30},{7,31},{8,16},{9,... | collective-permute-start | bytes 159752 | tf_op jit(solution)/shard_map/ppermute | solution.py:167
  41.4 2.2 %collective-permute-start.14 = (bf16[16,1664]{1,0:T(8,128)(2,1)S(1)}, bf16[16,1664]{1,0:T(8,128)(2,1)S(1)}, u32[]{:S(2)}, u32[]{:S(2)}) collective-permute-start(bf16[16,1664]{1,0:T(8,128)(2,1)S(1)} %get-tuple-element.24), channel_id=1, source_target_pairs={{0,18},{1,19},{2,16},{3,17},{4,22},{5,23},{6,20},{7,21},{8,26},{9,... | collective-permute-start | bytes 159752 | tf_op jit(solution)/shard_map/ppermute | solution.py:167
  43.6 1.2 %collective-permute-start.15 = (bf16[16,1664]{1,0:T(8,128)(2,1)S(1)}, bf16[16,1664]{1,0:T(8,128)(2,1)S(1)}, u32[]{:S(2)}, u32[]{:S(2)}) collective-permute-start(bf16[16,1664]{1,0:T(8,128)(2,1)S(1)} %get-tuple-element.25), channel_id=1, source_target_pairs={{0,22},{1,23},{2,20},{3,21},{4,18},{5,19},{6,16},{7,17},{8,30},{9,... | collective-permute-start | bytes 159752 | tf_op jit(solution)/shard_map/ppermute | solution.py:167
  44.8 4.4 %collective-permute-start.16 = (bf16[16,1664]{1,0:T(8,128)(2,1)S(1)}, bf16[16,1664]{1,0:T(8,128)(2,1)S(1)}, u32[]{:S(2)}, u32[]{:S(2)}) collective-permute-start(bf16[16,1664]{1,0:T(8,128)(2,1)S(1)} %get-tuple-element.26), channel_id=1, source_target_pairs={{0,26},{1,27},{2,24},{3,25},{4,30},{5,31},{6,28},{7,29},{8,18},{9,... | collective-permute-start | bytes 159752 | tf_op jit(solution)/shard_map/ppermute | solution.py:167
  49.9 1.3 %collective-permute-start.18 = (f32[64,128]{1,0:T(8,128)S(1)}, f32[64,128]{1,0:T(8,128)S(1)}, u32[]{:S(2)}, u32[]{:S(2)}) collective-permute-start(f32[64,128]{1,0:T(8,128)S(1)} %get-tuple-element.28), channel_id=1, source_target_pairs={{0,16},{1,17},{2,18},{3,19},{4,20},{5,21},{6,22},{7,23},{8,24},{9,... | collective-permute-start | bytes 98312 | tf_op jit(solution)/shard_map/ppermute | solution.py:167
  51.3 1.5 %collective-permute-done.16.refs_6_ = bf16[16,1664]{1,0:T(8,128)(2,1)S(1)} collective-permute-done((bf16[16,1664]{1,0:T(8,128)(2,1)S(1)}, bf16[16,1664]{1,0:T(8,128)(2,1)S(1)}, u32[]{:S(2)}, u32[]{:S(2)}) %collective-permute-start.16) | collective-permute-done | bytes 53280 | tf_op jit(solution)/shard_map/ppermute | solution.py:167
  52.8 4.2 %collective-permute-done.17.refs_7_ = bf16[16,1664]{1,0:T(8,128)(2,1)S(1)} collective-permute-done((bf16[16,1664]{1,0:T(8,128)(2,1)S(1)}, bf16[16,1664]{1,0:T(8,128)(2,1)S(1)}, u32[]{:S(2)}, u32[]{:S(2)}) %collective-permute-start.17) | collective-permute-done | bytes 53280 | tf_op jit(solution)/shard_map/ppermute | solution.py:167
  57.6 1.1 %mix.1 = bf16[128,2048]{1,0:T(8,128)(2,1)} custom-call(bf16[16,1664]{1,0:T(8,128)(2,1)S(1)} %collective-permute-done.10.refs_0_, bf16[16,1664]{1,0:T(8,128)(2,1)S(1)} %collective-permute-done.11.refs_1_, bf16[16,1664]{1,0:T(8,128)(2,1)S(1)} %collective-permute-done.12.refs_2_, bf16[16,1664]{1,0:T(8,128)(2,1)S(1)} %collective-permute-done.13.refs_3_, ...), custom_call_target="tpu_custom_call" | custom-call | tf_op jit(solution)/shard_map/mix/pallas_call | solution.py:210
  58.7 2.2 %collective-permute-done.19.tail_ref = f32[64,128]{1,0:T(8,128)S(1)} collective-permute-done((f32[64,128]{1,0:T(8,128)S(1)}, f32[64,128]{1,0:T(8,128)S(1)}, u32[]{:S(2)}, u32[]{:S(2)}) %collective-permute-start.19) | collective-permute-done | bytes 32800 | tf_op jit(solution)/shard_map/ppermute | solution.py:167
  (45 shorter events, 10.1 us)
Async XLA Ops:
  0.6 28.4 %copy-start = (bf16[1,2048,256]{2,1,0:T(8,128)(2,1)S(1)}, bf16[1,2048,256]{2,1,0:T(8,128)(2,1)}, u32[]{:S(2)}) copy-start(bf16[1,2048,256]{2,1,0:T(8,128)(2,1)} %param.11) | copy-start | bytes 3145732
  0.6 28.3 %collective-permute-start.7 = (bf16[2048,256]{1,0:T(8,128)(2,1)}, bf16[2048,256]{1,0:T(8,128)(2,1)S(1)}, u32[]{:S(2)}, u32[]{:S(2)}) collective-permute-start(bf16[2048,256]{1,0:T(8,128)(2,1)} %bitcast.15), channel_id=1, source_target_pairs={{0,1},{1,0},{2,3},{3,2},{4,5},{5,4},{6,7},{7,6},{8,9},{9,8},{10,11... | collective-permute-start | bytes 3145736 | tf_op jit(solution)/shard_map/ppermute | solution.py:167
  1.2 27.8 %collective-permute-start.8 = (bf16[2048,256]{1,0:T(8,128)(2,1)}, bf16[2048,256]{1,0:T(8,128)(2,1)S(1)}, u32[]{:S(2)}, u32[]{:S(2)}) collective-permute-start(bf16[2048,256]{1,0:T(8,128)(2,1)} %bitcast.17), channel_id=1, source_target_pairs={{0,1},{1,0},{2,3},{3,2},{4,5},{5,4},{6,7},{7,6},{8,9},{9,8},{10,11... | collective-permute-start | bytes 3145736 | tf_op jit(solution)/shard_map/ppermute | solution.py:167
  1.2 27.7 %collective-permute-start.9 = (bf16[256,2048]{1,0:T(8,128)(2,1)}, bf16[256,2048]{1,0:T(8,128)(2,1)S(1)}, u32[]{:S(2)}, u32[]{:S(2)}) collective-permute-start(bf16[256,2048]{1,0:T(8,128)(2,1)} %bitcast.19), channel_id=1, source_target_pairs={{0,1},{1,0},{2,3},{3,2},{4,5},{5,4},{6,7},{7,6},{8,9},{9,8},{10,11... | collective-permute-start | bytes 3145736 | tf_op jit(solution)/shard_map/ppermute | solution.py:167
  5.6 6.1 %collective-permute-start = (bf16[24,2048]{1,0:T(8,128)(2,1)S(1)}, bf16[24,2048]{1,0:T(8,128)(2,1)S(1)}, u32[]{:S(2)}, u32[]{:S(2)}) collective-permute-start(bf16[24,2048]{1,0:T(8,128)(2,1)S(1)} %get-tuple-element.17), channel_id=1, source_target_pairs={{0,4},{1,5},{2,6},{3,7},{4,0},{5,1},{6,2},{7,3},{8,12},{9,13},{10,... | collective-permute-start | bytes 294920 | tf_op jit(solution)/shard_map/ppermute | solution.py:167
  8.3 8.2 %collective-permute-start.1 = (bf16[24,2048]{1,0:T(8,128)(2,1)S(1)}, bf16[24,2048]{1,0:T(8,128)(2,1)S(1)}, u32[]{:S(2)}, u32[]{:S(2)}) collective-permute-start(bf16[24,2048]{1,0:T(8,128)(2,1)S(1)} %get-tuple-element.18), channel_id=1, source_target_pairs={{0,8},{1,9},{2,10},{3,11},{4,12},{5,13},{6,14},{7,15},{8,0},{9,1},... | collective-permute-start | bytes 294920 | tf_op jit(solution)/shard_map/ppermute | solution.py:167
  11.7 7.6 %collective-permute-start.2 = (bf16[24,2048]{1,0:T(8,128)(2,1)S(1)}, bf16[24,2048]{1,0:T(8,128)(2,1)S(1)}, u32[]{:S(2)}, u32[]{:S(2)}) collective-permute-start(bf16[24,2048]{1,0:T(8,128)(2,1)S(1)} %get-tuple-element.19), channel_id=1, source_target_pairs={{0,12},{1,13},{2,14},{3,15},{4,8},{5,9},{6,10},{7,11},{8,4},{9,5},... | collective-permute-start | bytes 294920 | tf_op jit(solution)/shard_map/ppermute | solution.py:167
  16.6 4.9 %collective-permute-start.3 = (bf16[24,2048]{1,0:T(8,128)(2,1)S(1)}, bf16[24,2048]{1,0:T(8,128)(2,1)S(1)}, u32[]{:S(2)}, u32[]{:S(2)}) collective-permute-start(bf16[24,2048]{1,0:T(8,128)(2,1)S(1)} %get-tuple-element.16.refs_0_), channel_id=1, source_target_pairs={{0,2},{1,3},{2,0},{3,1},{4,6},{5,7},{6,4},{7,5},{8,10},{9,11},{10,... | collective-permute-start | bytes 294920 | tf_op jit(solution)/shard_map/ppermute | solution.py:167
  19.3 5.1 %collective-permute-start.4 = (bf16[24,2048]{1,0:T(8,128)(2,1)S(1)}, bf16[24,2048]{1,0:T(8,128)(2,1)S(1)}, u32[]{:S(2)}, u32[]{:S(2)}) collective-permute-start(bf16[24,2048]{1,0:T(8,128)(2,1)S(1)} %collective-permute-done.refs_1_), channel_id=1, source_target_pairs={{0,2},{1,3},{2,0},{3,1},{4,6},{5,7},{6,4},{7,5},{8,10},{9,11},{10,... | collective-permute-start | bytes 294920 | tf_op jit(solution)/shard_map/ppermute | solution.py:167
  21.4 5.3 %collective-permute-start.5 = (bf16[24,2048]{1,0:T(8,128)(2,1)S(1)}, bf16[24,2048]{1,0:T(8,128)(2,1)S(1)}, u32[]{:S(2)}, u32[]{:S(2)}) collective-permute-start(bf16[24,2048]{1,0:T(8,128)(2,1)S(1)} %collective-permute-done.1.refs_2_), channel_id=1, source_target_pairs={{0,2},{1,3},{2,0},{3,1},{4,6},{5,7},{6,4},{7,5},{8,10},{9,11},{10,... | collective-permute-start | bytes 294920 | tf_op jit(solution)/shard_map/ppermute | solution.py:167
  24.4 4.6 %collective-permute-start.6 = (bf16[24,2048]{1,0:T(8,128)(2,1)S(1)}, bf16[24,2048]{1,0:T(8,128)(2,1)S(1)}, u32[]{:S(2)}, u32[]{:S(2)}) collective-permute-start(bf16[24,2048]{1,0:T(8,128)(2,1)S(1)} %collective-permute-done.2.refs_3_), channel_id=1, source_target_pairs={{0,2},{1,3},{2,0},{3,1},{4,6},{5,7},{6,4},{7,5},{8,10},{9,11},{10,... | collective-permute-start | bytes 294920 | tf_op jit(solution)/shard_map/ppermute | solution.py:167
  29.0 1.2 %copy-start.1 = (bf16[1,2048,256]{2,1,0:T(8,128)(2,1)S(1)}, bf16[1,2048,256]{2,1,0:T(8,128)(2,1)}, u32[]{:S(2)}) copy-start(bf16[1,2048,256]{2,1,0:T(8,128)(2,1)} %param.12) | copy-start | bytes 3145732
  30.2 1.2 %copy-start.2 = (bf16[1,256,2048]{2,1,0:T(8,128)(2,1)S(1)}, bf16[1,256,2048]{2,1,0:T(8,128)(2,1)}, u32[]{:S(2)}) copy-start(bf16[1,256,2048]{2,1,0:T(8,128)(2,1)} %param.13) | copy-start | bytes 3145732
  34.3 9.3 %collective-permute-start.10 = (bf16[16,1664]{1,0:T(8,128)(2,1)S(1)}, bf16[16,1664]{1,0:T(8,128)(2,1)S(1)}, u32[]{:S(2)}, u32[]{:S(2)}) collective-permute-start(bf16[16,1664]{1,0:T(8,128)(2,1)S(1)} %get-tuple-element.20), channel_id=1, source_target_pairs={{0,16},{1,17},{2,18},{3,19},{4,20},{5,21},{6,22},{7,23},{8,24},{9,... | collective-permute-start | bytes 159752 | tf_op jit(solution)/shard_map/ppermute | solution.py:167
  35.9 8.9 %collective-permute-start.11 = (bf16[16,1664]{1,0:T(8,128)(2,1)S(1)}, bf16[16,1664]{1,0:T(8,128)(2,1)S(1)}, u32[]{:S(2)}, u32[]{:S(2)}) collective-permute-start(bf16[16,1664]{1,0:T(8,128)(2,1)S(1)} %get-tuple-element.21), channel_id=1, source_target_pairs={{0,20},{1,21},{2,22},{3,23},{4,16},{5,17},{6,18},{7,19},{8,28},{9,... | collective-permute-start | bytes 159752 | tf_op jit(solution)/shard_map/ppermute | solution.py:167
  38.0 11.2 %collective-permute-start.12 = (bf16[16,1664]{1,0:T(8,128)(2,1)S(1)}, bf16[16,1664]{1,0:T(8,128)(2,1)S(1)}, u32[]{:S(2)}, u32[]{:S(2)}) collective-permute-start(bf16[16,1664]{1,0:T(8,128)(2,1)S(1)} %get-tuple-element.22), channel_id=1, source_target_pairs={{0,24},{1,25},{2,26},{3,27},{4,28},{5,29},{6,30},{7,31},{8,16},{9,... | collective-permute-start | bytes 159752 | tf_op jit(solution)/shard_map/ppermute | solution.py:167
  40.6 9.3 %collective-permute-start.13 = (bf16[16,1664]{1,0:T(8,128)(2,1)S(1)}, bf16[16,1664]{1,0:T(8,128)(2,1)S(1)}, u32[]{:S(2)}, u32[]{:S(2)}) collective-permute-start(bf16[16,1664]{1,0:T(8,128)(2,1)S(1)} %get-tuple-element.23), channel_id=1, source_target_pairs={{0,28},{1,29},{2,30},{3,31},{4,24},{5,25},{6,26},{7,27},{8,20},{9,... | collective-permute-start | bytes 159752 | tf_op jit(solution)/shard_map/ppermute | solution.py:167
  41.4 9.9 %collective-permute-start.14 = (bf16[16,1664]{1,0:T(8,128)(2,1)S(1)}, bf16[16,1664]{1,0:T(8,128)(2,1)S(1)}, u32[]{:S(2)}, u32[]{:S(2)}) collective-permute-start(bf16[16,1664]{1,0:T(8,128)(2,1)S(1)} %get-tuple-element.24), channel_id=1, source_target_pairs={{0,18},{1,19},{2,16},{3,17},{4,22},{5,23},{6,20},{7,21},{8,26},{9,... | collective-permute-start | bytes 159752 | tf_op jit(solution)/shard_map/ppermute | solution.py:167
  43.6 7.7 %collective-permute-start.15 = (bf16[16,1664]{1,0:T(8,128)(2,1)S(1)}, bf16[16,1664]{1,0:T(8,128)(2,1)S(1)}, u32[]{:S(2)}, u32[]{:S(2)}) collective-permute-start(bf16[16,1664]{1,0:T(8,128)(2,1)S(1)} %get-tuple-element.25), channel_id=1, source_target_pairs={{0,22},{1,23},{2,20},{3,21},{4,18},{5,19},{6,16},{7,17},{8,30},{9,... | collective-permute-start | bytes 159752 | tf_op jit(solution)/shard_map/ppermute | solution.py:167
  44.8 8.0 %collective-permute-start.16 = (bf16[16,1664]{1,0:T(8,128)(2,1)S(1)}, bf16[16,1664]{1,0:T(8,128)(2,1)S(1)}, u32[]{:S(2)}, u32[]{:S(2)}) collective-permute-start(bf16[16,1664]{1,0:T(8,128)(2,1)S(1)} %get-tuple-element.26), channel_id=1, source_target_pairs={{0,26},{1,27},{2,24},{3,25},{4,30},{5,31},{6,28},{7,29},{8,18},{9,... | collective-permute-start | bytes 159752 | tf_op jit(solution)/shard_map/ppermute | solution.py:167
  49.2 7.7 %collective-permute-start.17 = (bf16[16,1664]{1,0:T(8,128)(2,1)S(1)}, bf16[16,1664]{1,0:T(8,128)(2,1)S(1)}, u32[]{:S(2)}, u32[]{:S(2)}) collective-permute-start(bf16[16,1664]{1,0:T(8,128)(2,1)S(1)} %get-tuple-element.27), channel_id=1, source_target_pairs={{0,30},{1,31},{2,28},{3,29},{4,26},{5,27},{6,24},{7,25},{8,22},{9,... | collective-permute-start | bytes 159752 | tf_op jit(solution)/shard_map/ppermute | solution.py:167
  49.9 7.6 %collective-permute-start.18 = (f32[64,128]{1,0:T(8,128)S(1)}, f32[64,128]{1,0:T(8,128)S(1)}, u32[]{:S(2)}, u32[]{:S(2)}) collective-permute-start(f32[64,128]{1,0:T(8,128)S(1)} %get-tuple-element.28), channel_id=1, source_target_pairs={{0,16},{1,17},{2,18},{3,19},{4,20},{5,21},{6,22},{7,23},{8,24},{9,... | collective-permute-start | bytes 98312 | tf_op jit(solution)/shard_map/ppermute | solution.py:167
  56.9 4.0 %collective-permute-start.19 = (f32[64,128]{1,0:T(8,128)S(1)}, f32[64,128]{1,0:T(8,128)S(1)}, u32[]{:S(2)}, u32[]{:S(2)}) collective-permute-start(f32[64,128]{1,0:T(8,128)S(1)} %tails.1), channel_id=1, source_target_pairs={{0,16},{1,17},{2,18},{3,19},{4,20},{5,21},{6,22},{7,23},{8,24},{9,... | collective-permute-start | bytes 98312 | tf_op jit(solution)/shard_map/ppermute | solution.py:167
  57.6 3.4 %copy-start.6 = (s32[1,128,8]{1,2,0:T(8,128)S(1)}, s32[1,128,8]{1,2,0:T(8,128)}, u32[]{:S(2)}) copy-start(s32[1,128,8]{1,2,0:T(8,128)} %param.9) | copy-start | bytes 12292
  (4 other events, 3.5 us)

commit v2 on v1

v2 whole, which is shorter than its diff:
```python
import functools

import jax
import jax.numpy as jnp
from jax import lax
from jax.experimental import pallas as pl
from jax.experimental.pallas import tpu as pltpu
from jax.sharding import PartitionSpec as P

SLICES = 4
CAP = 12
PAD = 16
LANES = 128
BF = jnp.bfloat16
F32 = jnp.float32
PARAMS = pltpu.CompilerParams(vmem_limit_bytes=40 * 1024 * 1024)


def split(value):
    high = value.astype(BF)
    return high, (value - high.astype(F32)).astype(BF)


def select_kernel(flight, ids_hbm, gates_hbm, x_hbm, g_hbm, wg_hbm, wu_hbm, wd_hbm, *refs):
    blocks, (mix_ref, place_ref, pack_ref) = refs[:flight], refs[flight : flight + 3]
    ids_ref, gates_ref, x_ref, g_ref, sems = refs[flight + 3 :]
    width, hidden = wg_hbm.shape
    first = [
        pltpu.make_async_copy(src, dst, sems.at[i])
        for i, (src, dst) in enumerate(
            [(ids_hbm, ids_ref), (gates_hbm, gates_ref), (x_hbm, x_ref), (g_hbm, g_ref)]
        )
    ]
    later = [
        pltpu.make_async_copy(wg_hbm, pack_ref.at[pl.ds(0, width)], sems.at[4]),
        pltpu.make_async_copy(wu_hbm, pack_ref.at[pl.ds(width, width)], sems.at[5]),
    ]
    for k in range(width // hidden):
        part = pack_ref.at[pl.ds(2 * width + k * hidden, hidden)]
        later.append(pltpu.make_async_copy(wd_hbm.at[:, pl.ds(k * hidden, hidden)], part, sems.at[6 + k]))
    for copy in first + later:
        copy.start()
    own = lax.axis_index("expert") // SLICES
    first[0].wait()
    first[1].wait()
    ids = ids_ref[...]
    gates = gates_ref[...]
    count = ids.shape[1]
    routed, weight = [], []
    for s in range(flight):
        match = ids == (own ^ s)
        routed.append(jnp.sum(jnp.where(match, 1.0, 0.0), axis=0, keepdims=True))
        weight.append(jnp.sum(jnp.where(match, gates, 0.0), axis=0, keepdims=True))
    fill = [jnp.zeros((1, count), F32)] * (-flight % 8)
    table = jnp.concatenate(routed + fill, axis=0)
    earlier = lax.broadcasted_iota(jnp.int32, (count, count), 0) < lax.broadcasted_iota(
        jnp.int32, (count, count), 1
    )
    rank = jnp.dot(
        table.astype(BF), jnp.where(earlier, 1.0, 0.0).astype(BF), preferred_element_type=F32
    )
    key = jnp.where((table > 0.0) & (rank < float(CAP)), rank, -1.0)
    row = lax.broadcasted_iota(jnp.int32, (2 * CAP, count), 0)
    is_x = row < CAP
    slot = jnp.where(is_x, row, row - CAP).astype(F32)
    slot16 = lax.broadcasted_iota(jnp.int32, (PAD, count), 0)
    slot16 = jnp.where(slot16 < CAP, slot16, -2).astype(F32)
    picks_x, picks_g = [], []
    for s in range(flight):
        hit = key[s : s + 1] == slot
        picks_x.append(jnp.where(hit & is_x, 1.0, 0.0))
        picks_g.append(jnp.where(hit & ~is_x, 1.0, 0.0))
        at = jnp.where(key[s : s + 1] == slot16, 1.0, 0.0)
        place_ref[s * PAD : (s + 1) * PAD] = at
        for i, value in enumerate(split(at * weight[s])):
            mix_ref[:, (2 * s + i) * count : (2 * s + i + 1) * count] = value
    pick_x = jnp.concatenate(picks_x, axis=0).astype(BF)
    pick_g = jnp.concatenate(picks_g, axis=0).astype(BF)
    first[2].wait()
    rows = jnp.dot(pick_x, x_ref[...], preferred_element_type=F32)
    first[3].wait()
    rows = rows + jnp.dot(pick_g, g_ref[...], preferred_element_type=F32)
    rows = rows.astype(BF)
    for s in range(flight):
        blocks[s][...] = rows[s * 2 * CAP : (s + 1) * 2 * CAP]
    for copy in later:
        copy.wait()


def hidden_kernel(flight, *refs):
    blocks, packs = refs[: 2 * flight], refs[2 * flight : 2 * flight + 2]
    left_ref, part_ref = refs[2 * flight + 2 :]
    x = jnp.concatenate([b[:CAP] for b in blocks], axis=0)
    g = jnp.concatenate([b[CAP:] for b in blocks], axis=0)
    width = x.shape[1]
    hidden = packs[0].shape[1]
    nt = (((1,), (1,)), ((), ()))
    part = jnp.zeros((x.shape[0], 1), F32)
    for half, pack in enumerate(packs):
        a = jnp.dot(x, pack[:width], preferred_element_type=F32)
        u = jnp.dot(x, pack[width : 2 * width], preferred_element_type=F32)
        dh = jnp.zeros_like(a)
        for k in range(0, width, hidden):
            down = pack[2 * width + k : 2 * width + k + hidden]
            dh = dh + lax.dot_general(g[:, k : k + hidden], down, nt, preferred_element_type=F32)
        sig = jax.nn.sigmoid(a)
        act = a * sig
        part = part + jnp.sum(act * u * dh, axis=1, keepdims=True)
        at = 2 * half * hidden
        left_ref[:, at : at + hidden] = (dh * u * sig * (1.0 + a * (1.0 - sig))).astype(BF)
        left_ref[:, at + hidden : at + 2 * hidden] = (dh * act).astype(BF)
    high, low = split(part)
    high, low = high.astype(F32), low.astype(F32)
    lane = lax.broadcasted_iota(jnp.int32, (CAP, LANES), 1)
    tail = jnp.zeros((CAP, LANES), F32)
    for i in range(2 * flight):
        rows = slice(i * CAP, (i + 1) * CAP)
        tail = jnp.where(lane == 2 * i, high[rows], jnp.where(lane == 2 * i + 1, low[rows], tail))
    part_ref[...] = jnp.concatenate([tail, jnp.zeros((PAD - CAP, LANES), F32)], axis=0).astype(BF)


def inputs_kernel(flight, left_ref, own_ref, near_ref, keep_ref, send_ref):
    hidden = own_ref.shape[1]
    width = own_ref.shape[0] // 3
    nt = (((1,), (1,)), ((), ()))
    main = width * CAP // PAD
    step = width - main
    extra = PAD - CAP
    pieces = []
    for c in range(0, width, step):
        total = jnp.zeros((left_ref.shape[0], step), F32)
        for i in range(4):
            pack = (own_ref, near_ref)[i // 2]
            right = pack[i % 2 * width + c : i % 2 * width + c + step]
            left = left_ref[:, i * hidden : (i + 1) * hidden]
            total = total + lax.dot_general(left, right, nt, preferred_element_type=F32)
        pieces.append(total)
    last = pieces[-1]
    for i in range(2 * flight):
        base = i * CAP
        out_ref = (keep_ref, send_ref)[i // flight]
        at = i % flight * PAD
        for j, piece in enumerate(pieces[:-1]):
            under = last[base + extra * j : base + extra * (j + 1)]
            both = jnp.concatenate([piece[base : base + CAP], under], axis=0)
            out_ref[at : at + PAD, j * step : (j + 1) * step] = both.astype(out_ref.dtype)


def attach_kernel(flight, part_ref, keep_ref, send_ref, keep_out, send_out):
    del keep_ref, send_ref
    part = part_ref[...].astype(F32)
    lane = lax.broadcasted_iota(jnp.int32, part.shape, 1)
    for i in range(2 * flight):
        out_ref = (keep_out, send_out)[i // flight]
        at = i % flight * PAD
        tail = jnp.where((lane == 2 * i) | (lane == 2 * i + 1), part, 0.0)
        out_ref[at : at + PAD, out_ref.shape[1] - LANES :] = tail.astype(out_ref.dtype)


def add_kernel(flight, keep_ref, got_ref, mix_ref, *outs):
    main = keep_ref.shape[1] - LANES
    for s in range(flight):
        rows = pl.ds(s * PAD, PAD)
        total = keep_ref[rows] + got_ref[rows].astype(F32)
        outs[s][:, :main] = total[:, :main].astype(BF)
        high, low = split(jnp.sum(total[:, main:], axis=1, keepdims=True))
        lane = lax.broadcasted_iota(jnp.int32, (PAD, LANES), 1)
        tail = jnp.where(lane == 0, high.astype(F32), jnp.where(lane == 1, low.astype(F32), 0.0))
        outs[s][:, main : main + LANES] = tail.astype(BF)
    outs[0][:, main + LANES :] = mix_ref[...]


def mix_kernel(flight, ids_ref, place_ref, *refs):
    blocks, (out_ref, gates_ref) = refs[:flight], refs[flight:]
    count, width = out_ref.shape
    main = width * CAP // PAD
    step = width - main
    tn = (((0,), (0,)), ((), ()))
    base = main + LANES
    left = jnp.concatenate(
        [
            blocks[0][:, base + (2 * s + i) * count : base + (2 * s + i + 1) * count]
            for i in range(2)
            for s in range(flight)
        ],
        axis=0,
    )

    def blend(rows):
        right = jnp.concatenate([rows, rows], axis=0)
        return lax.dot_general(left, right, tn, preferred_element_type=F32).astype(BF)

    out_ref[:, :main] = blend(jnp.concatenate([b[:, :main] for b in blocks], axis=0))
    zero = jnp.zeros((PAD - CAP, step), BF)
    folded = []
    for s in range(flight):
        for j in range(main // step):
            folded.append(blocks[s][CAP:, j * step : (j + 1) * step])
        folded.append(zero)
    out_ref[:, main:] = blend(jnp.concatenate(folded, axis=0))
    own = lax.axis_index("expert") // SLICES
    ids = ids_ref[...]
    total = jnp.zeros(ids.shape, F32)
    for s in range(flight):
        q = jnp.sum(blocks[s][:, main:base].astype(F32), axis=1, keepdims=True)
        back = jnp.sum(place_ref[s * PAD : (s + 1) * PAD] * q, axis=0, keepdims=True)
        total = total + jnp.where(ids == (own ^ s), back, 0.0)
    gates_ref[...] = total


def moved(value, sections, devices, stage, flip, bits, only=None):
    route = []
    for p in range(sections):
        for e in range(devices):
            if only is not None and e % 2 != only:
                continue
            route.append((p * devices + e, (p + flip) % sections * devices + (e ^ bits)))
    return lax.ppermute(value, stage, route)


def per_device(inputs, out_grads, expert_ids, gate_values, w_gate, w_up, w_down):
    devices = lax.axis_size("expert")
    sections = lax.axis_size("pipe")
    flight = devices // SLICES
    count, width = inputs.shape[1:]
    axes = ("pipe", "expert")
    go = functools.partial(moved, sections=sections, devices=devices, stage=axes)
    ids = expert_ids[0].T
    gates = gate_values[0].T
    hidden = w_gate.shape[2]
    args = (ids, gates, inputs[0], out_grads[0], w_gate[0], w_up[0], w_down[0])
    shape = jax.ShapeDtypeStruct
    main = width * CAP // PAD
    *blocks, mix, place, pack = pl.pallas_call(
        functools.partial(select_kernel, flight),
        out_shape=[shape((2 * CAP, width), BF)] * flight
        + [shape((PAD, 2 * flight * count), BF), shape((flight * PAD, count), F32)]
        + [shape((3 * width, hidden), BF)],
        in_specs=[pl.BlockSpec(memory_space=pltpu.HBM)] * 7,
        scratch_shapes=[
            pltpu.VMEM(ids.shape, jnp.int32),
            pltpu.VMEM(gates.shape, F32),
            pltpu.VMEM((count, width), BF),
            pltpu.VMEM((count, width), BF),
            pltpu.SemaphoreType.DMA((6 + width // hidden,)),
        ],
        compiler_params=PARAMS,
        name="select",
    )(*[pltpu.with_memory_space_constraint(v, pltpu.HBM) for v in args])
    near = go(pack, flip=0, bits=1)
    rows = [blocks[0]] + [go(blocks[s], flip=0, bits=SLICES * s) for s in range(1, flight)]
    across = [go(rows[0], flip=0, bits=2)]
    rows[-1], near = lax.optimization_barrier((rows[-1], near))
    rows = rows + across + [go(r, flip=0, bits=2) for r in rows[1:]]
    left, part = pl.pallas_call(
        functools.partial(hidden_kernel, flight),
        out_shape=[shape((2 * flight * CAP, 4 * hidden), BF), shape((PAD, LANES), BF)],
        compiler_params=PARAMS,
        name="hidden",
    )(*rows, pack, near)
    part = go(part, flip=1, bits=0)
    r_shapes = [shape((flight * PAD, main + LANES), t) for t in (F32, BF)]
    r_keep, r_send = pl.pallas_call(
        functools.partial(inputs_kernel, flight),
        out_shape=r_shapes,
        compiler_params=PARAMS,
        name="inputs_back",
    )(left, pack, near)
    r_keep, r_send = pl.pallas_call(
        functools.partial(attach_kernel, flight),
        out_shape=r_shapes,
        input_output_aliases={1: 0, 2: 1},
        compiler_params=PARAMS,
        name="attach_gate_parts",
    )(part, r_keep, r_send)
    r_got = go(r_send, flip=0, bits=2)
    extra = 2 * flight * count
    r_parts = pl.pallas_call(
        functools.partial(add_kernel, flight),
        out_shape=[shape((PAD, main + LANES + (extra if s == 0 else 0)), BF) for s in range(flight)],
        compiler_params=PARAMS,
        name="add_inputs_back",
    )(r_keep, r_got, mix)
    r_home = [go(r_parts[s], flip=-1, bits=SLICES * s) for s in range(flight)]
    moe, d_gates = pl.pallas_call(
        functools.partial(mix_kernel, flight),
        out_shape=[shape((count, width), BF), shape(ids.shape, F32)],
        compiler_params=PARAMS,
        name="mix",
    )(ids, place, *r_home)
    return (moe[None], d_gates.T[None])


def solution(mesh):
    return jax.shard_map(
        per_device,
        mesh=mesh,
        in_specs=(
            P("pipe", "expert", None),
            P("pipe", "expert", None),
            P("pipe", "expert", None),
            P("pipe", "expert", None),
            P("pipe", None, "expert"),
            P("pipe", None, "expert"),
            P("pipe", "expert", None),
        ),
        out_specs=(P("pipe", "expert", None), P("pipe", "expert", None)),
        check_vma=False,
    )
```

time: 61.9 us -> 47.9 us (0.77)
  starting transfers between devices: 34.8 us -> 19.8 us
  local copies, waits for them, and re-layouts: 5.92 us -> 0.01 us
  waiting for transfers between devices: 15 us -> 20.9 us
  Pallas kernels: 5.18 us -> 6.44 us
    ppermute x20 -> x14, starting transfers between devices: 34.8 us -> 19.8 us  [moved(): return lax.ppermute(value, stage, route)]
    unnamed x16 -> x2, local copies, waits for them, and re-layouts: 5.91 us -> 0.01 us
    ppermute x20 -> x14, waiting for transfers between devices: 15 us -> 20.9 us  [moved(): return lax.ppermute(value, stage, route)]
    pallas_call x5 -> x6, Pallas kernels: 5.18 us -> 6.44 us  [the longest x1 2.3 us: per_device(): pl.pallas_call(functools.partial(select_kernel, flight), out_shape=[shape...]
  transfers between devices with their start and end apart: 20 -> 14, of which waited for: 9 -> 7; matrix products, arithmetic and copies ran while one was open for 0% -> 0% of each run, Pallas kernels for 3% -> 3%
where the time goes in v2:
time: 47.9 us; the launch traced here: 47.7 us
  waiting for transfers between devices  20.9 us (44%)
  starting transfers between devices  19.8 us (41%)
  Pallas kernels  6.44 us (13%)
  between operations  0.67 us (1%)
    ppermute x14, waiting for transfers between devices, moved(): return lax.ppermute(value, stage, route)  20.9 us
    ppermute x14, starting transfers between devices, moved(): return lax.ppermute(value, stage, route)  19.8 us
    pallas_call x1, Pallas kernels, per_device(): pl.pallas_call(functools.partial(select_kernel, flight), out_shape=[shape...  2.3 us
    pallas_call x1, Pallas kernels, per_device(): pl.pallas_call(functools.partial(hidden_kernel, flight), out_shape=[shape...  1.54 us
    pallas_call x1, Pallas kernels, per_device(): pl.pallas_call(functools.partial(inputs_kernel, flight), out_shape=r_shap...  1.39 us
    pallas_call x1, Pallas kernels, per_device(): pl.pallas_call(functools.partial(mix_kernel, flight), out_shape=[shape((c...  1.12 us
  transfers between devices with their start and end apart: 14, of which 7 were waited for; matrix products, arithmetic and copies ran while one was open for 0% of the time, Pallas kernels for 3%

profile of v2, /device:TPU:0, one launch (start us, length us, event | category | flops | bytes accessed | tf_op | source)
XLA Modules:
  0.0 47.7 jit_solution(2059590178100071367)
XLA Ops:
  0.6 2.3 %select.1 = (bf16[24,2048]{1,0:T(8,128)(2,1)S(1)}, bf16[24,2048]{1,0:T(8,128)(2,1)S(1)}, bf16[24,2048]{1,0:T(8,128)(2,1)S(1)}, bf16[24,2048]{1,0:T(8,128)(2,1)S(...) custom-call(s32[8,128]{1,0:T(8,128)} %bitcast.15, f32[8,128]{1,0:T(8,128)} %bitcast.22, ...), custom_call_target="tpu_custom_call" | custom-call | tf_op jit(solution)/shard_map/select/pallas_call | solution.py:234
  2.9 0.5 %collective-permute-start.3 = (bf16[6144,256]{1,0:T(8,128)(2,1)S(1)}, bf16[6144,256]{1,0:T(8,128)(2,1)S(1)}, u32[]{:S(2)}, u32[]{:S(2)}) collective-permute-start(bf16[6144,256]{1,0:T(8,128)(2,1)S(1)} %get-tuple-element.28.refs_8_.own_ref), channel_id=1, source_target_pairs={{0,1},{1,0},{2,3},{3,2},{4,5},{5,4},{6,7},{7,6},{8,9},{9,8},{10,11... | collective-permute-start | bytes 9437192 | tf_op jit(solution)/shard_map/ppermute | solution.py:218
  3.5 2.6 %collective-permute-start = (bf16[24,2048]{1,0:T(8,128)(2,1)S(1)}, bf16[24,2048]{1,0:T(8,128)(2,1)S(1)}, u32[]{:S(2)}, u32[]{:S(2)}) collective-permute-start(bf16[24,2048]{1,0:T(8,128)(2,1)S(1)} %get-tuple-element.25), channel_id=1, source_target_pairs={{0,4},{1,5},{2,6},{3,7},{4,0},{5,1},{6,2},{7,3},{8,12},{9,13},{10,... | collective-permute-start | bytes 294920 | tf_op jit(solution)/shard_map/ppermute | solution.py:218
  6.1 2.6 %collective-permute-start.1 = (bf16[24,2048]{1,0:T(8,128)(2,1)S(1)}, bf16[24,2048]{1,0:T(8,128)(2,1)S(1)}, u32[]{:S(2)}, u32[]{:S(2)}) collective-permute-start(bf16[24,2048]{1,0:T(8,128)(2,1)S(1)} %get-tuple-element.26), channel_id=1, source_target_pairs={{0,8},{1,9},{2,10},{3,11},{4,12},{5,13},{6,14},{7,15},{8,0},{9,1},... | collective-permute-start | bytes 294920 | tf_op jit(solution)/shard_map/ppermute | solution.py:218
  8.7 1.7 %collective-permute-start.4 = (bf16[24,2048]{1,0:T(8,128)(2,1)S(1)}, bf16[24,2048]{1,0:T(8,128)(2,1)S(1)}, u32[]{:S(2)}, u32[]{:S(2)}) collective-permute-start(bf16[24,2048]{1,0:T(8,128)(2,1)S(1)} %get-tuple-element.24.refs_0_), channel_id=1, source_target_pairs={{0,2},{1,3},{2,0},{3,1},{4,6},{5,7},{6,4},{7,5},{8,10},{9,11},{10,... | collective-permute-start | bytes 294920 | tf_op jit(solution)/shard_map/ppermute | solution.py:218
  10.4 0.8 %collective-permute-start.5 = (bf16[24,2048]{1,0:T(8,128)(2,1)S(1)}, bf16[24,2048]{1,0:T(8,128)(2,1)S(1)}, u32[]{:S(2)}, u32[]{:S(2)}) collective-permute-start(bf16[24,2048]{1,0:T(8,128)(2,1)S(1)} %collective-permute-done.refs_1_), channel_id=1, source_target_pairs={{0,2},{1,3},{2,0},{3,1},{4,6},{5,7},{6,4},{7,5},{8,10},{9,11},{10,... | collective-permute-start | bytes 294920 | tf_op jit(solution)/shard_map/ppermute | solution.py:218
  11.2 5.7 %collective-permute-done.1.refs_2_ = bf16[24,2048]{1,0:T(8,128)(2,1)S(1)} collective-permute-done((bf16[24,2048]{1,0:T(8,128)(2,1)S(1)}, bf16[24,2048]{1,0:T(8,128)(2,1)S(1)}, u32[]{:S(2)}, u32[]{:S(2)}) %collective-permute-start.1) | collective-permute-done | bytes 98336 | tf_op jit(solution)/shard_map/ppermute | solution.py:218
  16.9 1.5 %collective-permute-start.6 = (bf16[24,2048]{1,0:T(8,128)(2,1)S(1)}, bf16[24,2048]{1,0:T(8,128)(2,1)S(1)}, u32[]{:S(2)}, u32[]{:S(2)}) collective-permute-start(bf16[24,2048]{1,0:T(8,128)(2,1)S(1)} %collective-permute-done.1.refs_2_), channel_id=1, source_target_pairs={{0,2},{1,3},{2,0},{3,1},{4,6},{5,7},{6,4},{7,5},{8,10},{9,11},{10,... | collective-permute-start | bytes 294920 | tf_op jit(solution)/shard_map/ppermute | solution.py:218
  18.4 0.5 %collective-permute-start.7 = (bf16[24,2048]{1,0:T(8,128)(2,1)S(1)}, bf16[24,2048]{1,0:T(8,128)(2,1)S(1)}, u32[]{:S(2)}, u32[]{:S(2)}) collective-permute-start(bf16[24,2048]{1,0:T(8,128)(2,1)S(1)} %collective-permute-done.2.refs_3_), channel_id=1, source_target_pairs={{0,2},{1,3},{2,0},{3,1},{4,6},{5,7},{6,4},{7,5},{8,10},{9,11},{10,... | collective-permute-start | bytes 294920 | tf_op jit(solution)/shard_map/ppermute | solution.py:218
  18.9 2.6 %collective-permute-done.6.refs_6_ = bf16[24,2048]{1,0:T(8,128)(2,1)S(1)} collective-permute-done((bf16[24,2048]{1,0:T(8,128)(2,1)S(1)}, bf16[24,2048]{1,0:T(8,128)(2,1)S(1)}, u32[]{:S(2)}, u32[]{:S(2)}) %collective-permute-start.6) | collective-permute-done | bytes 98336 | tf_op jit(solution)/shard_map/ppermute | solution.py:218
  21.5 1.5 %collective-permute-done.7.refs_7_ = bf16[24,2048]{1,0:T(8,128)(2,1)S(1)} collective-permute-done((bf16[24,2048]{1,0:T(8,128)(2,1)S(1)}, bf16[24,2048]{1,0:T(8,128)(2,1)S(1)}, u32[]{:S(2)}, u32[]{:S(2)}) %collective-permute-start.7) | collective-permute-done | bytes 98336 | tf_op jit(solution)/shard_map/ppermute | solution.py:218
  23.0 1.5 %hidden.1 = (bf16[96,1024]{1,0:T(8,128)(2,1)S(1)}, bf16[16,128]{1,0:T(8,128)(2,1)S(1)}) custom-call(bf16[24,2048]{1,0:T(8,128)(2,1)S(1)} %get-tuple-element.24.refs_0_, bf16[24,2048]{1,0:T(8,128)(2,1)S(1)} %collective-permute-done.refs_1_, bf16[24,2048]{1,0:T(8,128)(2,1)S(1)} %collective-permute-done.1.refs_2_, ...), custom_call_target="tpu_custom_call" | custom-call | tf_op jit(solution)/shard_map/hidden/pallas_call | solution.py:255
  24.5 1.6 %collective-permute-start.8 = (bf16[16,128]{1,0:T(8,128)(2,1)S(1)}, bf16[16,128]{1,0:T(8,128)(2,1)S(1)}, u32[]{:S(2)}, u32[]{:S(2)}) collective-permute-start(bf16[16,128]{1,0:T(8,128)(2,1)S(1)} %get-tuple-element.31), channel_id=1, source_target_pairs={{0,16},{1,17},{2,18},{3,19},{4,20},{5,21},{6,22},{7,23},{8,24},{9,... | collective-permute-start | bytes 12296 | tf_op jit(solution)/shard_map/ppermute | solution.py:218
  26.1 1.4 %inputs_back.1 = (f32[64,1664]{1,0:T(8,128)S(1)}, bf16[64,1664]{1,0:T(8,128)(2,1)S(1)}) custom-call(bf16[96,1024]{1,0:T(8,128)(2,1)S(1)} %get-tuple-element.32.left_ref, bf16[6144,256]{1,0:T(8,128)(2,1)S(1)} %get-tuple-element.28.refs_8_.own_ref, bf16[6144,256]{1,0:T(8,128)(2,1)S(1)} %collective-permute-done.3.refs_9_.near_ref), custom_call_target="tpu_custom_call" | custom-call | tf_op jit(solution)/shard_map/inputs_back/pallas_call | solution.py:263
  27.5 0.7 %collective-permute-done.8.part_ref = bf16[16,128]{1,0:T(8,128)(2,1)S(1)} collective-permute-done((bf16[16,128]{1,0:T(8,128)(2,1)S(1)}, bf16[16,128]{1,0:T(8,128)(2,1)S(1)}, u32[]{:S(2)}, u32[]{:S(2)}) %collective-permute-start.8) | collective-permute-done | bytes 4128 | tf_op jit(solution)/shard_map/ppermute | solution.py:218
  28.2 1.1 %collective-permute-start.9 = (bf16[64,1664]{1,0:T(8,128)(2,1)S(1)}, bf16[64,1664]{1,0:T(8,128)(2,1)S(1)}, u32[]{:S(2)}, u32[]{:S(2)}) collective-permute-start(bf16[64,1664]{1,0:T(8,128)(2,1)S(1)} %get-tuple-element.36), channel_id=1, source_target_pairs={{0,2},{1,3},{2,0},{3,1},{4,6},{5,7},{6,4},{7,5},{8,10},{9,11},{10,... | collective-permute-start | bytes 638984 | tf_op jit(solution)/shard_map/ppermute | solution.py:218
  29.3 4.8 %collective-permute-done.9.got_ref = bf16[64,1664]{1,0:T(8,128)(2,1)S(1)} collective-permute-done((bf16[64,1664]{1,0:T(8,128)(2,1)S(1)}, bf16[64,1664]{1,0:T(8,128)(2,1)S(1)}, u32[]{:S(2)}, u32[]{:S(2)}) %collective-permute-start.9) | collective-permute-done | bytes 213024 | tf_op jit(solution)/shard_map/ppermute | solution.py:218
  34.2 1.6 %collective-permute-start.10 = (bf16[16,2688]{1,0:T(8,128)(2,1)S(1)}, bf16[16,2688]{1,0:T(8,128)(2,1)S(1)}, u32[]{:S(2)}, u32[]{:S(2)}) collective-permute-start(bf16[16,2688]{1,0:T(8,128)(2,1)S(1)} %get-tuple-element.38), channel_id=1, source_target_pairs={{0,16},{1,17},{2,18},{3,19},{4,20},{5,21},{6,22},{7,23},{8,24},{9,... | collective-permute-start | bytes 258056 | tf_op jit(solution)/shard_map/ppermute | solution.py:218
  35.8 0.3 collective-permute-start.11
  36.1 3.6 %collective-permute-start.12 = (bf16[16,1664]{1,0:T(8,128)(2,1)S(1)}, bf16[16,1664]{1,0:T(8,128)(2,1)S(1)}, u32[]{:S(2)}, u32[]{:S(2)}) collective-permute-start(bf16[16,1664]{1,0:T(8,128)(2,1)S(1)} %get-tuple-element.40), channel_id=1, source_target_pairs={{0,24},{1,25},{2,26},{3,27},{4,28},{5,29},{6,30},{7,31},{8,16},{9,... | collective-permute-start | bytes 159752 | tf_op jit(solution)/shard_map/ppermute | solution.py:218
  39.8 1.3 %collective-permute-start.13 = (bf16[16,1664]{1,0:T(8,128)(2,1)S(1)}, bf16[16,1664]{1,0:T(8,128)(2,1)S(1)}, u32[]{:S(2)}, u32[]{:S(2)}) collective-permute-start(bf16[16,1664]{1,0:T(8,128)(2,1)S(1)} %get-tuple-element.41), channel_id=1, source_target_pairs={{0,28},{1,29},{2,30},{3,31},{4,24},{5,25},{6,26},{7,27},{8,20},{9,... | collective-permute-start | bytes 159752 | tf_op jit(solution)/shard_map/ppermute | solution.py:218
  41.1 1.0 %collective-permute-done.12.refs_2_ = bf16[16,1664]{1,0:T(8,128)(2,1)S(1)} collective-permute-done((bf16[16,1664]{1,0:T(8,128)(2,1)S(1)}, bf16[16,1664]{1,0:T(8,128)(2,1)S(1)}, u32[]{:S(2)}, u32[]{:S(2)}) %collective-permute-start.12) | collective-permute-done | bytes 53280 | tf_op jit(solution)/shard_map/ppermute | solution.py:218
  42.1 4.5 %collective-permute-done.13.refs_3_ = bf16[16,1664]{1,0:T(8,128)(2,1)S(1)} collective-permute-done((bf16[16,1664]{1,0:T(8,128)(2,1)S(1)}, bf16[16,1664]{1,0:T(8,128)(2,1)S(1)}, u32[]{:S(2)}, u32[]{:S(2)}) %collective-permute-start.13) | collective-permute-done | bytes 53280 | tf_op jit(solution)/shard_map/ppermute | solution.py:218
  46.6 1.1 %mix.1 = (bf16[128,2048]{1,0:T(8,128)(2,1)}, f32[8,128]{1,0:T(8,128)}) custom-call(s32[8,128]{1,0:T(8,128)S(1)} %bitcast.16, f32[64,128]{1,0:T(8,128)S(1)} %get-tuple-element.23.place_ref, bf16[16,2688]{1,0:T(8,128)(2,1)S(1)} %collective-permute-done.10.refs_0_, bf16[16,1664]{1,0:T(8,128)(2,1)S(1)} %collective-permute-done.11.refs_1_, ...), custom_call_target="tpu_custom_call" | custom-call | tf_op jit(solution)/shard_map/mix/pallas_call | solution.py:285
  (12 shorter events, 0.1 us)
Async XLA Ops:
  2.9 15.4 %collective-permute-start.3 = (bf16[6144,256]{1,0:T(8,128)(2,1)S(1)}, bf16[6144,256]{1,0:T(8,128)(2,1)S(1)}, u32[]{:S(2)}, u32[]{:S(2)}) collective-permute-start(bf16[6144,256]{1,0:T(8,128)(2,1)S(1)} %get-tuple-element.28.refs_8_.own_ref), channel_id=1, source_target_pairs={{0,1},{1,0},{2,3},{3,2},{4,5},{5,4},{6,7},{7,6},{8,9},{9,8},{10,11... | collective-permute-start | bytes 9437192 | tf_op jit(solution)/shard_map/ppermute | solution.py:218
  3.5 7.0 %collective-permute-start = (bf16[24,2048]{1,0:T(8,128)(2,1)S(1)}, bf16[24,2048]{1,0:T(8,128)(2,1)S(1)}, u32[]{:S(2)}, u32[]{:S(2)}) collective-permute-start(bf16[24,2048]{1,0:T(8,128)(2,1)S(1)} %get-tuple-element.25), channel_id=1, source_target_pairs={{0,4},{1,5},{2,6},{3,7},{4,0},{5,1},{6,2},{7,3},{8,12},{9,13},{10,... | collective-permute-start | bytes 294920 | tf_op jit(solution)/shard_map/ppermute | solution.py:218
  6.1 10.8 %collective-permute-start.1 = (bf16[24,2048]{1,0:T(8,128)(2,1)S(1)}, bf16[24,2048]{1,0:T(8,128)(2,1)S(1)}, u32[]{:S(2)}, u32[]{:S(2)}) collective-permute-start(bf16[24,2048]{1,0:T(8,128)(2,1)S(1)} %get-tuple-element.26), channel_id=1, source_target_pairs={{0,8},{1,9},{2,10},{3,11},{4,12},{5,13},{6,14},{7,15},{8,0},{9,1},... | collective-permute-start | bytes 294920 | tf_op jit(solution)/shard_map/ppermute | solution.py:218
  8.7 9.7 %collective-permute-start.2 = (bf16[24,2048]{1,0:T(8,128)(2,1)S(1)}, bf16[24,2048]{1,0:T(8,128)(2,1)S(1)}, u32[]{:S(2)}, u32[]{:S(2)}) collective-permute-start(bf16[24,2048]{1,0:T(8,128)(2,1)S(1)} %get-tuple-element.27), channel_id=1, source_target_pairs={{0,12},{1,13},{2,14},{3,15},{4,8},{5,9},{6,10},{7,11},{8,4},{9,5},... | collective-permute-start | bytes 294920 | tf_op jit(solution)/shard_map/ppermute | solution.py:218
  8.7 10.2 %collective-permute-start.4 = (bf16[24,2048]{1,0:T(8,128)(2,1)S(1)}, bf16[24,2048]{1,0:T(8,128)(2,1)S(1)}, u32[]{:S(2)}, u32[]{:S(2)}) collective-permute-start(bf16[24,2048]{1,0:T(8,128)(2,1)S(1)} %get-tuple-element.24.refs_0_), channel_id=1, source_target_pairs={{0,2},{1,3},{2,0},{3,1},{4,6},{5,7},{6,4},{7,5},{8,10},{9,11},{10,... | collective-permute-start | bytes 294920 | tf_op jit(solution)/shard_map/ppermute | solution.py:218
  10.4 8.5 %collective-permute-start.5 = (bf16[24,2048]{1,0:T(8,128)(2,1)S(1)}, bf16[24,2048]{1,0:T(8,128)(2,1)S(1)}, u32[]{:S(2)}, u32[]{:S(2)}) collective-permute-start(bf16[24,2048]{1,0:T(8,128)(2,1)S(1)} %collective-permute-done.refs_1_), channel_id=1, source_target_pairs={{0,2},{1,3},{2,0},{3,1},{4,6},{5,7},{6,4},{7,5},{8,10},{9,11},{10,... | collective-permute-start | bytes 294920 | tf_op jit(solution)/shard_map/ppermute | solution.py:218
  16.9 4.6 %collective-permute-start.6 = (bf16[24,2048]{1,0:T(8,128)(2,1)S(1)}, bf16[24,2048]{1,0:T(8,128)(2,1)S(1)}, u32[]{:S(2)}, u32[]{:S(2)}) collective-permute-start(bf16[24,2048]{1,0:T(8,128)(2,1)S(1)} %collective-permute-done.1.refs_2_), channel_id=1, source_target_pairs={{0,2},{1,3},{2,0},{3,1},{4,6},{5,7},{6,4},{7,5},{8,10},{9,11},{10,... | collective-permute-start | bytes 294920 | tf_op jit(solution)/shard_map/ppermute | solution.py:218
  18.4 4.6 %collective-permute-start.7 = (bf16[24,2048]{1,0:T(8,128)(2,1)S(1)}, bf16[24,2048]{1,0:T(8,128)(2,1)S(1)}, u32[]{:S(2)}, u32[]{:S(2)}) collective-permute-start(bf16[24,2048]{1,0:T(8,128)(2,1)S(1)} %collective-permute-done.2.refs_3_), channel_id=1, source_target_pairs={{0,2},{1,3},{2,0},{3,1},{4,6},{5,7},{6,4},{7,5},{8,10},{9,11},{10,... | collective-permute-start | bytes 294920 | tf_op jit(solution)/shard_map/ppermute | solution.py:218
  24.5 3.7 %collective-permute-start.8 = (bf16[16,128]{1,0:T(8,128)(2,1)S(1)}, bf16[16,128]{1,0:T(8,128)(2,1)S(1)}, u32[]{:S(2)}, u32[]{:S(2)}) collective-permute-start(bf16[16,128]{1,0:T(8,128)(2,1)S(1)} %get-tuple-element.31), channel_id=1, source_target_pairs={{0,16},{1,17},{2,18},{3,19},{4,20},{5,21},{6,22},{7,23},{8,24},{9,... | collective-permute-start | bytes 12296 | tf_op jit(solution)/shard_map/ppermute | solution.py:218
  26.1 20.5 %copy-start = (s32[1,128,8]{1,2,0:T(8,128)S(1)}, s32[1,128,8]{1,2,0:T(8,128)}, u32[]{:S(2)}) copy-start(s32[1,128,8]{1,2,0:T(8,128)} %param.9) | copy-start | bytes 12292
  28.2 5.9 %collective-permute-start.9 = (bf16[64,1664]{1,0:T(8,128)(2,1)S(1)}, bf16[64,1664]{1,0:T(8,128)(2,1)S(1)}, u32[]{:S(2)}, u32[]{:S(2)}) collective-permute-start(bf16[64,1664]{1,0:T(8,128)(2,1)S(1)} %get-tuple-element.36), channel_id=1, source_target_pairs={{0,2},{1,3},{2,0},{3,1},{4,6},{5,7},{6,4},{7,5},{8,10},{9,11},{10,... | collective-permute-start | bytes 638984 | tf_op jit(solution)/shard_map/ppermute | solution.py:218
  34.2 12.4 %collective-permute-start.10 = (bf16[16,2688]{1,0:T(8,128)(2,1)S(1)}, bf16[16,2688]{1,0:T(8,128)(2,1)S(1)}, u32[]{:S(2)}, u32[]{:S(2)}) collective-permute-start(bf16[16,2688]{1,0:T(8,128)(2,1)S(1)} %get-tuple-element.38), channel_id=1, source_target_pairs={{0,16},{1,17},{2,18},{3,19},{4,20},{5,21},{6,22},{7,23},{8,24},{9,... | collective-permute-start | bytes 258056 | tf_op jit(solution)/shard_map/ppermute | solution.py:218
  35.8 5.3 %collective-permute-start.11 = (bf16[16,1664]{1,0:T(8,128)(2,1)S(1)}, bf16[16,1664]{1,0:T(8,128)(2,1)S(1)}, u32[]{:S(2)}, u32[]{:S(2)}) collective-permute-start(bf16[16,1664]{1,0:T(8,128)(2,1)S(1)} %get-tuple-element.39), channel_id=1, source_target_pairs={{0,20},{1,21},{2,22},{3,23},{4,16},{5,17},{6,18},{7,19},{8,28},{9,... | collective-permute-start | bytes 159752 | tf_op jit(solution)/shard_map/ppermute | solution.py:218
  36.1 5.9 %collective-permute-start.12 = (bf16[16,1664]{1,0:T(8,128)(2,1)S(1)}, bf16[16,1664]{1,0:T(8,128)(2,1)S(1)}, u32[]{:S(2)}, u32[]{:S(2)}) collective-permute-start(bf16[16,1664]{1,0:T(8,128)(2,1)S(1)} %get-tuple-element.40), channel_id=1, source_target_pairs={{0,24},{1,25},{2,26},{3,27},{4,28},{5,29},{6,30},{7,31},{8,16},{9,... | collective-permute-start | bytes 159752 | tf_op jit(solution)/shard_map/ppermute | solution.py:218
  39.8 6.8 %collective-permute-start.13 = (bf16[16,1664]{1,0:T(8,128)(2,1)S(1)}, bf16[16,1664]{1,0:T(8,128)(2,1)S(1)}, u32[]{:S(2)}, u32[]{:S(2)}) collective-permute-start(bf16[16,1664]{1,0:T(8,128)(2,1)S(1)} %get-tuple-element.41), channel_id=1, source_target_pairs={{0,28},{1,29},{2,30},{3,31},{4,24},{5,25},{6,26},{7,27},{8,20},{9,... | collective-permute-start | bytes 159752 | tf_op jit(solution)/shard_map/ppermute | solution.py:218

commit v3 on v2

v3 whole, which is shorter than its diff:
```python
import functools

import jax
import jax.numpy as jnp
from jax import lax
from jax.experimental import pallas as pl
from jax.experimental.pallas import tpu as pltpu
from jax.sharding import PartitionSpec as P

SLICES = 4
CAP = 12
PAD = 16
LANES = 128
BF = jnp.bfloat16
F32 = jnp.float32
PARAMS = pltpu.CompilerParams(vmem_limit_bytes=40 * 1024 * 1024)


def split(value):
    high = value.astype(BF)
    return high, (value - high.astype(F32)).astype(BF)


def weight_copies(wg_hbm, wu_hbm, wd_hbm, pack_ref, sems):
    width, hidden = wg_hbm.shape
    copies = [
        pltpu.make_async_copy(wg_hbm, pack_ref.at[pl.ds(0, width)], sems.at[0]),
        pltpu.make_async_copy(wu_hbm, pack_ref.at[pl.ds(width, width)], sems.at[1]),
    ]
    for k in range(width // hidden):
        part = pack_ref.at[pl.ds(2 * width + k * hidden, hidden)]
        copies.append(pltpu.make_async_copy(wd_hbm.at[:, pl.ds(k * hidden, hidden)], part, sems.at[2 + k]))
    return copies


def select_kernel(flight, ids_hbm, gates_hbm, x_hbm, g_hbm, wg_hbm, wu_hbm, wd_hbm, *refs):
    blocks, (mix_ref, place_ref, pack_ref) = refs[:flight], refs[flight : flight + 3]
    ids_ref, gates_ref, x_ref, g_ref, sems, pack_sems = refs[flight + 3 :]
    later = weight_copies(wg_hbm, wu_hbm, wd_hbm, pack_ref, pack_sems)
    first = [
        pltpu.make_async_copy(src, dst, sems.at[i])
        for i, (src, dst) in enumerate(
            [(ids_hbm, ids_ref), (gates_hbm, gates_ref), (x_hbm, x_ref), (g_hbm, g_ref)]
        )
    ]
    for copy in first + later:
        copy.start()
    own = lax.axis_index("expert") // SLICES
    parity = lax.axis_index("expert") % 2
    first[0].wait()
    first[1].wait()
    ids = ids_ref[...]
    gates = gates_ref[...]
    count = ids.shape[1]
    routed, weight = [], []
    for s in range(flight):
        match = ids == (own ^ s ^ parity)
        routed.append(jnp.sum(jnp.where(match, 1.0, 0.0), axis=0, keepdims=True))
        weight.append(jnp.sum(jnp.where(match, gates, 0.0), axis=0, keepdims=True))
    fill = [jnp.zeros((1, count), F32)] * (-flight % 8)
    table = jnp.concatenate(routed + fill, axis=0)
    earlier = lax.broadcasted_iota(jnp.int32, (count, count), 0) < lax.broadcasted_iota(
        jnp.int32, (count, count), 1
    )
    rank = jnp.dot(
        table.astype(BF), jnp.where(earlier, 1.0, 0.0).astype(BF), preferred_element_type=F32
    )
    key = jnp.where((table > 0.0) & (rank < float(CAP)), rank, -1.0)
    row = lax.broadcasted_iota(jnp.int32, (2 * CAP, count), 0)
    is_x = row < CAP
    slot = jnp.where(is_x, row, row - CAP).astype(F32)
    slot16 = lax.broadcasted_iota(jnp.int32, (PAD, count), 0)
    slot16 = jnp.where(slot16 < CAP, slot16, -2).astype(F32)
    picks_x, picks_g = [], []
    for s in [*range(0, flight, 2), *range(1, flight, 2)]:
        hit = key[s : s + 1] == slot
        picks_x.append(jnp.where(hit & is_x, 1.0, 0.0))
        picks_g.append(jnp.where(hit & ~is_x, 1.0, 0.0))
        at = jnp.where(key[s : s + 1] == slot16, 1.0, 0.0)
        place_ref[s * PAD : (s + 1) * PAD] = at
        for i, value in enumerate(split(at * weight[s])):
            mix_ref[:, (2 * s + i) * count : (2 * s + i + 1) * count] = value
    pick_x = jnp.concatenate(picks_x, axis=0).astype(BF)
    pick_g = jnp.concatenate(picks_g, axis=0).astype(BF)
    first[2].wait()
    rows = jnp.dot(pick_x, x_ref[...], preferred_element_type=F32)
    first[3].wait()
    rows = rows + jnp.dot(pick_g, g_ref[...], preferred_element_type=F32)
    rows = rows.astype(BF)
    for i in range(flight):
        blocks[i][...] = rows[i * 2 * CAP : (i + 1) * 2 * CAP]
    for copy in later:
        copy.wait()


def join_kernel(mine_ref, got_ref, out_ref):
    out_ref[: 2 * CAP] = mine_ref[...]
    out_ref[2 * CAP :] = got_ref[...]


def hidden_kernel(many, *refs):
    blocks, packs = refs[:many], refs[many : many + 2]
    left_ref, part_ref = refs[many + 2 :]
    step = 2 * CAP
    spots = [(b, at) for b in blocks for at in range(0, b.shape[0], step)]
    x = jnp.concatenate([b[at : at + CAP] for b, at in spots], axis=0)
    g = jnp.concatenate([b[at + CAP : at + step] for b, at in spots], axis=0)
    width = x.shape[1]
    hidden = packs[0].shape[1]
    nt = (((1,), (1,)), ((), ()))
    part = jnp.zeros((x.shape[0], 1), F32)
    for half, pack in enumerate(packs):
        a = jnp.dot(x, pack[:width], preferred_element_type=F32)
        u = jnp.dot(x, pack[width : 2 * width], preferred_element_type=F32)
        dh = jnp.zeros_like(a)
        for k in range(0, width, hidden):
            down = pack[2 * width + k : 2 * width + k + hidden]
            dh = dh + lax.dot_general(g[:, k : k + hidden], down, nt, preferred_element_type=F32)
        sig = jax.nn.sigmoid(a)
        act = a * sig
        part = part + jnp.sum(act * u * dh, axis=1, keepdims=True)
        at = 2 * half * hidden
        left_ref[:, at : at + hidden] = (dh * u * sig * (1.0 + a * (1.0 - sig))).astype(BF)
        left_ref[:, at + hidden : at + 2 * hidden] = (dh * act).astype(BF)
    high, low = split(part)
    high, low = high.astype(F32), low.astype(F32)
    lane = lax.broadcasted_iota(jnp.int32, (CAP, LANES), 1)
    tail = jnp.zeros((CAP, LANES), F32)
    for i in range(len(spots)):
        rows = slice(i * CAP, (i + 1) * CAP)
        tail = jnp.where(lane == 2 * i, high[rows], jnp.where(lane == 2 * i + 1, low[rows], tail))
    part_ref[...] = jnp.concatenate([tail, jnp.zeros((PAD - CAP, LANES), F32)], axis=0).astype(BF)


def inputs_kernel(left_ref, own_ref, near_ref, *outs):
    hidden = own_ref.shape[1]
    width = own_ref.shape[0] // 3
    nt = (((1,), (1,)), ((), ()))
    main = width * CAP // PAD
    step = width - main
    extra = PAD - CAP
    pieces = []
    for c in range(0, width, step):
        total = jnp.zeros((left_ref.shape[0], step), F32)
        for i in range(4):
            pack = (own_ref, near_ref)[i // 2]
            right = pack[i % 2 * width + c : i % 2 * width + c + step]
            left = left_ref[:, i * hidden : (i + 1) * hidden]
            total = total + lax.dot_general(left, right, nt, preferred_element_type=F32)
        pieces.append(total)
    last = pieces[-1]
    each = outs[0].shape[0] // PAD
    for i in range(left_ref.shape[0] // CAP):
        base = i * CAP
        out_ref, at = outs[i // each], i % each * PAD
        for j, piece in enumerate(pieces[:-1]):
            under = last[base + extra * j : base + extra * (j + 1)]
            both = jnp.concatenate([piece[base : base + CAP], under], axis=0)
            out_ref[at : at + PAD, j * step : (j + 1) * step] = both.astype(out_ref.dtype)


def attach_kernel(part_ref, *refs):
    outs = refs[len(refs) // 2 :]
    part = part_ref[...].astype(F32)
    lane = lax.broadcasted_iota(jnp.int32, part.shape, 1)
    each = outs[0].shape[0] // PAD
    for i in range(len(outs) * each):
        out_ref, at = outs[i // each], i % each * PAD
        tail = jnp.where(lane // 2 == i, part, 0.0)
        out_ref[at : at + PAD, out_ref.shape[1] - LANES :] = tail.astype(out_ref.dtype)


def add_kernel(keep_ref, got_ref, out_ref):
    main = keep_ref.shape[1] - LANES
    lane = lax.broadcasted_iota(jnp.int32, (PAD, LANES), 1)
    for i in range(2):
        rows = pl.ds(i * PAD, PAD)
        total = keep_ref[rows] + got_ref[rows].astype(F32)
        out_ref[rows, :main] = total[:, :main].astype(BF)
        high, low = split(jnp.sum(total[:, main:], axis=1, keepdims=True))
        tail = jnp.where(lane == 0, high.astype(F32), jnp.where(lane == 1, low.astype(F32), 0.0))
        out_ref[rows, main:] = tail.astype(BF)


def stack_kernel(*refs):
    for k, ref in enumerate(refs[:-1]):
        refs[-1][k * 2 * CAP : (k + 1) * 2 * CAP] = ref[...]


def unstack_kernel(ref, *outs):
    for k, out in enumerate(outs):
        out[...] = ref[k * 2 * CAP : (k + 1) * 2 * CAP]


def other_kernel(*refs):
    half = len(refs) - 1
    for k, ref in zip(reversed(range(half)), refs):
        refs[-1][k * PAD : (k + 1) * PAD] = ref[PAD:]


def mix_kernel(flight, ids_ref, place_ref, mix_ref, near_ref, *refs):
    half = flight // 2
    home, (out_ref, gates_ref) = refs[:half], refs[half:]
    home = home[::-1]
    blocks = []
    for k in range(half):
        blocks += [home[k].at[pl.ds(0, PAD)], near_ref.at[pl.ds(k * PAD, PAD)]]
    count, width = out_ref.shape
    main = width * CAP // PAD
    step = width - main
    tn = (((0,), (0,)), ((), ()))
    left = jnp.concatenate(
        [
            mix_ref[:, (2 * s + i) * count : (2 * s + i + 1) * count]
            for i in range(2)
            for s in range(flight)
        ],
        axis=0,
    )

    def blend(rows):
        right = jnp.concatenate([rows, rows], axis=0)
        return lax.dot_general(left, right, tn, preferred_element_type=F32).astype(BF)

    out_ref[:, :main] = blend(jnp.concatenate([b[:, :main] for b in blocks], axis=0))
    zero = jnp.zeros((PAD - CAP, step), BF)
    folded = []
    for s in range(flight):
        for j in range(main // step):
            folded.append(blocks[s][CAP:, j * step : (j + 1) * step])
        folded.append(zero)
    out_ref[:, main:] = blend(jnp.concatenate(folded, axis=0))
    own = lax.axis_index("expert") // SLICES
    parity = lax.axis_index("expert") % 2
    ids = ids_ref[...]
    total = jnp.zeros(ids.shape, F32)
    for s in range(flight):
        q = jnp.sum(blocks[s][:, main:].astype(F32), axis=1, keepdims=True)
        back = jnp.sum(place_ref[s * PAD : (s + 1) * PAD] * q, axis=0, keepdims=True)
        total = total + jnp.where(ids == (own ^ s ^ parity), back, 0.0)
    gates_ref[...] = total


def moved(value, sections, devices, stage, flip, bits, along=0):
    route = []
    for p in range(sections):
        for e in range(devices):
            there = e ^ bits ^ (along + SLICES * (e % 2) if along is not None else 0)
            route.append((p * devices + e, (p + flip) % sections * devices + there))
    return lax.ppermute(value, stage, route)


def per_device(inputs, out_grads, expert_ids, gate_values, w_gate, w_up, w_down):
    devices = lax.axis_size("expert")
    sections = lax.axis_size("pipe")
    flight = devices // SLICES
    half = flight // 2
    count, width = inputs.shape[1:]
    go = functools.partial(moved, sections=sections, devices=devices, stage=("pipe", "expert"))
    ids = expert_ids[0].T
    gates = gate_values[0].T
    hidden = w_gate.shape[2]
    shape = jax.ShapeDtypeStruct
    main = width * CAP // PAD
    hbm = [pl.BlockSpec(memory_space=pltpu.HBM)]
    args = (ids, gates, inputs[0], out_grads[0], w_gate[0], w_up[0], w_down[0])
    *blocks, mix, place, pack = pl.pallas_call(
        functools.partial(select_kernel, flight),
        out_shape=[shape((2 * CAP, width), BF)] * flight
        + [
            shape((PAD, 2 * flight * count), BF),
            shape((flight * PAD, count), F32),
            shape((3 * width, hidden), BF),
        ],
        in_specs=hbm * 7,
        scratch_shapes=[
            pltpu.VMEM(ids.shape, jnp.int32),
            pltpu.VMEM(gates.shape, F32),
            pltpu.VMEM((count, width), BF),
            pltpu.VMEM((count, width), BF),
            pltpu.SemaphoreType.DMA((4,)),
            pltpu.SemaphoreType.DMA((2 + width // hidden,)),
        ],
        compiler_params=PARAMS,
        name="select",
    )(*[pltpu.with_memory_space_constraint(v, pltpu.HBM) for v in args])
    mine, theirs = blocks[:half], blocks[half:]
    both = pl.pallas_call(
        stack_kernel,
        out_shape=shape((half * 2 * CAP, width), BF),
        compiler_params=PARAMS,
        name="stack",
    )(*theirs)
    both = go(both, flip=0, bits=1, along=None)
    got = pl.pallas_call(
        unstack_kernel,
        out_shape=[shape((2 * CAP, width), BF)] * half,
        compiler_params=PARAMS,
        name="unstack",
    )(both)
    joined = pl.pallas_call(
        join_kernel,
        out_shape=shape((4 * CAP, width), BF),
        compiler_params=PARAMS,
        name="join",
    )(mine[0], got[0])
    sends = [(0, joined)]
    for k in range(1, half):
        sends += [(k, mine[k]), (k, got[k])]
    rows = [go(v, flip=0, bits=0, along=2 * k * SLICES) for k, v in sends]
    far_mix = go(mix, flip=-1, bits=0, along=None)
    rows[-1], far_mix = lax.optimization_barrier((rows[-1], far_mix))
    pack, *_ = lax.optimization_barrier((pack, *got))
    near = go(pack, flip=0, bits=1, along=None)
    rows = rows + [go(r, flip=0, bits=2, along=None) for r in rows]
    left, part = pl.pallas_call(
        functools.partial(hidden_kernel, len(rows)),
        out_shape=[shape((2 * flight * CAP, 4 * hidden), BF), shape((PAD, LANES), BF)],
        compiler_params=PARAMS,
        name="hidden",
    )(*rows, pack, near)
    part = go(part, flip=1, bits=0, along=None)
    r_shapes = [shape((2 * PAD, main + LANES), t) for t in [F32] * half + [BF] * half]
    r_sums = pl.pallas_call(
        inputs_kernel,
        out_shape=r_shapes,
        compiler_params=PARAMS,
        name="inputs_back",
    )(left, pack, near)
    r_sums = pl.pallas_call(
        attach_kernel,
        out_shape=r_shapes,
        input_output_aliases={i + 1: i for i in range(2 * half)},
        compiler_params=PARAMS,
        name="attach_gate_parts",
    )(part, *r_sums)
    r_home = []
    for k in reversed(range(half)):
        r_got = go(r_sums[half + k], flip=0, bits=2, along=None)
        r_part = pl.pallas_call(
            add_kernel,
            out_shape=shape((2 * PAD, main + LANES), BF),
            compiler_params=PARAMS,
            name="add_inputs_back",
        )(r_sums[k], r_got)
        r_home.append(go(r_part, flip=-1, bits=0, along=2 * k * SLICES))
    others = pl.pallas_call(
        other_kernel,
        out_shape=shape((half * PAD, main + LANES), BF),
        compiler_params=PARAMS,
        name="other_core",
    )(*r_home)
    r_near = go(others, flip=0, bits=1, along=None)
    moe, d_gates = pl.pallas_call(
        functools.partial(mix_kernel, flight),
        out_shape=[shape((count, width), BF), shape(ids.shape, F32)],
        compiler_params=PARAMS,
        name="mix",
    )(ids, place, far_mix, r_near, *r_home)
    return (moe[None], d_gates.T[None])


def solution(mesh):
    return jax.shard_map(
        per_device,
        mesh=mesh,
        in_specs=(
            P("pipe", "expert", None),
            P("pipe", "expert", None),
            P("pipe", "expert", None),
            P("pipe", "expert", None),
            P("pipe", None, "expert"),
            P("pipe", None, "expert"),
            P("pipe", "expert", None),
        ),
        out_specs=(P("pipe", "expert", None), P("pipe", "expert", None)),
        check_vma=False,
    )
```

time: 47.9 us -> 44.5 us (0.929)
  waiting for transfers between devices: 20.9 us -> 18.4 us
  starting transfers between devices: 19.8 us -> 18.2 us
  Pallas kernels: 6.44 us -> 6.94 us
    ppermute x14 -> x15, waiting for transfers between devices: 20.9 us -> 18.4 us  [moved(): return lax.ppermute(value, stage, route)]
    ppermute x14 -> x15, starting transfers between devices: 19.8 us -> 18.2 us  [moved(): return lax.ppermute(value, stage, route)]
    pallas_call x4 -> x9, Pallas kernels: 3.03 us -> 3.16 us  [the longest x1 1.54 us: per_device(): pl.pallas_call(functools.partial(hidden_kernel, len(rows)), out_shape=[sh...]
  transfers between devices with their start and end apart: 14 -> 15, of which waited for: 7 -> 9; matrix products, arithmetic and copies ran while one was open for 0% -> 0% of each run, Pallas kernels for 3% -> 4%
where the time goes in v3:
time: 44.5 us; the launch traced here: 44.3 us
  waiting for transfers between devices  18.4 us (41%)
  starting transfers between devices  18.2 us (41%)
  Pallas kernels  6.94 us (16%)
  between operations  0.71 us (2%)
    ppermute x15, waiting for transfers between devices, moved(): return lax.ppermute(value, stage, route)  18.4 us
    ppermute x15, starting transfers between devices, moved(): return lax.ppermute(value, stage, route)  18.2 us
    pallas_call x1, Pallas kernels, per_device(): pl.pallas_call(functools.partial(select_kernel, flight), out_shape=[shape...  2.65 us
    pallas_call x1, Pallas kernels, per_device(): pl.pallas_call(functools.partial(hidden_kernel, len(rows)), out_shape=[sh...  1.54 us
    pallas_call x1, Pallas kernels, per_device(): pl.pallas_call(inputs_kernel, out_shape=r_shapes, compiler_params=PARAMS,...  1.39 us
    pallas_call x1, Pallas kernels, per_device(): pl.pallas_call(functools.partial(mix_kernel, flight), out_shape=[shape((c...  1.12 us
  transfers between devices with their start and end apart: 15, of which 9 were waited for; matrix products, arithmetic and copies ran while one was open for 0% of the time, Pallas kernels for 4%

profile of v3, /device:TPU:0, one launch (start us, length us, event | category | flops | bytes accessed | tf_op | source)
XLA Modules:
  0.0 44.3 jit_solution(10255715170793295963)
XLA Ops:
  0.6 2.7 %select.1 = (bf16[24,2048]{1,0:T(8,128)(2,1)S(1)}, bf16[24,2048]{1,0:T(8,128)(2,1)S(1)}, bf16[24,2048]{1,0:T(8,128)(2,1)S(1)}, bf16[24,2048]{1,0:T(8,128)(2,1)S(...) custom-call(s32[8,128]{1,0:T(8,128)} %bitcast.15, f32[8,128]{1,0:T(8,128)} %bitcast.22, ...), custom_call_target="tpu_custom_call" | custom-call | tf_op jit(solution)/shard_map/select/pallas_call | solution.py:267
  3.3 0.5 %collective-permute-start = (bf16[48,2048]{1,0:T(8,128)(2,1)S(1)}, bf16[48,2048]{1,0:T(8,128)(2,1)S(1)}, u32[]{:S(2)}, u32[]{:S(2)}) collective-permute-start(bf16[48,2048]{1,0:T(8,128)(2,1)S(1)} %stack.1), channel_id=1, source_target_pairs={{0,1},{1,0},{2,3},{3,2},{4,5},{5,4},{6,7},{7,6},{8,9},{9,8},{10,11... | collective-permute-start | bytes 589832 | tf_op jit(solution)/shard_map/ppermute | solution.py:250
  3.8 1.1 %collective-permute-done.ref = bf16[48,2048]{1,0:T(8,128)(2,1)S(1)} collective-permute-done((bf16[48,2048]{1,0:T(8,128)(2,1)S(1)}, bf16[48,2048]{1,0:T(8,128)(2,1)S(1)}, u32[]{:S(2)}, u32[]{:S(2)}) %collective-permute-start) | collective-permute-done | bytes 196640 | tf_op jit(solution)/shard_map/ppermute | solution.py:250
  5.4 0.7 %collective-permute-start.3 = (bf16[48,2048]{1,0:T(8,128)(2,1)S(1)}, bf16[48,2048]{1,0:T(8,128)(2,1)S(1)}, u32[]{:S(2)}, u32[]{:S(2)}) collective-permute-start(bf16[48,2048]{1,0:T(8,128)(2,1)S(1)} %join.1), channel_id=1, source_target_pairs={{0,0},{1,5},{2,2},{3,7},{4,4},{5,1},{6,6},{7,3},{8,8},{9,13},{10,1... | collective-permute-start | bytes 589832 | tf_op jit(solution)/shard_map/ppermute | solution.py:250
  6.1 3.8 %collective-permute-start.4 = (bf16[24,2048]{1,0:T(8,128)(2,1)S(1)}, bf16[24,2048]{1,0:T(8,128)(2,1)S(1)}, u32[]{:S(2)}, u32[]{:S(2)}) collective-permute-start(bf16[24,2048]{1,0:T(8,128)(2,1)S(1)} %get-tuple-element.34), channel_id=1, source_target_pairs={{0,8},{1,13},{2,10},{3,15},{4,12},{5,9},{6,14},{7,11},{8,0},{9,5},... | collective-permute-start | bytes 294920 | tf_op jit(solution)/shard_map/ppermute | solution.py:250
  9.9 1.8 %collective-permute-start.5 = (bf16[48,2048]{1,0:T(8,128)(2,1)S(1)}, bf16[48,2048]{1,0:T(8,128)(2,1)S(1)}, u32[]{:S(2)}, u32[]{:S(2)}) collective-permute-start(bf16[48,2048]{1,0:T(8,128)(2,1)S(1)} %collective-permute-done.3.refs_0_), channel_id=1, source_target_pairs={{0,2},{1,3},{2,0},{3,1},{4,6},{5,7},{6,4},{7,5},{8,10},{9,11},{10,... | collective-permute-start | bytes 589832 | tf_op jit(solution)/shard_map/ppermute | solution.py:250
  11.7 1.5 %collective-permute-start.2 = (bf16[16,1024]{1,0:T(8,128)(2,1)S(1)}, bf16[16,1024]{1,0:T(8,128)(2,1)S(1)}, u32[]{:S(2)}, u32[]{:S(2)}) collective-permute-start(bf16[16,1024]{1,0:T(8,128)(2,1)S(1)} %get-tuple-element.30), channel_id=1, source_target_pairs={{0,16},{1,17},{2,18},{3,19},{4,20},{5,21},{6,22},{7,23},{8,24},{9,... | collective-permute-start | bytes 98312 | tf_op jit(solution)/shard_map/ppermute | solution.py:250
  13.2 1.3 %collective-permute-start.6 = (bf16[24,2048]{1,0:T(8,128)(2,1)S(1)}, bf16[24,2048]{1,0:T(8,128)(2,1)S(1)}, u32[]{:S(2)}, u32[]{:S(2)}) collective-permute-start(bf16[24,2048]{1,0:T(8,128)(2,1)S(1)} %collective-permute-done.4.refs_1_), channel_id=1, source_target_pairs={{0,2},{1,3},{2,0},{3,1},{4,6},{5,7},{6,4},{7,5},{8,10},{9,11},{10,... | collective-permute-start | bytes 294920 | tf_op jit(solution)/shard_map/ppermute | solution.py:250
  14.5 1.1 %collective-permute-done.2.mix_ref = bf16[16,1024]{1,0:T(8,128)(2,1)S(1)} collective-permute-done((bf16[16,1024]{1,0:T(8,128)(2,1)S(1)}, bf16[16,1024]{1,0:T(8,128)(2,1)S(1)}, u32[]{:S(2)}, u32[]{:S(2)}) %collective-permute-start.2) | collective-permute-done | bytes 32800 | tf_op jit(solution)/shard_map/ppermute | solution.py:250
  15.6 3.9 %collective-permute-done.1.refs_2_ = bf16[24,2048]{1,0:T(8,128)(2,1)S(1)} collective-permute-done((bf16[24,2048]{1,0:T(8,128)(2,1)S(1)}, bf16[24,2048]{1,0:T(8,128)(2,1)S(1)}, u32[]{:S(2)}, u32[]{:S(2)}) %collective-permute-start.1) | collective-permute-done | bytes 98336 | tf_op jit(solution)/shard_map/ppermute | solution.py:250
  19.5 1.5 %collective-permute-start.7 = (bf16[24,2048]{1,0:T(8,128)(2,1)S(1)}, bf16[24,2048]{1,0:T(8,128)(2,1)S(1)}, u32[]{:S(2)}, u32[]{:S(2)}) collective-permute-start(bf16[24,2048]{1,0:T(8,128)(2,1)S(1)} %collective-permute-done.1.refs_2_), channel_id=1, source_target_pairs={{0,2},{1,3},{2,0},{3,1},{4,6},{5,7},{6,4},{7,5},{8,10},{9,11},{10,... | collective-permute-start | bytes 294920 | tf_op jit(solution)/shard_map/ppermute | solution.py:250
  21.0 3.1 %collective-permute-done.7.refs_5_ = bf16[24,2048]{1,0:T(8,128)(2,1)S(1)} collective-permute-done((bf16[24,2048]{1,0:T(8,128)(2,1)S(1)}, bf16[24,2048]{1,0:T(8,128)(2,1)S(1)}, u32[]{:S(2)}, u32[]{:S(2)}) %collective-permute-start.7) | collective-permute-done | bytes 98336 | tf_op jit(solution)/shard_map/ppermute | solution.py:250
  24.1 1.5 %hidden.1 = (bf16[96,1024]{1,0:T(8,128)(2,1)S(1)}, bf16[16,128]{1,0:T(8,128)(2,1)S(1)}) custom-call(bf16[48,2048]{1,0:T(8,128)(2,1)S(1)} %collective-permute-done.3.refs_0_, bf16[24,2048]{1,0:T(8,128)(2,1)S(1)} %collective-permute-done.4.refs_1_, bf16[24,2048]{1,0:T(8,128)(2,1)S(1)} %collective-permute-done.1.refs_2_, ...), custom_call_target="tpu_custom_call" | custom-call | tf_op jit(solution)/shard_map/hidden/pallas_call | solution.py:316
  25.7 1.6 %collective-permute-start.9 = (bf16[16,128]{1,0:T(8,128)(2,1)S(1)}, bf16[16,128]{1,0:T(8,128)(2,1)S(1)}, u32[]{:S(2)}, u32[]{:S(2)}) collective-permute-start(bf16[16,128]{1,0:T(8,128)(2,1)S(1)} %get-tuple-element.38), channel_id=1, source_target_pairs={{0,16},{1,17},{2,18},{3,19},{4,20},{5,21},{6,22},{7,23},{8,24},{9,... | collective-permute-start | bytes 12296 | tf_op jit(solution)/shard_map/ppermute | solution.py:250
  27.3 1.4 %inputs_back.1 = (f32[32,1664]{1,0:T(8,128)S(1)}, f32[32,1664]{1,0:T(8,128)S(1)}, bf16[32,1664]{1,0:T(8,128)(2,1)S(1)}, bf16[32,1664]{1,0:T(8,128)(2,1)S(1)}) custom-call(bf16[96,1024]{1,0:T(8,128)(2,1)S(1)} %get-tuple-element.39.left_ref, bf16[6144,256]{1,0:T(8,128)(2,1)S(1)} %get-tuple-element.37.refs_6_.own_ref, ...), custom_call_target="tpu_custom_call" | custom-call | tf_op jit(solution)/shard_map/inputs_back/pallas_call | solution.py:324
  28.6 0.7 %collective-permute-done.9.part_ref = bf16[16,128]{1,0:T(8,128)(2,1)S(1)} collective-permute-done((bf16[16,128]{1,0:T(8,128)(2,1)S(1)}, bf16[16,128]{1,0:T(8,128)(2,1)S(1)}, u32[]{:S(2)}, u32[]{:S(2)}) %collective-permute-start.9) | collective-permute-done | bytes 4128 | tf_op jit(solution)/shard_map/ppermute | solution.py:250
  29.4 1.6 %collective-permute-start.10 = (bf16[32,1664]{1,0:T(8,128)(2,1)S(1)}, bf16[32,1664]{1,0:T(8,128)(2,1)S(1)}, u32[]{:S(2)}, u32[]{:S(2)}) collective-permute-start(bf16[32,1664]{1,0:T(8,128)(2,1)S(1)} %get-tuple-element.45), channel_id=1, source_target_pairs={{0,2},{1,3},{2,0},{3,1},{4,6},{5,7},{6,4},{7,5},{8,10},{9,11},{10,... | collective-permute-start | bytes 319496 | tf_op jit(solution)/shard_map/ppermute | solution.py:250
  31.5 2.7 %collective-permute-done.10.got_ref = bf16[32,1664]{1,0:T(8,128)(2,1)S(1)} collective-permute-done((bf16[32,1664]{1,0:T(8,128)(2,1)S(1)}, bf16[32,1664]{1,0:T(8,128)(2,1)S(1)}, u32[]{:S(2)}, u32[]{:S(2)}) %collective-permute-start.10) | collective-permute-done | bytes 106528 | tf_op jit(solution)/shard_map/ppermute | solution.py:250
  34.2 1.6 %collective-permute-start.11 = (bf16[32,1664]{1,0:T(8,128)(2,1)S(1)}, bf16[32,1664]{1,0:T(8,128)(2,1)S(1)}, u32[]{:S(2)}, u32[]{:S(2)}) collective-permute-start(bf16[32,1664]{1,0:T(8,128)(2,1)S(1)} %add_inputs_back.2), channel_id=1, source_target_pairs={{0,24},{1,29},{2,26},{3,31},{4,28},{5,25},{6,30},{7,27},{8,16},{9,... | collective-permute-start | bytes 319496 | tf_op jit(solution)/shard_map/ppermute | solution.py:250
  35.9 1.4 %collective-permute-start.13 = (bf16[32,1664]{1,0:T(8,128)(2,1)S(1)}, bf16[32,1664]{1,0:T(8,128)(2,1)S(1)}, u32[]{:S(2)}, u32[]{:S(2)}) collective-permute-start(bf16[32,1664]{1,0:T(8,128)(2,1)S(1)} %add_inputs_back.3), channel_id=1, source_target_pairs={{0,16},{1,21},{2,18},{3,23},{4,20},{5,17},{6,22},{7,19},{8,24},{9,... | collective-permute-start | bytes 319496 | tf_op jit(solution)/shard_map/ppermute | solution.py:250
  37.3 3.6 %collective-permute-done.11.refs_0_ = bf16[32,1664]{1,0:T(8,128)(2,1)S(1)} collective-permute-done((bf16[32,1664]{1,0:T(8,128)(2,1)S(1)}, bf16[32,1664]{1,0:T(8,128)(2,1)S(1)}, u32[]{:S(2)}, u32[]{:S(2)}) %collective-permute-start.11) | collective-permute-done | bytes 106528 | tf_op jit(solution)/shard_map/ppermute | solution.py:250
  40.9 0.9 %collective-permute-done.13.refs_1_ = bf16[32,1664]{1,0:T(8,128)(2,1)S(1)} collective-permute-done((bf16[32,1664]{1,0:T(8,128)(2,1)S(1)}, bf16[32,1664]{1,0:T(8,128)(2,1)S(1)}, u32[]{:S(2)}, u32[]{:S(2)}) %collective-permute-start.13) | collective-permute-done | bytes 106528 | tf_op jit(solution)/shard_map/ppermute | solution.py:250
  41.9 1.3 %collective-permute-done.14.near_ref = bf16[32,1664]{1,0:T(8,128)(2,1)S(1)} collective-permute-done((bf16[32,1664]{1,0:T(8,128)(2,1)S(1)}, bf16[32,1664]{1,0:T(8,128)(2,1)S(1)}, u32[]{:S(2)}, u32[]{:S(2)}) %collective-permute-start.14) | collective-permute-done | bytes 106528 | tf_op jit(solution)/shard_map/ppermute | solution.py:250
  43.2 1.1 %mix.1 = (bf16[128,2048]{1,0:T(8,128)(2,1)}, f32[8,128]{1,0:T(8,128)}) custom-call(s32[8,128]{1,0:T(8,128)S(1)} %bitcast.16, f32[64,128]{1,0:T(8,128)S(1)} %get-tuple-element.26.place_ref, bf16[16,1024]{1,0:T(8,128)(2,1)S(1)} %collective-permute-done.2.mix_ref, bf16[32,1664]{1,0:T(8,128)(2,1)S(1)} %collective-permute-done.14.near_ref, ...), custom_call_target="tpu_custom_call" | custom-call | tf_op jit(solution)/shard_map/mix/pallas_call | solution.py:354
  (19 shorter events, 1.3 us)
Async XLA Ops:
  3.3 1.6 %collective-permute-start = (bf16[48,2048]{1,0:T(8,128)(2,1)S(1)}, bf16[48,2048]{1,0:T(8,128)(2,1)S(1)}, u32[]{:S(2)}, u32[]{:S(2)}) collective-permute-start(bf16[48,2048]{1,0:T(8,128)(2,1)S(1)} %stack.1), channel_id=1, source_target_pairs={{0,1},{1,0},{2,3},{3,2},{4,5},{5,4},{6,7},{7,6},{8,9},{9,8},{10,11... | collective-permute-start | bytes 589832 | tf_op jit(solution)/shard_map/ppermute | solution.py:250
  4.9 19.2 %collective-permute-start.8 = (bf16[6144,256]{1,0:T(8,128)(2,1)S(1)}, bf16[6144,256]{1,0:T(8,128)(2,1)S(1)}, u32[]{:S(2)}, u32[]{:S(2)}) collective-permute-start(bf16[6144,256]{1,0:T(8,128)(2,1)S(1)} %get-tuple-element.37.refs_6_.own_ref), channel_id=1, source_target_pairs={{0,1},{1,0},{2,3},{3,2},{4,5},{5,4},{6,7},{7,6},{8,9},{9,8},{10,11... | collective-permute-start | bytes 9437192 | tf_op jit(solution)/shard_map/ppermute | solution.py:250
  5.4 4.5 %collective-permute-start.3 = (bf16[48,2048]{1,0:T(8,128)(2,1)S(1)}, bf16[48,2048]{1,0:T(8,128)(2,1)S(1)}, u32[]{:S(2)}, u32[]{:S(2)}) collective-permute-start(bf16[48,2048]{1,0:T(8,128)(2,1)S(1)} %join.1), channel_id=1, source_target_pairs={{0,0},{1,5},{2,2},{3,7},{4,4},{5,1},{6,6},{7,3},{8,8},{9,13},{10,1... | collective-permute-start | bytes 589832 | tf_op jit(solution)/shard_map/ppermute | solution.py:250
  6.1 7.1 %collective-permute-start.4 = (bf16[24,2048]{1,0:T(8,128)(2,1)S(1)}, bf16[24,2048]{1,0:T(8,128)(2,1)S(1)}, u32[]{:S(2)}, u32[]{:S(2)}) collective-permute-start(bf16[24,2048]{1,0:T(8,128)(2,1)S(1)} %get-tuple-element.34), channel_id=1, source_target_pairs={{0,8},{1,13},{2,10},{3,15},{4,12},{5,9},{6,14},{7,11},{8,0},{9,5},... | collective-permute-start | bytes 294920 | tf_op jit(solution)/shard_map/ppermute | solution.py:250
  9.8 9.7 %collective-permute-start.1 = (bf16[24,2048]{1,0:T(8,128)(2,1)S(1)}, bf16[24,2048]{1,0:T(8,128)(2,1)S(1)}, u32[]{:S(2)}, u32[]{:S(2)}) collective-permute-start(bf16[24,2048]{1,0:T(8,128)(2,1)S(1)} %get-tuple-element.29), channel_id=1, source_target_pairs={{0,8},{1,13},{2,10},{3,15},{4,12},{5,9},{6,14},{7,11},{8,0},{9,5},... | collective-permute-start | bytes 294920 | tf_op jit(solution)/shard_map/ppermute | solution.py:250
  9.9 14.2 %collective-permute-start.5 = (bf16[48,2048]{1,0:T(8,128)(2,1)S(1)}, bf16[48,2048]{1,0:T(8,128)(2,1)S(1)}, u32[]{:S(2)}, u32[]{:S(2)}) collective-permute-start(bf16[48,2048]{1,0:T(8,128)(2,1)S(1)} %collective-permute-done.3.refs_0_), channel_id=1, source_target_pairs={{0,2},{1,3},{2,0},{3,1},{4,6},{5,7},{6,4},{7,5},{8,10},{9,11},{10,... | collective-permute-start | bytes 589832 | tf_op jit(solution)/shard_map/ppermute | solution.py:250
  11.7 3.9 %collective-permute-start.2 = (bf16[16,1024]{1,0:T(8,128)(2,1)S(1)}, bf16[16,1024]{1,0:T(8,128)(2,1)S(1)}, u32[]{:S(2)}, u32[]{:S(2)}) collective-permute-start(bf16[16,1024]{1,0:T(8,128)(2,1)S(1)} %get-tuple-element.30), channel_id=1, source_target_pairs={{0,16},{1,17},{2,18},{3,19},{4,20},{5,21},{6,22},{7,23},{8,24},{9,... | collective-permute-start | bytes 98312 | tf_op jit(solution)/shard_map/ppermute | solution.py:250
  13.2 7.8 %collective-permute-start.6 = (bf16[24,2048]{1,0:T(8,128)(2,1)S(1)}, bf16[24,2048]{1,0:T(8,128)(2,1)S(1)}, u32[]{:S(2)}, u32[]{:S(2)}) collective-permute-start(bf16[24,2048]{1,0:T(8,128)(2,1)S(1)} %collective-permute-done.4.refs_1_), channel_id=1, source_target_pairs={{0,2},{1,3},{2,0},{3,1},{4,6},{5,7},{6,4},{7,5},{8,10},{9,11},{10,... | collective-permute-start | bytes 294920 | tf_op jit(solution)/shard_map/ppermute | solution.py:250
  19.5 4.6 %collective-permute-start.7 = (bf16[24,2048]{1,0:T(8,128)(2,1)S(1)}, bf16[24,2048]{1,0:T(8,128)(2,1)S(1)}, u32[]{:S(2)}, u32[]{:S(2)}) collective-permute-start(bf16[24,2048]{1,0:T(8,128)(2,1)S(1)} %collective-permute-done.1.refs_2_), channel_id=1, source_target_pairs={{0,2},{1,3},{2,0},{3,1},{4,6},{5,7},{6,4},{7,5},{8,10},{9,11},{10,... | collective-permute-start | bytes 294920 | tf_op jit(solution)/shard_map/ppermute | solution.py:250
  25.7 3.7 %collective-permute-start.9 = (bf16[16,128]{1,0:T(8,128)(2,1)S(1)}, bf16[16,128]{1,0:T(8,128)(2,1)S(1)}, u32[]{:S(2)}, u32[]{:S(2)}) collective-permute-start(bf16[16,128]{1,0:T(8,128)(2,1)S(1)} %get-tuple-element.38), channel_id=1, source_target_pairs={{0,16},{1,17},{2,18},{3,19},{4,20},{5,21},{6,22},{7,23},{8,24},{9,... | collective-permute-start | bytes 12296 | tf_op jit(solution)/shard_map/ppermute | solution.py:250
  27.2 15.9 %copy-start = (s32[1,128,8]{1,2,0:T(8,128)S(1)}, s32[1,128,8]{1,2,0:T(8,128)}, u32[]{:S(2)}) copy-start(s32[1,128,8]{1,2,0:T(8,128)} %param.9) | copy-start | bytes 12292
  29.4 4.8 %collective-permute-start.10 = (bf16[32,1664]{1,0:T(8,128)(2,1)S(1)}, bf16[32,1664]{1,0:T(8,128)(2,1)S(1)}, u32[]{:S(2)}, u32[]{:S(2)}) collective-permute-start(bf16[32,1664]{1,0:T(8,128)(2,1)S(1)} %get-tuple-element.45), channel_id=1, source_target_pairs={{0,2},{1,3},{2,0},{3,1},{4,6},{5,7},{6,4},{7,5},{8,10},{9,11},{10,... | collective-permute-start | bytes 319496 | tf_op jit(solution)/shard_map/ppermute | solution.py:250
  31.0 4.9 %collective-permute-start.12 = (bf16[32,1664]{1,0:T(8,128)(2,1)S(1)}, bf16[32,1664]{1,0:T(8,128)(2,1)S(1)}, u32[]{:S(2)}, u32[]{:S(2)}) collective-permute-start(bf16[32,1664]{1,0:T(8,128)(2,1)S(1)} %get-tuple-element.47), channel_id=1, source_target_pairs={{0,2},{1,3},{2,0},{3,1},{4,6},{5,7},{6,4},{7,5},{8,10},{9,11},{10,... | collective-permute-start | bytes 319496 | tf_op jit(solution)/shard_map/ppermute | solution.py:250
  34.2 6.6 %collective-permute-start.11 = (bf16[32,1664]{1,0:T(8,128)(2,1)S(1)}, bf16[32,1664]{1,0:T(8,128)(2,1)S(1)}, u32[]{:S(2)}, u32[]{:S(2)}) collective-permute-start(bf16[32,1664]{1,0:T(8,128)(2,1)S(1)} %add_inputs_back.2), channel_id=1, source_target_pairs={{0,24},{1,29},{2,26},{3,31},{4,28},{5,25},{6,30},{7,27},{8,16},{9,... | collective-permute-start | bytes 319496 | tf_op jit(solution)/shard_map/ppermute | solution.py:250
  35.9 5.9 %collective-permute-start.13 = (bf16[32,1664]{1,0:T(8,128)(2,1)S(1)}, bf16[32,1664]{1,0:T(8,128)(2,1)S(1)}, u32[]{:S(2)}, u32[]{:S(2)}) collective-permute-start(bf16[32,1664]{1,0:T(8,128)(2,1)S(1)} %add_inputs_back.3), channel_id=1, source_target_pairs={{0,16},{1,21},{2,18},{3,23},{4,20},{5,17},{6,22},{7,19},{8,24},{9,... | collective-permute-start | bytes 319496 | tf_op jit(solution)/shard_map/ppermute | solution.py:250
  41.8 1.4 %collective-permute-start.14 = (bf16[32,1664]{1,0:T(8,128)(2,1)S(1)}, bf16[32,1664]{1,0:T(8,128)(2,1)S(1)}, u32[]{:S(2)}, u32[]{:S(2)}) collective-permute-start(bf16[32,1664]{1,0:T(8,128)(2,1)S(1)} %other_core.1), channel_id=1, source_target_pairs={{0,1},{1,0},{2,3},{3,2},{4,5},{5,4},{6,7},{7,6},{8,9},{9,8},{10,11... | collective-permute-start | bytes 319496 | tf_op jit(solution)/shard_map/ppermute | solution.py:250

commit v4 on v3

--- a/solution.py
+++ b/solution.py
@@ -11,6 +11,7 @@
 CAP = 12
 PAD = 16
 LANES = 128
+ORDER = ((1, 3, 2, 0), (1, 0, 3, 2))
 BF = jnp.bfloat16
 F32 = jnp.float32
 PARAMS = pltpu.CompilerParams(vmem_limit_bytes=40 * 1024 * 1024)
@@ -93,14 +94,11 @@
         copy.wait()
 
 
-def join_kernel(mine_ref, got_ref, out_ref):
-    out_ref[: 2 * CAP] = mine_ref[...]
-    out_ref[2 * CAP :] = got_ref[...]
-
-
-def hidden_kernel(many, *refs):
+def hidden_kernel(order, *refs):
+    many = len(order)
     blocks, packs = refs[:many], refs[many : many + 2]
     left_ref, part_ref = refs[many + 2 :]
+    blocks = [blocks[order.index(i)] for i in range(many)]
     step = 2 * CAP
     spots = [(b, at) for b in blocks for at in range(0, b.shape[0], step)]
     x = jnp.concatenate([b[at : at + CAP] for b, at in spots], axis=0)
@@ -182,16 +180,6 @@
         out_ref[rows, main:] = tail.astype(BF)
 
 
-def stack_kernel(*refs):
-    for k, ref in enumerate(refs[:-1]):
-        refs[-1][k * 2 * CAP : (k + 1) * 2 * CAP] = ref[...]
-
-
-def unstack_kernel(ref, *outs):
-    for k, out in enumerate(outs):
-        out[...] = ref[k * 2 * CAP : (k + 1) * 2 * CAP]
-
-
 def other_kernel(*refs):
     half = len(refs) - 1
     for k, ref in zip(reversed(range(half)), refs):
@@ -245,7 +233,7 @@
     route = []
     for p in range(sections):
         for e in range(devices):
-            there = e ^ bits ^ (along + SLICES * (e % 2) if along is not None else 0)
+            there = e ^ bits ^ (along + SLICES * ((e ^ bits) % 2) if along is not None else 0)
             route.append((p * devices + e, (p + flip) % sections * devices + there))
     return lax.ppermute(value, stage, route)
 
@@ -285,40 +273,20 @@
         name="select",
     )(*[pltpu.with_memory_space_constraint(v, pltpu.HBM) for v in args])
     mine, theirs = blocks[:half], blocks[half:]
-    both = pl.pallas_call(
-        stack_kernel,
-        out_shape=shape((half * 2 * CAP, width), BF),
-        compiler_params=PARAMS,
-        name="stack",
-    )(*theirs)
-    both = go(both, flip=0, bits=1, along=None)
-    got = pl.pallas_call(
-        unstack_kernel,
-        out_shape=[shape((2 * CAP, width), BF)] * half,
-        compiler_params=PARAMS,
-        name="unstack",
-    )(both)
-    joined = pl.pallas_call(
-        join_kernel,
-        out_shape=shape((4 * CAP, width), BF),
-        compiler_params=PARAMS,
-        name="join",
-    )(mine[0], got[0])
-    sends = [(0, joined)]
-    for k in range(1, half):
-        sends += [(k, mine[k]), (k, got[k])]
-    rows = [go(v, flip=0, bits=0, along=2 * k * SLICES) for k, v in sends]
-    far_mix = go(mix, flip=-1, bits=0, along=None)
-    rows[-1], far_mix = lax.optimization_barrier((rows[-1], far_mix))
-    pack, *_ = lax.optimization_barrier((pack, *got))
+    rows = []
+    for k in range(half):
+        rows.append(go(mine[k], flip=0, bits=0, along=2 * k * SLICES))
+        rows.append(go(theirs[k], flip=0, bits=1, along=2 * k * SLICES))
     near = go(pack, flip=0, bits=1, along=None)
+    rows[-1], near = lax.optimization_barrier((rows[-1], near))
     rows = rows + [go(r, flip=0, bits=2, along=None) for r in rows]
+    order = [*ORDER[0], *range(4, flight), *(flight + i for i in ORDER[1]), *range(flight + 4, 2 * flight)]
     left, part = pl.pallas_call(
-        functools.partial(hidden_kernel, len(rows)),
+        functools.partial(hidden_kernel, order),
         out_shape=[shape((2 * flight * CAP, 4 * hidden), BF), shape((PAD, LANES), BF)],
         compiler_params=PARAMS,
         name="hidden",
-    )(*rows, pack, near)
+    )(*[rows[i] for i in order], pack, near)
     part = go(part, flip=1, bits=0, along=None)
     r_shapes = [shape((2 * PAD, main + LANES), t) for t in [F32] * half + [BF] * half]
     r_sums = pl.pallas_call(
@@ -335,7 +303,7 @@
         name="attach_gate_parts",
     )(part, *r_sums)
     r_home = []
-    for k in reversed(range(half)):
+    for k in range(half):
         r_got = go(r_sums[half + k], flip=0, bits=2, along=None)
         r_part = pl.pallas_call(
             add_kernel,
@@ -344,19 +312,21 @@
             name="add_inputs_back",
         )(r_sums[k], r_got)
         r_home.append(go(r_part, flip=-1, bits=0, along=2 * k * SLICES))
+    far_mix = go(mix, flip=-1, bits=0, along=None)
+    r_home[-1], far_mix = lax.optimization_barrier((r_home[-1], far_mix))
     others = pl.pallas_call(
         other_kernel,
         out_shape=shape((half * PAD, main + LANES), BF),
         compiler_params=PARAMS,
         name="other_core",
-    )(*r_home)
+    )(*r_home[::-1])
     r_near = go(others, flip=0, bits=1, along=None)
     moe, d_gates = pl.pallas_call(
         functools.partial(mix_kernel, flight),
         out_shape=[shape((count, width), BF), shape(ids.shape, F32)],
         compiler_params=PARAMS,
         name="mix",
-    )(ids, place, far_mix, r_near, *r_home)
+    )(ids, place, far_mix, r_near, *r_home[::-1])
     return (moe[None], d_gates.T[None])
 
 

time: 44.5 us -> 43.4 us (0.975)
  waiting for transfers between devices: 18.4 us -> 14.1 us
  starting transfers between devices: 18.2 us -> 21.5 us
    ppermute x15 -> x16, waiting for transfers between devices: 18.4 us -> 14.1 us  [moved(): return lax.ppermute(value, stage, route)]
    ppermute x15 -> x16, starting transfers between devices: 18.2 us -> 21.5 us  [moved(): return lax.ppermute(value, stage, route)]
    pallas_call x4 -> x1, Pallas kernels: 1.58 us -> 1.51 us  [per_device(): pl.pallas_call(functools.partial(hidden_kernel, order), out_shape=[shape(...]
  transfers between devices with their start and end apart: 15 -> 16, of which waited for: 9 -> 8; matrix products, arithmetic and copies ran while one was open for 0% -> 0% of each run, Pallas kernels for 4% -> 4%
where the time goes in v4:
time: 43.4 us; the launch traced here: 43.2 us
  starting transfers between devices  21.5 us (50%)
  waiting for transfers between devices  14.1 us (32%)
  Pallas kernels  6.87 us (16%)
  between operations  0.69 us (2%)
    ppermute x16, starting transfers between devices, moved(): return lax.ppermute(value, stage, route)  21.5 us
    ppermute x16, waiting for transfers between devices, moved(): return lax.ppermute(value, stage, route)  14.1 us
    pallas_call x1, Pallas kernels, per_device(): pl.pallas_call(functools.partial(select_kernel, flight), out_shape=[shape...  2.65 us
    pallas_call x1, Pallas kernels, per_device(): pl.pallas_call(functools.partial(hidden_kernel, order), out_shape=[shape(...  1.51 us
    pallas_call x1, Pallas kernels, per_device(): pl.pallas_call(inputs_kernel, out_shape=r_shapes, compiler_params=PARAMS,...  1.39 us
    pallas_call x1, Pallas kernels, per_device(): pl.pallas_call(functools.partial(mix_kernel, flight), out_shape=[shape((c...  1.12 us
  transfers between devices with their start and end apart: 16, of which 8 were waited for; matrix products, arithmetic and copies ran while one was open for 0% of the time, Pallas kernels for 4%

profile of v4, /device:TPU:0, one launch (start us, length us, event | category | flops | bytes accessed | tf_op | source)
XLA Modules:
  0.0 43.2 jit_solution(7979502641331630853)
XLA Ops:
  0.6 2.7 %select.1 = (bf16[24,2048]{1,0:T(8,128)(2,1)S(1)}, bf16[24,2048]{1,0:T(8,128)(2,1)S(1)}, bf16[24,2048]{1,0:T(8,128)(2,1)S(1)}, bf16[24,2048]{1,0:T(8,128)(2,1)S(...) custom-call(s32[8,128]{1,0:T(8,128)} %bitcast.15, f32[8,128]{1,0:T(8,128)} %bitcast.22, ...), custom_call_target="tpu_custom_call" | custom-call | tf_op jit(solution)/shard_map/select/pallas_call | solution.py:255
  3.3 0.5 %collective-permute-start.2 = (bf16[6144,256]{1,0:T(8,128)(2,1)S(1)}, bf16[6144,256]{1,0:T(8,128)(2,1)S(1)}, u32[]{:S(2)}, u32[]{:S(2)}) collective-permute-start(bf16[6144,256]{1,0:T(8,128)(2,1)S(1)} %get-tuple-element.28.refs_8_.own_ref), channel_id=1, source_target_pairs={{0,1},{1,0},{2,3},{3,2},{4,5},{5,4},{6,7},{7,6},{8,9},{9,8},{10,11... | collective-permute-start | bytes 9437192 | tf_op jit(solution)/shard_map/ppermute | solution.py:238
  3.8 2.7 %collective-permute-start = (bf16[24,2048]{1,0:T(8,128)(2,1)S(1)}, bf16[24,2048]{1,0:T(8,128)(2,1)S(1)}, u32[]{:S(2)}, u32[]{:S(2)}) collective-permute-start(bf16[24,2048]{1,0:T(8,128)(2,1)S(1)} %get-tuple-element.26), channel_id=1, source_target_pairs={{0,5},{1,0},{2,7},{3,2},{4,1},{5,4},{6,3},{7,6},{8,13},{9,8},{10,1... | collective-permute-start | bytes 294920 | tf_op jit(solution)/shard_map/ppermute | solution.py:238
  6.5 2.6 %collective-permute-start.3 = (bf16[24,2048]{1,0:T(8,128)(2,1)S(1)}, bf16[24,2048]{1,0:T(8,128)(2,1)S(1)}, u32[]{:S(2)}, u32[]{:S(2)}) collective-permute-start(bf16[24,2048]{1,0:T(8,128)(2,1)S(1)} %get-tuple-element.30), channel_id=1, source_target_pairs={{0,8},{1,13},{2,10},{3,15},{4,12},{5,9},{6,14},{7,11},{8,0},{9,5},... | collective-permute-start | bytes 294920 | tf_op jit(solution)/shard_map/ppermute | solution.py:238
  9.1 0.7 %collective-permute-start.4 = (bf16[24,2048]{1,0:T(8,128)(2,1)S(1)}, bf16[24,2048]{1,0:T(8,128)(2,1)S(1)}, u32[]{:S(2)}, u32[]{:S(2)}) collective-permute-start(bf16[24,2048]{1,0:T(8,128)(2,1)S(1)} %get-tuple-element.31), channel_id=1, source_target_pairs={{0,0},{1,5},{2,2},{3,7},{4,4},{5,1},{6,6},{7,3},{8,8},{9,13},{10,1... | collective-permute-start | bytes 294920 | tf_op jit(solution)/shard_map/ppermute | solution.py:238
  9.7 1.1 %collective-permute-start.1 = (bf16[24,2048]{1,0:T(8,128)(2,1)S(1)}, bf16[24,2048]{1,0:T(8,128)(2,1)S(1)}, u32[]{:S(2)}, u32[]{:S(2)}) collective-permute-start(bf16[24,2048]{1,0:T(8,128)(2,1)S(1)} %get-tuple-element.27), channel_id=1, source_target_pairs={{0,13},{1,8},{2,15},{3,10},{4,9},{5,12},{6,11},{7,14},{8,5},{9,0},... | collective-permute-start | bytes 294920 | tf_op jit(solution)/shard_map/ppermute | solution.py:238
  10.9 1.5 %collective-permute-start.5 = (bf16[24,2048]{1,0:T(8,128)(2,1)S(1)}, bf16[24,2048]{1,0:T(8,128)(2,1)S(1)}, u32[]{:S(2)}, u32[]{:S(2)}) collective-permute-start(bf16[24,2048]{1,0:T(8,128)(2,1)S(1)} %collective-permute-done.refs_0_), channel_id=1, source_target_pairs={{0,2},{1,3},{2,0},{3,1},{4,6},{5,7},{6,4},{7,5},{8,10},{9,11},{10,... | collective-permute-start | bytes 294920 | tf_op jit(solution)/shard_map/ppermute | solution.py:238
  12.6 1.5 %collective-permute-start.8 = (bf16[24,2048]{1,0:T(8,128)(2,1)S(1)}, bf16[24,2048]{1,0:T(8,128)(2,1)S(1)}, u32[]{:S(2)}, u32[]{:S(2)}) collective-permute-start(bf16[24,2048]{1,0:T(8,128)(2,1)S(1)} %collective-permute-done.3.refs_2_), channel_id=1, source_target_pairs={{0,2},{1,3},{2,0},{3,1},{4,6},{5,7},{6,4},{7,5},{8,10},{9,11},{10,... | collective-permute-start | bytes 294920 | tf_op jit(solution)/shard_map/ppermute | solution.py:238
  14.7 3.1 %collective-permute-done.1.refs_1_ = bf16[24,2048]{1,0:T(8,128)(2,1)S(1)} collective-permute-done((bf16[24,2048]{1,0:T(8,128)(2,1)S(1)}, bf16[24,2048]{1,0:T(8,128)(2,1)S(1)}, u32[]{:S(2)}, u32[]{:S(2)}) %collective-permute-start.1) | collective-permute-done | bytes 98336 | tf_op jit(solution)/shard_map/ppermute | solution.py:238
  17.7 1.5 %collective-permute-start.7 = (bf16[24,2048]{1,0:T(8,128)(2,1)S(1)}, bf16[24,2048]{1,0:T(8,128)(2,1)S(1)}, u32[]{:S(2)}, u32[]{:S(2)}) collective-permute-start(bf16[24,2048]{1,0:T(8,128)(2,1)S(1)} %collective-permute-done.1.refs_1_), channel_id=1, source_target_pairs={{0,2},{1,3},{2,0},{3,1},{4,6},{5,7},{6,4},{7,5},{8,10},{9,11},{10,... | collective-permute-start | bytes 294920 | tf_op jit(solution)/shard_map/ppermute | solution.py:238
  19.3 0.8 %collective-permute-done.6.refs_5_ = bf16[24,2048]{1,0:T(8,128)(2,1)S(1)} collective-permute-done((bf16[24,2048]{1,0:T(8,128)(2,1)S(1)}, bf16[24,2048]{1,0:T(8,128)(2,1)S(1)}, u32[]{:S(2)}, u32[]{:S(2)}) %collective-permute-start.6) | collective-permute-done | bytes 98336 | tf_op jit(solution)/shard_map/ppermute | solution.py:238
  20.0 2.3 %collective-permute-done.7.refs_6_ = bf16[24,2048]{1,0:T(8,128)(2,1)S(1)} collective-permute-done((bf16[24,2048]{1,0:T(8,128)(2,1)S(1)}, bf16[24,2048]{1,0:T(8,128)(2,1)S(1)}, u32[]{:S(2)}, u32[]{:S(2)}) %collective-permute-start.7) | collective-permute-done | bytes 98336 | tf_op jit(solution)/shard_map/ppermute | solution.py:238
  22.3 1.5 %hidden.1 = (bf16[96,1024]{1,0:T(8,128)(2,1)S(1)}, bf16[16,128]{1,0:T(8,128)(2,1)S(1)}) custom-call(bf16[24,2048]{1,0:T(8,128)(2,1)S(1)} %collective-permute-done.refs_0_, bf16[24,2048]{1,0:T(8,128)(2,1)S(1)} %collective-permute-done.1.refs_1_, bf16[24,2048]{1,0:T(8,128)(2,1)S(1)} %collective-permute-done.3.refs_2_, ...), custom_call_target="tpu_custom_call" | custom-call | tf_op jit(solution)/shard_map/hidden/pallas_call | solution.py:284
  23.9 1.6 %collective-permute-start.9 = (bf16[16,128]{1,0:T(8,128)(2,1)S(1)}, bf16[16,128]{1,0:T(8,128)(2,1)S(1)}, u32[]{:S(2)}, u32[]{:S(2)}) collective-permute-start(bf16[16,128]{1,0:T(8,128)(2,1)S(1)} %get-tuple-element.33), channel_id=1, source_target_pairs={{0,16},{1,17},{2,18},{3,19},{4,20},{5,21},{6,22},{7,23},{8,24},{9,... | collective-permute-start | bytes 12296 | tf_op jit(solution)/shard_map/ppermute | solution.py:238
  25.4 1.4 %inputs_back.1 = (f32[32,1664]{1,0:T(8,128)S(1)}, f32[32,1664]{1,0:T(8,128)S(1)}, bf16[32,1664]{1,0:T(8,128)(2,1)S(1)}, bf16[32,1664]{1,0:T(8,128)(2,1)S(1)}) custom-call(bf16[96,1024]{1,0:T(8,128)(2,1)S(1)} %get-tuple-element.34.left_ref, bf16[6144,256]{1,0:T(8,128)(2,1)S(1)} %get-tuple-element.28.refs_8_.own_ref, ...), custom_call_target="tpu_custom_call" | custom-call | tf_op jit(solution)/shard_map/inputs_back/pallas_call | solution.py:292
  26.8 0.7 %collective-permute-done.9.part_ref = bf16[16,128]{1,0:T(8,128)(2,1)S(1)} collective-permute-done((bf16[16,128]{1,0:T(8,128)(2,1)S(1)}, bf16[16,128]{1,0:T(8,128)(2,1)S(1)}, u32[]{:S(2)}, u32[]{:S(2)}) %collective-permute-start.9) | collective-permute-done | bytes 4128 | tf_op jit(solution)/shard_map/ppermute | solution.py:238
  27.5 1.6 %collective-permute-start.10 = (bf16[32,1664]{1,0:T(8,128)(2,1)S(1)}, bf16[32,1664]{1,0:T(8,128)(2,1)S(1)}, u32[]{:S(2)}, u32[]{:S(2)}) collective-permute-start(bf16[32,1664]{1,0:T(8,128)(2,1)S(1)} %get-tuple-element.40), channel_id=1, source_target_pairs={{0,2},{1,3},{2,0},{3,1},{4,6},{5,7},{6,4},{7,5},{8,10},{9,11},{10,... | collective-permute-start | bytes 319496 | tf_op jit(solution)/shard_map/ppermute | solution.py:238
  29.6 2.7 %collective-permute-done.10.got_ref = bf16[32,1664]{1,0:T(8,128)(2,1)S(1)} collective-permute-done((bf16[32,1664]{1,0:T(8,128)(2,1)S(1)}, bf16[32,1664]{1,0:T(8,128)(2,1)S(1)}, u32[]{:S(2)}, u32[]{:S(2)}) %collective-permute-start.10) | collective-permute-done | bytes 106528 | tf_op jit(solution)/shard_map/ppermute | solution.py:238
  32.4 3.1 %collective-permute-start.11 = (bf16[32,1664]{1,0:T(8,128)(2,1)S(1)}, bf16[32,1664]{1,0:T(8,128)(2,1)S(1)}, u32[]{:S(2)}, u32[]{:S(2)}) collective-permute-start(bf16[32,1664]{1,0:T(8,128)(2,1)S(1)} %add_inputs_back.2), channel_id=1, source_target_pairs={{0,24},{1,29},{2,26},{3,31},{4,28},{5,25},{6,30},{7,27},{8,16},{9,... | collective-permute-start | bytes 319496 | tf_op jit(solution)/shard_map/ppermute | solution.py:238
  35.5 0.7 %collective-permute-start.14 = (bf16[32,1664]{1,0:T(8,128)(2,1)S(1)}, bf16[32,1664]{1,0:T(8,128)(2,1)S(1)}, u32[]{:S(2)}, u32[]{:S(2)}) collective-permute-start(bf16[32,1664]{1,0:T(8,128)(2,1)S(1)} %add_inputs_back.3), channel_id=1, source_target_pairs={{0,16},{1,21},{2,18},{3,23},{4,20},{5,17},{6,22},{7,19},{8,24},{9,... | collective-permute-start | bytes 319496 | tf_op jit(solution)/shard_map/ppermute | solution.py:238
  36.3 1.3 %collective-permute-start.12 = (bf16[16,1024]{1,0:T(8,128)(2,1)S(1)}, bf16[16,1024]{1,0:T(8,128)(2,1)S(1)}, u32[]{:S(2)}, u32[]{:S(2)}) collective-permute-start(bf16[16,1024]{1,0:T(8,128)(2,1)S(1)} %get-tuple-element.41), channel_id=1, source_target_pairs={{0,16},{1,17},{2,18},{3,19},{4,20},{5,21},{6,22},{7,23},{8,24},{9,... | collective-permute-start | bytes 98312 | tf_op jit(solution)/shard_map/ppermute | solution.py:238
  37.6 3.0 %collective-permute-done.12.mix_ref = bf16[16,1024]{1,0:T(8,128)(2,1)S(1)} collective-permute-done((bf16[16,1024]{1,0:T(8,128)(2,1)S(1)}, bf16[16,1024]{1,0:T(8,128)(2,1)S(1)}, u32[]{:S(2)}, u32[]{:S(2)}) %collective-permute-start.12) | collective-permute-done | bytes 32800 | tf_op jit(solution)/shard_map/ppermute | solution.py:238
  40.7 1.3 %collective-permute-done.15.near_ref = bf16[32,1664]{1,0:T(8,128)(2,1)S(1)} collective-permute-done((bf16[32,1664]{1,0:T(8,128)(2,1)S(1)}, bf16[32,1664]{1,0:T(8,128)(2,1)S(1)}, u32[]{:S(2)}, u32[]{:S(2)}) %collective-permute-start.15) | collective-permute-done | bytes 106528 | tf_op jit(solution)/shard_map/ppermute | solution.py:238
  42.0 1.1 %mix.1 = (bf16[128,2048]{1,0:T(8,128)(2,1)}, f32[8,128]{1,0:T(8,128)}) custom-call(s32[8,128]{1,0:T(8,128)S(1)} %bitcast.16, f32[64,128]{1,0:T(8,128)S(1)} %get-tuple-element.25.place_ref, bf16[16,1024]{1,0:T(8,128)(2,1)S(1)} %collective-permute-done.12.mix_ref, bf16[32,1664]{1,0:T(8,128)(2,1)S(1)} %collective-permute-done.15.near_ref, ...), custom_call_target="tpu_custom_call" | custom-call | tf_op jit(solution)/shard_map/mix/pallas_call | solution.py:324
  (18 shorter events, 1.5 us)
Async XLA Ops:
  3.3 14.4 %collective-permute-start.2 = (bf16[6144,256]{1,0:T(8,128)(2,1)S(1)}, bf16[6144,256]{1,0:T(8,128)(2,1)S(1)}, u32[]{:S(2)}, u32[]{:S(2)}) collective-permute-start(bf16[6144,256]{1,0:T(8,128)(2,1)S(1)} %get-tuple-element.28.refs_8_.own_ref), channel_id=1, source_target_pairs={{0,1},{1,0},{2,3},{3,2},{4,5},{5,4},{6,7},{7,6},{8,9},{9,8},{10,11... | collective-permute-start | bytes 9437192 | tf_op jit(solution)/shard_map/ppermute | solution.py:238
  3.8 7.1 %collective-permute-start = (bf16[24,2048]{1,0:T(8,128)(2,1)S(1)}, bf16[24,2048]{1,0:T(8,128)(2,1)S(1)}, u32[]{:S(2)}, u32[]{:S(2)}) collective-permute-start(bf16[24,2048]{1,0:T(8,128)(2,1)S(1)} %get-tuple-element.26), channel_id=1, source_target_pairs={{0,5},{1,0},{2,7},{3,2},{4,1},{5,4},{6,3},{7,6},{8,13},{9,8},{10,1... | collective-permute-start | bytes 294920 | tf_op jit(solution)/shard_map/ppermute | solution.py:238
  6.5 6.1 %collective-permute-start.3 = (bf16[24,2048]{1,0:T(8,128)(2,1)S(1)}, bf16[24,2048]{1,0:T(8,128)(2,1)S(1)}, u32[]{:S(2)}, u32[]{:S(2)}) collective-permute-start(bf16[24,2048]{1,0:T(8,128)(2,1)S(1)} %get-tuple-element.30), channel_id=1, source_target_pairs={{0,8},{1,13},{2,10},{3,15},{4,12},{5,9},{6,14},{7,11},{8,0},{9,5},... | collective-permute-start | bytes 294920 | tf_op jit(solution)/shard_map/ppermute | solution.py:238
  9.1 5.0 %collective-permute-start.4 = (bf16[24,2048]{1,0:T(8,128)(2,1)S(1)}, bf16[24,2048]{1,0:T(8,128)(2,1)S(1)}, u32[]{:S(2)}, u32[]{:S(2)}) collective-permute-start(bf16[24,2048]{1,0:T(8,128)(2,1)S(1)} %get-tuple-element.31), channel_id=1, source_target_pairs={{0,0},{1,5},{2,2},{3,7},{4,4},{5,1},{6,6},{7,3},{8,8},{9,13},{10,1... | collective-permute-start | bytes 294920 | tf_op jit(solution)/shard_map/ppermute | solution.py:238
  9.7 8.0 %collective-permute-start.1 = (bf16[24,2048]{1,0:T(8,128)(2,1)S(1)}, bf16[24,2048]{1,0:T(8,128)(2,1)S(1)}, u32[]{:S(2)}, u32[]{:S(2)}) collective-permute-start(bf16[24,2048]{1,0:T(8,128)(2,1)S(1)} %get-tuple-element.27), channel_id=1, source_target_pairs={{0,13},{1,8},{2,15},{3,10},{4,9},{5,12},{6,11},{7,14},{8,5},{9,0},... | collective-permute-start | bytes 294920 | tf_op jit(solution)/shard_map/ppermute | solution.py:238
  10.9 8.4 %collective-permute-start.5 = (bf16[24,2048]{1,0:T(8,128)(2,1)S(1)}, bf16[24,2048]{1,0:T(8,128)(2,1)S(1)}, u32[]{:S(2)}, u32[]{:S(2)}) collective-permute-start(bf16[24,2048]{1,0:T(8,128)(2,1)S(1)} %collective-permute-done.refs_0_), channel_id=1, source_target_pairs={{0,2},{1,3},{2,0},{3,1},{4,6},{5,7},{6,4},{7,5},{8,10},{9,11},{10,... | collective-permute-start | bytes 294920 | tf_op jit(solution)/shard_map/ppermute | solution.py:238
  12.6 6.6 %collective-permute-start.8 = (bf16[24,2048]{1,0:T(8,128)(2,1)S(1)}, bf16[24,2048]{1,0:T(8,128)(2,1)S(1)}, u32[]{:S(2)}, u32[]{:S(2)}) collective-permute-start(bf16[24,2048]{1,0:T(8,128)(2,1)S(1)} %collective-permute-done.3.refs_2_), channel_id=1, source_target_pairs={{0,2},{1,3},{2,0},{3,1},{4,6},{5,7},{6,4},{7,5},{8,10},{9,11},{10,... | collective-permute-start | bytes 294920 | tf_op jit(solution)/shard_map/ppermute | solution.py:238
  14.1 5.9 %collective-permute-start.6 = (bf16[24,2048]{1,0:T(8,128)(2,1)S(1)}, bf16[24,2048]{1,0:T(8,128)(2,1)S(1)}, u32[]{:S(2)}, u32[]{:S(2)}) collective-permute-start(bf16[24,2048]{1,0:T(8,128)(2,1)S(1)} %collective-permute-done.4.refs_3_), channel_id=1, source_target_pairs={{0,2},{1,3},{2,0},{3,1},{4,6},{5,7},{6,4},{7,5},{8,10},{9,11},{10,... | collective-permute-start | bytes 294920 | tf_op jit(solution)/shard_map/ppermute | solution.py:238
  17.7 4.6 %collective-permute-start.7 = (bf16[24,2048]{1,0:T(8,128)(2,1)S(1)}, bf16[24,2048]{1,0:T(8,128)(2,1)S(1)}, u32[]{:S(2)}, u32[]{:S(2)}) collective-permute-start(bf16[24,2048]{1,0:T(8,128)(2,1)S(1)} %collective-permute-done.1.refs_1_), channel_id=1, source_target_pairs={{0,2},{1,3},{2,0},{3,1},{4,6},{5,7},{6,4},{7,5},{8,10},{9,11},{10,... | collective-permute-start | bytes 294920 | tf_op jit(solution)/shard_map/ppermute | solution.py:238
  23.9 3.7 %collective-permute-start.9 = (bf16[16,128]{1,0:T(8,128)(2,1)S(1)}, bf16[16,128]{1,0:T(8,128)(2,1)S(1)}, u32[]{:S(2)}, u32[]{:S(2)}) collective-permute-start(bf16[16,128]{1,0:T(8,128)(2,1)S(1)} %get-tuple-element.33), channel_id=1, source_target_pairs={{0,16},{1,17},{2,18},{3,19},{4,20},{5,21},{6,22},{7,23},{8,24},{9,... | collective-permute-start | bytes 12296 | tf_op jit(solution)/shard_map/ppermute | solution.py:238
  25.4 16.6 %copy-start = (s32[1,128,8]{1,2,0:T(8,128)S(1)}, s32[1,128,8]{1,2,0:T(8,128)}, u32[]{:S(2)}) copy-start(s32[1,128,8]{1,2,0:T(8,128)} %param.9) | copy-start | bytes 12292
  27.5 4.8 %collective-permute-start.10 = (bf16[32,1664]{1,0:T(8,128)(2,1)S(1)}, bf16[32,1664]{1,0:T(8,128)(2,1)S(1)}, u32[]{:S(2)}, u32[]{:S(2)}) collective-permute-start(bf16[32,1664]{1,0:T(8,128)(2,1)S(1)} %get-tuple-element.40), channel_id=1, source_target_pairs={{0,2},{1,3},{2,0},{3,1},{4,6},{5,7},{6,4},{7,5},{8,10},{9,11},{10,... | collective-permute-start | bytes 319496 | tf_op jit(solution)/shard_map/ppermute | solution.py:238
  29.1 6.3 %collective-permute-start.13 = (bf16[32,1664]{1,0:T(8,128)(2,1)S(1)}, bf16[32,1664]{1,0:T(8,128)(2,1)S(1)}, u32[]{:S(2)}, u32[]{:S(2)}) collective-permute-start(bf16[32,1664]{1,0:T(8,128)(2,1)S(1)} %get-tuple-element.45), channel_id=1, source_target_pairs={{0,2},{1,3},{2,0},{3,1},{4,6},{5,7},{6,4},{7,5},{8,10},{9,11},{10,... | collective-permute-start | bytes 319496 | tf_op jit(solution)/shard_map/ppermute | solution.py:238
  32.4 8.2 %collective-permute-start.11 = (bf16[32,1664]{1,0:T(8,128)(2,1)S(1)}, bf16[32,1664]{1,0:T(8,128)(2,1)S(1)}, u32[]{:S(2)}, u32[]{:S(2)}) collective-permute-start(bf16[32,1664]{1,0:T(8,128)(2,1)S(1)} %add_inputs_back.2), channel_id=1, source_target_pairs={{0,24},{1,29},{2,26},{3,31},{4,28},{5,25},{6,30},{7,27},{8,16},{9,... | collective-permute-start | bytes 319496 | tf_op jit(solution)/shard_map/ppermute | solution.py:238
  35.5 5.1 %collective-permute-start.14 = (bf16[32,1664]{1,0:T(8,128)(2,1)S(1)}, bf16[32,1664]{1,0:T(8,128)(2,1)S(1)}, u32[]{:S(2)}, u32[]{:S(2)}) collective-permute-start(bf16[32,1664]{1,0:T(8,128)(2,1)S(1)} %add_inputs_back.3), channel_id=1, source_target_pairs={{0,16},{1,21},{2,18},{3,23},{4,20},{5,17},{6,22},{7,19},{8,24},{9,... | collective-permute-start | bytes 319496 | tf_op jit(solution)/shard_map/ppermute | solution.py:238
  36.3 4.3 %collective-permute-start.12 = (bf16[16,1024]{1,0:T(8,128)(2,1)S(1)}, bf16[16,1024]{1,0:T(8,128)(2,1)S(1)}, u32[]{:S(2)}, u32[]{:S(2)}) collective-permute-start(bf16[16,1024]{1,0:T(8,128)(2,1)S(1)} %get-tuple-element.41), channel_id=1, source_target_pairs={{0,16},{1,17},{2,18},{3,19},{4,20},{5,21},{6,22},{7,23},{8,24},{9,... | collective-permute-start | bytes 98312 | tf_op jit(solution)/shard_map/ppermute | solution.py:238
  40.7 1.4 %collective-permute-start.15 = (bf16[32,1664]{1,0:T(8,128)(2,1)S(1)}, bf16[32,1664]{1,0:T(8,128)(2,1)S(1)}, u32[]{:S(2)}, u32[]{:S(2)}) collective-permute-start(bf16[32,1664]{1,0:T(8,128)(2,1)S(1)} %other_core.1), channel_id=1, source_target_pairs={{0,1},{1,0},{2,3},{3,2},{4,5},{5,4},{6,7},{7,6},{8,9},{9,8},{10,11... | collective-permute-start | bytes 319496 | tf_op jit(solution)/shard_map/ppermute | solution.py:238

commit v5 on v4

--- a/solution.py
+++ b/solution.py
@@ -44,8 +44,10 @@
             [(ids_hbm, ids_ref), (gates_hbm, gates_ref), (x_hbm, x_ref), (g_hbm, g_ref)]
         )
     ]
-    for copy in first + later:
+    for copy in first:
         copy.start()
+    for copy in later:
+        copy.start(priority=1)
     own = lax.axis_index("expert") // SLICES
     parity = lax.axis_index("expert") % 2
     first[0].wait()

time: 43.4 us -> 43 us (level)
  no operation moved by 1% of the time
where the time goes in v5:
time: 43 us; the launch traced here: 42.8 us
  starting transfers between devices  21.5 us (50%)
  waiting for transfers between devices  14.1 us (33%)
  Pallas kernels  6.5 us (15%)
  between operations  0.69 us (2%)
    ppermute x16, starting transfers between devices, moved(): return lax.ppermute(value, stage, route)  21.5 us
    ppermute x16, waiting for transfers between devices, moved(): return lax.ppermute(value, stage, route)  14.1 us
    pallas_call x1, Pallas kernels, per_device(): pl.pallas_call(functools.partial(select_kernel, flight), out_shape=[shape...  2.28 us
    pallas_call x1, Pallas kernels, per_device(): pl.pallas_call(functools.partial(hidden_kernel, order), out_shape=[shape(...  1.52 us
    pallas_call x1, Pallas kernels, per_device(): pl.pallas_call(inputs_kernel, out_shape=r_shapes, compiler_params=PARAMS,...  1.39 us
    pallas_call x1, Pallas kernels, per_device(): pl.pallas_call(functools.partial(mix_kernel, flight), out_shape=[shape((c...  1.12 us
  transfers between devices with their start and end apart: 16, of which 8 were waited for; matrix products, arithmetic and copies ran while one was open for 0% of the time, Pallas kernels for 4%

profile of v5, /device:TPU:0, one launch (start us, length us, event | category | flops | bytes accessed | tf_op | source)
XLA Modules:
  0.0 42.8 jit_solution(204546131926592687)
XLA Ops:
  0.6 2.3 %select.1 = (bf16[24,2048]{1,0:T(8,128)(2,1)S(1)}, bf16[24,2048]{1,0:T(8,128)(2,1)S(1)}, bf16[24,2048]{1,0:T(8,128)(2,1)S(1)}, bf16[24,2048]{1,0:T(8,128)(2,1)S(...) custom-call(s32[8,128]{1,0:T(8,128)} %bitcast.15, f32[8,128]{1,0:T(8,128)} %bitcast.22, ...), custom_call_target="tpu_custom_call" | custom-call | tf_op jit(solution)/shard_map/select/pallas_call | solution.py:257
  2.9 0.5 %collective-permute-start.2 = (bf16[6144,256]{1,0:T(8,128)(2,1)S(1)}, bf16[6144,256]{1,0:T(8,128)(2,1)S(1)}, u32[]{:S(2)}, u32[]{:S(2)}) collective-permute-start(bf16[6144,256]{1,0:T(8,128)(2,1)S(1)} %get-tuple-element.28.refs_8_.own_ref), channel_id=1, source_target_pairs={{0,1},{1,0},{2,3},{3,2},{4,5},{5,4},{6,7},{7,6},{8,9},{9,8},{10,11... | collective-permute-start | bytes 9437192 | tf_op jit(solution)/shard_map/ppermute | solution.py:240
  3.4 2.7 %collective-permute-start = (bf16[24,2048]{1,0:T(8,128)(2,1)S(1)}, bf16[24,2048]{1,0:T(8,128)(2,1)S(1)}, u32[]{:S(2)}, u32[]{:S(2)}) collective-permute-start(bf16[24,2048]{1,0:T(8,128)(2,1)S(1)} %get-tuple-element.26), channel_id=1, source_target_pairs={{0,5},{1,0},{2,7},{3,2},{4,1},{5,4},{6,3},{7,6},{8,13},{9,8},{10,1... | collective-permute-start | bytes 294920 | tf_op jit(solution)/shard_map/ppermute | solution.py:240
  6.1 2.6 %collective-permute-start.3 = (bf16[24,2048]{1,0:T(8,128)(2,1)S(1)}, bf16[24,2048]{1,0:T(8,128)(2,1)S(1)}, u32[]{:S(2)}, u32[]{:S(2)}) collective-permute-start(bf16[24,2048]{1,0:T(8,128)(2,1)S(1)} %get-tuple-element.30), channel_id=1, source_target_pairs={{0,8},{1,13},{2,10},{3,15},{4,12},{5,9},{6,14},{7,11},{8,0},{9,5},... | collective-permute-start | bytes 294920 | tf_op jit(solution)/shard_map/ppermute | solution.py:240
  8.7 0.7 %collective-permute-start.4 = (bf16[24,2048]{1,0:T(8,128)(2,1)S(1)}, bf16[24,2048]{1,0:T(8,128)(2,1)S(1)}, u32[]{:S(2)}, u32[]{:S(2)}) collective-permute-start(bf16[24,2048]{1,0:T(8,128)(2,1)S(1)} %get-tuple-element.31), channel_id=1, source_target_pairs={{0,0},{1,5},{2,2},{3,7},{4,4},{5,1},{6,6},{7,3},{8,8},{9,13},{10,1... | collective-permute-start | bytes 294920 | tf_op jit(solution)/shard_map/ppermute | solution.py:240
  9.4 1.1 %collective-permute-start.1 = (bf16[24,2048]{1,0:T(8,128)(2,1)S(1)}, bf16[24,2048]{1,0:T(8,128)(2,1)S(1)}, u32[]{:S(2)}, u32[]{:S(2)}) collective-permute-start(bf16[24,2048]{1,0:T(8,128)(2,1)S(1)} %get-tuple-element.27), channel_id=1, source_target_pairs={{0,13},{1,8},{2,15},{3,10},{4,9},{5,12},{6,11},{7,14},{8,5},{9,0},... | collective-permute-start | bytes 294920 | tf_op jit(solution)/shard_map/ppermute | solution.py:240
  10.5 1.5 %collective-permute-start.5 = (bf16[24,2048]{1,0:T(8,128)(2,1)S(1)}, bf16[24,2048]{1,0:T(8,128)(2,1)S(1)}, u32[]{:S(2)}, u32[]{:S(2)}) collective-permute-start(bf16[24,2048]{1,0:T(8,128)(2,1)S(1)} %collective-permute-done.refs_0_), channel_id=1, source_target_pairs={{0,2},{1,3},{2,0},{3,1},{4,6},{5,7},{6,4},{7,5},{8,10},{9,11},{10,... | collective-permute-start | bytes 294920 | tf_op jit(solution)/shard_map/ppermute | solution.py:240
  12.2 1.5 %collective-permute-start.8 = (bf16[24,2048]{1,0:T(8,128)(2,1)S(1)}, bf16[24,2048]{1,0:T(8,128)(2,1)S(1)}, u32[]{:S(2)}, u32[]{:S(2)}) collective-permute-start(bf16[24,2048]{1,0:T(8,128)(2,1)S(1)} %collective-permute-done.3.refs_2_), channel_id=1, source_target_pairs={{0,2},{1,3},{2,0},{3,1},{4,6},{5,7},{6,4},{7,5},{8,10},{9,11},{10,... | collective-permute-start | bytes 294920 | tf_op jit(solution)/shard_map/ppermute | solution.py:240
  14.3 3.1 %collective-permute-done.1.refs_1_ = bf16[24,2048]{1,0:T(8,128)(2,1)S(1)} collective-permute-done((bf16[24,2048]{1,0:T(8,128)(2,1)S(1)}, bf16[24,2048]{1,0:T(8,128)(2,1)S(1)}, u32[]{:S(2)}, u32[]{:S(2)}) %collective-permute-start.1) | collective-permute-done | bytes 98336 | tf_op jit(solution)/shard_map/ppermute | solution.py:240
  17.4 1.5 %collective-permute-start.7 = (bf16[24,2048]{1,0:T(8,128)(2,1)S(1)}, bf16[24,2048]{1,0:T(8,128)(2,1)S(1)}, u32[]{:S(2)}, u32[]{:S(2)}) collective-permute-start(bf16[24,2048]{1,0:T(8,128)(2,1)S(1)} %collective-permute-done.1.refs_1_), channel_id=1, source_target_pairs={{0,2},{1,3},{2,0},{3,1},{4,6},{5,7},{6,4},{7,5},{8,10},{9,11},{10,... | collective-permute-start | bytes 294920 | tf_op jit(solution)/shard_map/ppermute | solution.py:240
  18.9 0.8 %collective-permute-done.6.refs_5_ = bf16[24,2048]{1,0:T(8,128)(2,1)S(1)} collective-permute-done((bf16[24,2048]{1,0:T(8,128)(2,1)S(1)}, bf16[24,2048]{1,0:T(8,128)(2,1)S(1)}, u32[]{:S(2)}, u32[]{:S(2)}) %collective-permute-start.6) | collective-permute-done | bytes 98336 | tf_op jit(solution)/shard_map/ppermute | solution.py:240
  19.7 2.3 %collective-permute-done.7.refs_6_ = bf16[24,2048]{1,0:T(8,128)(2,1)S(1)} collective-permute-done((bf16[24,2048]{1,0:T(8,128)(2,1)S(1)}, bf16[24,2048]{1,0:T(8,128)(2,1)S(1)}, u32[]{:S(2)}, u32[]{:S(2)}) %collective-permute-start.7) | collective-permute-done | bytes 98336 | tf_op jit(solution)/shard_map/ppermute | solution.py:240
  22.0 1.5 %hidden.1 = (bf16[96,1024]{1,0:T(8,128)(2,1)S(1)}, bf16[16,128]{1,0:T(8,128)(2,1)S(1)}) custom-call(bf16[24,2048]{1,0:T(8,128)(2,1)S(1)} %collective-permute-done.refs_0_, bf16[24,2048]{1,0:T(8,128)(2,1)S(1)} %collective-permute-done.1.refs_1_, bf16[24,2048]{1,0:T(8,128)(2,1)S(1)} %collective-permute-done.3.refs_2_, ...), custom_call_target="tpu_custom_call" | custom-call | tf_op jit(solution)/shard_map/hidden/pallas_call | solution.py:286
  23.5 1.6 %collective-permute-start.9 = (bf16[16,128]{1,0:T(8,128)(2,1)S(1)}, bf16[16,128]{1,0:T(8,128)(2,1)S(1)}, u32[]{:S(2)}, u32[]{:S(2)}) collective-permute-start(bf16[16,128]{1,0:T(8,128)(2,1)S(1)} %get-tuple-element.33), channel_id=1, source_target_pairs={{0,16},{1,17},{2,18},{3,19},{4,20},{5,21},{6,22},{7,23},{8,24},{9,... | collective-permute-start | bytes 12296 | tf_op jit(solution)/shard_map/ppermute | solution.py:240
  25.1 1.4 %inputs_back.1 = (f32[32,1664]{1,0:T(8,128)S(1)}, f32[32,1664]{1,0:T(8,128)S(1)}, bf16[32,1664]{1,0:T(8,128)(2,1)S(1)}, bf16[32,1664]{1,0:T(8,128)(2,1)S(1)}) custom-call(bf16[96,1024]{1,0:T(8,128)(2,1)S(1)} %get-tuple-element.34.left_ref, bf16[6144,256]{1,0:T(8,128)(2,1)S(1)} %get-tuple-element.28.refs_8_.own_ref, ...), custom_call_target="tpu_custom_call" | custom-call | tf_op jit(solution)/shard_map/inputs_back/pallas_call | solution.py:294
  26.5 0.7 %collective-permute-done.9.part_ref = bf16[16,128]{1,0:T(8,128)(2,1)S(1)} collective-permute-done((bf16[16,128]{1,0:T(8,128)(2,1)S(1)}, bf16[16,128]{1,0:T(8,128)(2,1)S(1)}, u32[]{:S(2)}, u32[]{:S(2)}) %collective-permute-start.9) | collective-permute-done | bytes 4128 | tf_op jit(solution)/shard_map/ppermute | solution.py:240
  27.2 1.6 %collective-permute-start.10 = (bf16[32,1664]{1,0:T(8,128)(2,1)S(1)}, bf16[32,1664]{1,0:T(8,128)(2,1)S(1)}, u32[]{:S(2)}, u32[]{:S(2)}) collective-permute-start(bf16[32,1664]{1,0:T(8,128)(2,1)S(1)} %get-tuple-element.40), channel_id=1, source_target_pairs={{0,2},{1,3},{2,0},{3,1},{4,6},{5,7},{6,4},{7,5},{8,10},{9,11},{10,... | collective-permute-start | bytes 319496 | tf_op jit(solution)/shard_map/ppermute | solution.py:240
  29.3 2.7 %collective-permute-done.10.got_ref = bf16[32,1664]{1,0:T(8,128)(2,1)S(1)} collective-permute-done((bf16[32,1664]{1,0:T(8,128)(2,1)S(1)}, bf16[32,1664]{1,0:T(8,128)(2,1)S(1)}, u32[]{:S(2)}, u32[]{:S(2)}) %collective-permute-start.10) | collective-permute-done | bytes 106528 | tf_op jit(solution)/shard_map/ppermute | solution.py:240
  32.0 3.0 %collective-permute-start.11 = (bf16[32,1664]{1,0:T(8,128)(2,1)S(1)}, bf16[32,1664]{1,0:T(8,128)(2,1)S(1)}, u32[]{:S(2)}, u32[]{:S(2)}) collective-permute-start(bf16[32,1664]{1,0:T(8,128)(2,1)S(1)} %add_inputs_back.2), channel_id=1, source_target_pairs={{0,24},{1,29},{2,26},{3,31},{4,28},{5,25},{6,30},{7,27},{8,16},{9,... | collective-permute-start | bytes 319496 | tf_op jit(solution)/shard_map/ppermute | solution.py:240
  35.2 0.7 %collective-permute-start.14 = (bf16[32,1664]{1,0:T(8,128)(2,1)S(1)}, bf16[32,1664]{1,0:T(8,128)(2,1)S(1)}, u32[]{:S(2)}, u32[]{:S(2)}) collective-permute-start(bf16[32,1664]{1,0:T(8,128)(2,1)S(1)} %add_inputs_back.3), channel_id=1, source_target_pairs={{0,16},{1,21},{2,18},{3,23},{4,20},{5,17},{6,22},{7,19},{8,24},{9,... | collective-permute-start | bytes 319496 | tf_op jit(solution)/shard_map/ppermute | solution.py:240
  35.9 1.3 %collective-permute-start.12 = (bf16[16,1024]{1,0:T(8,128)(2,1)S(1)}, bf16[16,1024]{1,0:T(8,128)(2,1)S(1)}, u32[]{:S(2)}, u32[]{:S(2)}) collective-permute-start(bf16[16,1024]{1,0:T(8,128)(2,1)S(1)} %get-tuple-element.41), channel_id=1, source_target_pairs={{0,16},{1,17},{2,18},{3,19},{4,20},{5,21},{6,22},{7,23},{8,24},{9,... | collective-permute-start | bytes 98312 | tf_op jit(solution)/shard_map/ppermute | solution.py:240
  37.2 3.0 %collective-permute-done.12.mix_ref = bf16[16,1024]{1,0:T(8,128)(2,1)S(1)} collective-permute-done((bf16[16,1024]{1,0:T(8,128)(2,1)S(1)}, bf16[16,1024]{1,0:T(8,128)(2,1)S(1)}, u32[]{:S(2)}, u32[]{:S(2)}) %collective-permute-start.12) | collective-permute-done | bytes 32800 | tf_op jit(solution)/shard_map/ppermute | solution.py:240
  40.4 1.3 %collective-permute-done.15.near_ref = bf16[32,1664]{1,0:T(8,128)(2,1)S(1)} collective-permute-done((bf16[32,1664]{1,0:T(8,128)(2,1)S(1)}, bf16[32,1664]{1,0:T(8,128)(2,1)S(1)}, u32[]{:S(2)}, u32[]{:S(2)}) %collective-permute-start.15) | collective-permute-done | bytes 106528 | tf_op jit(solution)/shard_map/ppermute | solution.py:240
  41.7 1.1 %mix.1 = (bf16[128,2048]{1,0:T(8,128)(2,1)}, f32[8,128]{1,0:T(8,128)}) custom-call(s32[8,128]{1,0:T(8,128)S(1)} %bitcast.16, f32[64,128]{1,0:T(8,128)S(1)} %get-tuple-element.25.place_ref, bf16[16,1024]{1,0:T(8,128)(2,1)S(1)} %collective-permute-done.12.mix_ref, bf16[32,1664]{1,0:T(8,128)(2,1)S(1)} %collective-permute-done.15.near_ref, ...), custom_call_target="tpu_custom_call" | custom-call | tf_op jit(solution)/shard_map/mix/pallas_call | solution.py:326
  (18 shorter events, 1.5 us)
Async XLA Ops:
  2.9 14.4 %collective-permute-start.2 = (bf16[6144,256]{1,0:T(8,128)(2,1)S(1)}, bf16[6144,256]{1,0:T(8,128)(2,1)S(1)}, u32[]{:S(2)}, u32[]{:S(2)}) collective-permute-start(bf16[6144,256]{1,0:T(8,128)(2,1)S(1)} %get-tuple-element.28.refs_8_.own_ref), channel_id=1, source_target_pairs={{0,1},{1,0},{2,3},{3,2},{4,5},{5,4},{6,7},{7,6},{8,9},{9,8},{10,11... | collective-permute-start | bytes 9437192 | tf_op jit(solution)/shard_map/ppermute | solution.py:240
  3.4 7.1 %collective-permute-start = (bf16[24,2048]{1,0:T(8,128)(2,1)S(1)}, bf16[24,2048]{1,0:T(8,128)(2,1)S(1)}, u32[]{:S(2)}, u32[]{:S(2)}) collective-permute-start(bf16[24,2048]{1,0:T(8,128)(2,1)S(1)} %get-tuple-element.26), channel_id=1, source_target_pairs={{0,5},{1,0},{2,7},{3,2},{4,1},{5,4},{6,3},{7,6},{8,13},{9,8},{10,1... | collective-permute-start | bytes 294920 | tf_op jit(solution)/shard_map/ppermute | solution.py:240
  6.1 6.1 %collective-permute-start.3 = (bf16[24,2048]{1,0:T(8,128)(2,1)S(1)}, bf16[24,2048]{1,0:T(8,128)(2,1)S(1)}, u32[]{:S(2)}, u32[]{:S(2)}) collective-permute-start(bf16[24,2048]{1,0:T(8,128)(2,1)S(1)} %get-tuple-element.30), channel_id=1, source_target_pairs={{0,8},{1,13},{2,10},{3,15},{4,12},{5,9},{6,14},{7,11},{8,0},{9,5},... | collective-permute-start | bytes 294920 | tf_op jit(solution)/shard_map/ppermute | solution.py:240
  8.7 5.0 %collective-permute-start.4 = (bf16[24,2048]{1,0:T(8,128)(2,1)S(1)}, bf16[24,2048]{1,0:T(8,128)(2,1)S(1)}, u32[]{:S(2)}, u32[]{:S(2)}) collective-permute-start(bf16[24,2048]{1,0:T(8,128)(2,1)S(1)} %get-tuple-element.31), channel_id=1, source_target_pairs={{0,0},{1,5},{2,2},{3,7},{4,4},{5,1},{6,6},{7,3},{8,8},{9,13},{10,1... | collective-permute-start | bytes 294920 | tf_op jit(solution)/shard_map/ppermute | solution.py:240
  9.4 8.0 %collective-permute-start.1 = (bf16[24,2048]{1,0:T(8,128)(2,1)S(1)}, bf16[24,2048]{1,0:T(8,128)(2,1)S(1)}, u32[]{:S(2)}, u32[]{:S(2)}) collective-permute-start(bf16[24,2048]{1,0:T(8,128)(2,1)S(1)} %get-tuple-element.27), channel_id=1, source_target_pairs={{0,13},{1,8},{2,15},{3,10},{4,9},{5,12},{6,11},{7,14},{8,5},{9,0},... | collective-permute-start | bytes 294920 | tf_op jit(solution)/shard_map/ppermute | solution.py:240
  10.5 8.4 %collective-permute-start.5 = (bf16[24,2048]{1,0:T(8,128)(2,1)S(1)}, bf16[24,2048]{1,0:T(8,128)(2,1)S(1)}, u32[]{:S(2)}, u32[]{:S(2)}) collective-permute-start(bf16[24,2048]{1,0:T(8,128)(2,1)S(1)} %collective-permute-done.refs_0_), channel_id=1, source_target_pairs={{0,2},{1,3},{2,0},{3,1},{4,6},{5,7},{6,4},{7,5},{8,10},{9,11},{10,... | collective-permute-start | bytes 294920 | tf_op jit(solution)/shard_map/ppermute | solution.py:240
  12.2 6.6 %collective-permute-start.8 = (bf16[24,2048]{1,0:T(8,128)(2,1)S(1)}, bf16[24,2048]{1,0:T(8,128)(2,1)S(1)}, u32[]{:S(2)}, u32[]{:S(2)}) collective-permute-start(bf16[24,2048]{1,0:T(8,128)(2,1)S(1)} %collective-permute-done.3.refs_2_), channel_id=1, source_target_pairs={{0,2},{1,3},{2,0},{3,1},{4,6},{5,7},{6,4},{7,5},{8,10},{9,11},{10,... | collective-permute-start | bytes 294920 | tf_op jit(solution)/shard_map/ppermute | solution.py:240
  13.8 5.9 %collective-permute-start.6 = (bf16[24,2048]{1,0:T(8,128)(2,1)S(1)}, bf16[24,2048]{1,0:T(8,128)(2,1)S(1)}, u32[]{:S(2)}, u32[]{:S(2)}) collective-permute-start(bf16[24,2048]{1,0:T(8,128)(2,1)S(1)} %collective-permute-done.4.refs_3_), channel_id=1, source_target_pairs={{0,2},{1,3},{2,0},{3,1},{4,6},{5,7},{6,4},{7,5},{8,10},{9,11},{10,... | collective-permute-start | bytes 294920 | tf_op jit(solution)/shard_map/ppermute | solution.py:240
  17.4 4.6 %collective-permute-start.7 = (bf16[24,2048]{1,0:T(8,128)(2,1)S(1)}, bf16[24,2048]{1,0:T(8,128)(2,1)S(1)}, u32[]{:S(2)}, u32[]{:S(2)}) collective-permute-start(bf16[24,2048]{1,0:T(8,128)(2,1)S(1)} %collective-permute-done.1.refs_1_), channel_id=1, source_target_pairs={{0,2},{1,3},{2,0},{3,1},{4,6},{5,7},{6,4},{7,5},{8,10},{9,11},{10,... | collective-permute-start | bytes 294920 | tf_op jit(solution)/shard_map/ppermute | solution.py:240
  23.5 3.7 %collective-permute-start.9 = (bf16[16,128]{1,0:T(8,128)(2,1)S(1)}, bf16[16,128]{1,0:T(8,128)(2,1)S(1)}, u32[]{:S(2)}, u32[]{:S(2)}) collective-permute-start(bf16[16,128]{1,0:T(8,128)(2,1)S(1)} %get-tuple-element.33), channel_id=1, source_target_pairs={{0,16},{1,17},{2,18},{3,19},{4,20},{5,21},{6,22},{7,23},{8,24},{9,... | collective-permute-start | bytes 12296 | tf_op jit(solution)/shard_map/ppermute | solution.py:240
  25.1 16.6 %copy-start = (s32[1,128,8]{1,2,0:T(8,128)S(1)}, s32[1,128,8]{1,2,0:T(8,128)}, u32[]{:S(2)}) copy-start(s32[1,128,8]{1,2,0:T(8,128)} %param.9) | copy-start | bytes 12292
  27.2 4.8 %collective-permute-start.10 = (bf16[32,1664]{1,0:T(8,128)(2,1)S(1)}, bf16[32,1664]{1,0:T(8,128)(2,1)S(1)}, u32[]{:S(2)}, u32[]{:S(2)}) collective-permute-start(bf16[32,1664]{1,0:T(8,128)(2,1)S(1)} %get-tuple-element.40), channel_id=1, source_target_pairs={{0,2},{1,3},{2,0},{3,1},{4,6},{5,7},{6,4},{7,5},{8,10},{9,11},{10,... | collective-permute-start | bytes 319496 | tf_op jit(solution)/shard_map/ppermute | solution.py:240
  28.8 6.3 %collective-permute-start.13 = (bf16[32,1664]{1,0:T(8,128)(2,1)S(1)}, bf16[32,1664]{1,0:T(8,128)(2,1)S(1)}, u32[]{:S(2)}, u32[]{:S(2)}) collective-permute-start(bf16[32,1664]{1,0:T(8,128)(2,1)S(1)} %get-tuple-element.45), channel_id=1, source_target_pairs={{0,2},{1,3},{2,0},{3,1},{4,6},{5,7},{6,4},{7,5},{8,10},{9,11},{10,... | collective-permute-start | bytes 319496 | tf_op jit(solution)/shard_map/ppermute | solution.py:240
  32.0 8.2 %collective-permute-start.11 = (bf16[32,1664]{1,0:T(8,128)(2,1)S(1)}, bf16[32,1664]{1,0:T(8,128)(2,1)S(1)}, u32[]{:S(2)}, u32[]{:S(2)}) collective-permute-start(bf16[32,1664]{1,0:T(8,128)(2,1)S(1)} %add_inputs_back.2), channel_id=1, source_target_pairs={{0,24},{1,29},{2,26},{3,31},{4,28},{5,25},{6,30},{7,27},{8,16},{9,... | collective-permute-start | bytes 319496 | tf_op jit(solution)/shard_map/ppermute | solution.py:240
  35.2 5.1 %collective-permute-start.14 = (bf16[32,1664]{1,0:T(8,128)(2,1)S(1)}, bf16[32,1664]{1,0:T(8,128)(2,1)S(1)}, u32[]{:S(2)}, u32[]{:S(2)}) collective-permute-start(bf16[32,1664]{1,0:T(8,128)(2,1)S(1)} %add_inputs_back.3), channel_id=1, source_target_pairs={{0,16},{1,21},{2,18},{3,23},{4,20},{5,17},{6,22},{7,19},{8,24},{9,... | collective-permute-start | bytes 319496 | tf_op jit(solution)/shard_map/ppermute | solution.py:240
  35.9 4.4 %collective-permute-start.12 = (bf16[16,1024]{1,0:T(8,128)(2,1)S(1)}, bf16[16,1024]{1,0:T(8,128)(2,1)S(1)}, u32[]{:S(2)}, u32[]{:S(2)}) collective-permute-start(bf16[16,1024]{1,0:T(8,128)(2,1)S(1)} %get-tuple-element.41), channel_id=1, source_target_pairs={{0,16},{1,17},{2,18},{3,19},{4,20},{5,21},{6,22},{7,23},{8,24},{9,... | collective-permute-start | bytes 98312 | tf_op jit(solution)/shard_map/ppermute | solution.py:240
  40.3 1.4 %collective-permute-start.15 = (bf16[32,1664]{1,0:T(8,128)(2,1)S(1)}, bf16[32,1664]{1,0:T(8,128)(2,1)S(1)}, u32[]{:S(2)}, u32[]{:S(2)}) collective-permute-start(bf16[32,1664]{1,0:T(8,128)(2,1)S(1)} %other_core.1), channel_id=1, source_target_pairs={{0,1},{1,0},{2,3},{3,2},{4,5},{5,4},{6,7},{7,6},{8,9},{9,8},{10,11... | collective-permute-start | bytes 319496 | tf_op jit(solution)/shard_map/ppermute | solution.py:240

commit v6 on v5

--- a/solution.py
+++ b/solution.py
@@ -149,55 +149,57 @@
             total = total + lax.dot_general(left, right, nt, preferred_element_type=F32)
         pieces.append(total)
     last = pieces[-1]
-    each = outs[0].shape[0] // PAD
     for i in range(left_ref.shape[0] // CAP):
         base = i * CAP
-        out_ref, at = outs[i // each], i % each * PAD
+        out_ref, at = outs[i // 2], i % 2 * main
         for j, piece in enumerate(pieces[:-1]):
             under = last[base + extra * j : base + extra * (j + 1)]
             both = jnp.concatenate([piece[base : base + CAP], under], axis=0)
-            out_ref[at : at + PAD, j * step : (j + 1) * step] = both.astype(out_ref.dtype)
+            out_ref[:, at + j * step : at + (j + 1) * step] = both.astype(out_ref.dtype)
 
 
 def attach_kernel(part_ref, *refs):
-    outs = refs[len(refs) // 2 :]
     part = part_ref[...].astype(F32)
     lane = lax.broadcasted_iota(jnp.int32, part.shape, 1)
-    each = outs[0].shape[0] // PAD
-    for i in range(len(outs) * each):
-        out_ref, at = outs[i // each], i % each * PAD
-        tail = jnp.where(lane // 2 == i, part, 0.0)
-        out_ref[at : at + PAD, out_ref.shape[1] - LANES :] = tail.astype(out_ref.dtype)
+    for i, out_ref in enumerate(refs[len(refs) // 2 :]):
+        tail = jnp.where(lane // 4 == i, part, 0.0)
+        out_ref[:, out_ref.shape[1] - LANES :] = tail.astype(out_ref.dtype)
 
 
 def add_kernel(keep_ref, got_ref, out_ref):
-    main = keep_ref.shape[1] - LANES
+    both = keep_ref.shape[1] - LANES
     lane = lax.broadcasted_iota(jnp.int32, (PAD, LANES), 1)
-    for i in range(2):
-        rows = pl.ds(i * PAD, PAD)
-        total = keep_ref[rows] + got_ref[rows].astype(F32)
-        out_ref[rows, :main] = total[:, :main].astype(BF)
-        high, low = split(jnp.sum(total[:, main:], axis=1, keepdims=True))
-        tail = jnp.where(lane == 0, high.astype(F32), jnp.where(lane == 1, low.astype(F32), 0.0))
-        out_ref[rows, main:] = tail.astype(BF)
+    total = keep_ref[...] + got_ref[...].astype(F32)
+    out_ref[:, :both] = total[:, :both].astype(BF)
+    tail = jnp.zeros((PAD, LANES), F32)
+    for o in range(2):
+        mine = jnp.where(lane // 2 % 2 == o, total[:, both:], 0.0)
+        high, low = split(jnp.sum(mine, axis=1, keepdims=True))
+        tail = jnp.where(lane == 2 * o, high.astype(F32), tail)
+        tail = jnp.where(lane == 2 * o + 1, low.astype(F32), tail)
+    out_ref[:, both:] = tail.astype(BF)
 
 
 def other_kernel(*refs):
     half = len(refs) - 1
+    main = refs[-1].shape[1] - LANES
     for k, ref in zip(reversed(range(half)), refs):
-        refs[-1][k * PAD : (k + 1) * PAD] = ref[PAD:]
+        refs[-1][k * PAD : (k + 1) * PAD] = ref[:, main:]
 
 
 def mix_kernel(flight, ids_ref, place_ref, mix_ref, near_ref, *refs):
     half = flight // 2
     home, (out_ref, gates_ref) = refs[:half], refs[half:]
     home = home[::-1]
-    blocks = []
-    for k in range(half):
-        blocks += [home[k].at[pl.ds(0, PAD)], near_ref.at[pl.ds(k * PAD, PAD)]]
+    blocks, tails = [], []
     count, width = out_ref.shape
     main = width * CAP // PAD
     step = width - main
+    lane = lax.broadcasted_iota(jnp.int32, (PAD, LANES), 1)
+    for k in range(half):
+        near = near_ref.at[pl.ds(k * PAD, PAD)]
+        blocks += [home[k], near]
+        tails += [jnp.where(lane // 2 == o, v[...].astype(F32), 0.0) for o, v in enumerate((home[k].at[:, pl.ds(2 * main, LANES)], near.at[:, pl.ds(main, LANES)]))]
     tn = (((0,), (0,)), ((), ()))
     left = jnp.concatenate(
         [
@@ -225,7 +227,7 @@
     ids = ids_ref[...]
     total = jnp.zeros(ids.shape, F32)
     for s in range(flight):
-        q = jnp.sum(blocks[s][:, main:].astype(F32), axis=1, keepdims=True)
+        q = jnp.sum(tails[s], axis=1, keepdims=True)
         back = jnp.sum(place_ref[s * PAD : (s + 1) * PAD] * q, axis=0, keepdims=True)
         total = total + jnp.where(ids == (own ^ s ^ parity), back, 0.0)
     gates_ref[...] = total
@@ -290,7 +292,7 @@
         name="hidden",
     )(*[rows[i] for i in order], pack, near)
     part = go(part, flip=1, bits=0, along=None)
-    r_shapes = [shape((2 * PAD, main + LANES), t) for t in [F32] * half + [BF] * half]
+    r_shapes = [shape((PAD, 2 * main + LANES), t) for t in [F32] * half + [BF] * half]
     r_sums = pl.pallas_call(
         inputs_kernel,
         out_shape=r_shapes,
@@ -309,7 +311,7 @@
         r_got = go(r_sums[half + k], flip=0, bits=2, along=None)
         r_part = pl.pallas_call(
             add_kernel,
-            out_shape=shape((2 * PAD, main + LANES), BF),
+            out_shape=shape((PAD, 2 * main + LANES), BF),
             compiler_params=PARAMS,
             name="add_inputs_back",
         )(r_sums[k], r_got)

time: 43 us -> 42.9 us (level)
  no operation moved by 1% of the time
where the time goes in v6:
time: 42.9 us; the launch traced here: 42.6 us
  starting transfers between devices  21.4 us (50%)
  waiting for transfers between devices  14 us (33%)
  Pallas kernels  6.53 us (15%)
  between operations  0.69 us (2%)
    ppermute x16, starting transfers between devices, moved(): return lax.ppermute(value, stage, route)  21.4 us
    ppermute x16, waiting for transfers between devices, moved(): return lax.ppermute(value, stage, route)  14 us
    pallas_call x1, Pallas kernels, per_device(): pl.pallas_call(functools.partial(select_kernel, flight), out_shape=[shape...  2.28 us
    pallas_call x1, Pallas kernels, per_device(): pl.pallas_call(functools.partial(hidden_kernel, order), out_shape=[shape(...  1.52 us
    pallas_call x1, Pallas kernels, per_device(): pl.pallas_call(inputs_kernel, out_shape=r_shapes, compiler_params=PARAMS,...  1.39 us
    pallas_call x1, Pallas kernels, per_device(): pl.pallas_call(functools.partial(mix_kernel, flight), out_shape=[shape((c...  1.13 us
  transfers between devices with their start and end apart: 16, of which 8 were waited for; matrix products, arithmetic and copies ran while one was open for 0% of the time, Pallas kernels for 4%

profile of v6, /device:TPU:0, one launch (start us, length us, event | category | flops | bytes accessed | tf_op | source)
XLA Modules:
  0.0 42.6 jit_solution(8950016999383946135)
XLA Ops:
  0.6 2.3 %select.1 = (bf16[24,2048]{1,0:T(8,128)(2,1)S(1)}, bf16[24,2048]{1,0:T(8,128)(2,1)S(1)}, bf16[24,2048]{1,0:T(8,128)(2,1)S(1)}, bf16[24,2048]{1,0:T(8,128)(2,1)S(...) custom-call(s32[8,128]{1,0:T(8,128)} %bitcast.15, f32[8,128]{1,0:T(8,128)} %bitcast.22, ...), custom_call_target="tpu_custom_call" | custom-call | tf_op jit(solution)/shard_map/select/pallas_call | solution.py:259
  2.9 0.5 %collective-permute-start.2 = (bf16[6144,256]{1,0:T(8,128)(2,1)S(1)}, bf16[6144,256]{1,0:T(8,128)(2,1)S(1)}, u32[]{:S(2)}, u32[]{:S(2)}) collective-permute-start(bf16[6144,256]{1,0:T(8,128)(2,1)S(1)} %get-tuple-element.28.refs_8_.own_ref), channel_id=1, source_target_pairs={{0,1},{1,0},{2,3},{3,2},{4,5},{5,4},{6,7},{7,6},{8,9},{9,8},{10,11... | collective-permute-start | bytes 9437192 | tf_op jit(solution)/shard_map/ppermute | solution.py:242
  3.4 2.7 %collective-permute-start = (bf16[24,2048]{1,0:T(8,128)(2,1)S(1)}, bf16[24,2048]{1,0:T(8,128)(2,1)S(1)}, u32[]{:S(2)}, u32[]{:S(2)}) collective-permute-start(bf16[24,2048]{1,0:T(8,128)(2,1)S(1)} %get-tuple-element.26), channel_id=1, source_target_pairs={{0,5},{1,0},{2,7},{3,2},{4,1},{5,4},{6,3},{7,6},{8,13},{9,8},{10,1... | collective-permute-start | bytes 294920 | tf_op jit(solution)/shard_map/ppermute | solution.py:242
  6.1 2.6 %collective-permute-start.3 = (bf16[24,2048]{1,0:T(8,128)(2,1)S(1)}, bf16[24,2048]{1,0:T(8,128)(2,1)S(1)}, u32[]{:S(2)}, u32[]{:S(2)}) collective-permute-start(bf16[24,2048]{1,0:T(8,128)(2,1)S(1)} %get-tuple-element.30), channel_id=1, source_target_pairs={{0,8},{1,13},{2,10},{3,15},{4,12},{5,9},{6,14},{7,11},{8,0},{9,5},... | collective-permute-start | bytes 294920 | tf_op jit(solution)/shard_map/ppermute | solution.py:242
  8.7 0.7 %collective-permute-start.4 = (bf16[24,2048]{1,0:T(8,128)(2,1)S(1)}, bf16[24,2048]{1,0:T(8,128)(2,1)S(1)}, u32[]{:S(2)}, u32[]{:S(2)}) collective-permute-start(bf16[24,2048]{1,0:T(8,128)(2,1)S(1)} %get-tuple-element.31), channel_id=1, source_target_pairs={{0,0},{1,5},{2,2},{3,7},{4,4},{5,1},{6,6},{7,3},{8,8},{9,13},{10,1... | collective-permute-start | bytes 294920 | tf_op jit(solution)/shard_map/ppermute | solution.py:242
  9.4 1.1 %collective-permute-start.1 = (bf16[24,2048]{1,0:T(8,128)(2,1)S(1)}, bf16[24,2048]{1,0:T(8,128)(2,1)S(1)}, u32[]{:S(2)}, u32[]{:S(2)}) collective-permute-start(bf16[24,2048]{1,0:T(8,128)(2,1)S(1)} %get-tuple-element.27), channel_id=1, source_target_pairs={{0,13},{1,8},{2,15},{3,10},{4,9},{5,12},{6,11},{7,14},{8,5},{9,0},... | collective-permute-start | bytes 294920 | tf_op jit(solution)/shard_map/ppermute | solution.py:242
  10.5 1.5 %collective-permute-start.5 = (bf16[24,2048]{1,0:T(8,128)(2,1)S(1)}, bf16[24,2048]{1,0:T(8,128)(2,1)S(1)}, u32[]{:S(2)}, u32[]{:S(2)}) collective-permute-start(bf16[24,2048]{1,0:T(8,128)(2,1)S(1)} %collective-permute-done.refs_0_), channel_id=1, source_target_pairs={{0,2},{1,3},{2,0},{3,1},{4,6},{5,7},{6,4},{7,5},{8,10},{9,11},{10,... | collective-permute-start | bytes 294920 | tf_op jit(solution)/shard_map/ppermute | solution.py:242
  12.2 1.5 %collective-permute-start.8 = (bf16[24,2048]{1,0:T(8,128)(2,1)S(1)}, bf16[24,2048]{1,0:T(8,128)(2,1)S(1)}, u32[]{:S(2)}, u32[]{:S(2)}) collective-permute-start(bf16[24,2048]{1,0:T(8,128)(2,1)S(1)} %collective-permute-done.3.refs_2_), channel_id=1, source_target_pairs={{0,2},{1,3},{2,0},{3,1},{4,6},{5,7},{6,4},{7,5},{8,10},{9,11},{10,... | collective-permute-start | bytes 294920 | tf_op jit(solution)/shard_map/ppermute | solution.py:242
  14.3 3.1 %collective-permute-done.1.refs_1_ = bf16[24,2048]{1,0:T(8,128)(2,1)S(1)} collective-permute-done((bf16[24,2048]{1,0:T(8,128)(2,1)S(1)}, bf16[24,2048]{1,0:T(8,128)(2,1)S(1)}, u32[]{:S(2)}, u32[]{:S(2)}) %collective-permute-start.1) | collective-permute-done | bytes 98336 | tf_op jit(solution)/shard_map/ppermute | solution.py:242
  17.4 1.5 %collective-permute-start.7 = (bf16[24,2048]{1,0:T(8,128)(2,1)S(1)}, bf16[24,2048]{1,0:T(8,128)(2,1)S(1)}, u32[]{:S(2)}, u32[]{:S(2)}) collective-permute-start(bf16[24,2048]{1,0:T(8,128)(2,1)S(1)} %collective-permute-done.1.refs_1_), channel_id=1, source_target_pairs={{0,2},{1,3},{2,0},{3,1},{4,6},{5,7},{6,4},{7,5},{8,10},{9,11},{10,... | collective-permute-start | bytes 294920 | tf_op jit(solution)/shard_map/ppermute | solution.py:242
  18.9 0.8 %collective-permute-done.6.refs_5_ = bf16[24,2048]{1,0:T(8,128)(2,1)S(1)} collective-permute-done((bf16[24,2048]{1,0:T(8,128)(2,1)S(1)}, bf16[24,2048]{1,0:T(8,128)(2,1)S(1)}, u32[]{:S(2)}, u32[]{:S(2)}) %collective-permute-start.6) | collective-permute-done | bytes 98336 | tf_op jit(solution)/shard_map/ppermute | solution.py:242
  19.7 2.3 %collective-permute-done.7.refs_6_ = bf16[24,2048]{1,0:T(8,128)(2,1)S(1)} collective-permute-done((bf16[24,2048]{1,0:T(8,128)(2,1)S(1)}, bf16[24,2048]{1,0:T(8,128)(2,1)S(1)}, u32[]{:S(2)}, u32[]{:S(2)}) %collective-permute-start.7) | collective-permute-done | bytes 98336 | tf_op jit(solution)/shard_map/ppermute | solution.py:242
  22.0 1.5 %hidden.1 = (bf16[96,1024]{1,0:T(8,128)(2,1)S(1)}, bf16[16,128]{1,0:T(8,128)(2,1)S(1)}) custom-call(bf16[24,2048]{1,0:T(8,128)(2,1)S(1)} %collective-permute-done.refs_0_, bf16[24,2048]{1,0:T(8,128)(2,1)S(1)} %collective-permute-done.1.refs_1_, bf16[24,2048]{1,0:T(8,128)(2,1)S(1)} %collective-permute-done.3.refs_2_, ...), custom_call_target="tpu_custom_call" | custom-call | tf_op jit(solution)/shard_map/hidden/pallas_call | solution.py:288
  23.5 1.6 %collective-permute-start.9 = (bf16[16,128]{1,0:T(8,128)(2,1)S(1)}, bf16[16,128]{1,0:T(8,128)(2,1)S(1)}, u32[]{:S(2)}, u32[]{:S(2)}) collective-permute-start(bf16[16,128]{1,0:T(8,128)(2,1)S(1)} %get-tuple-element.33), channel_id=1, source_target_pairs={{0,16},{1,17},{2,18},{3,19},{4,20},{5,21},{6,22},{7,23},{8,24},{9,... | collective-permute-start | bytes 12296 | tf_op jit(solution)/shard_map/ppermute | solution.py:242
  25.1 1.4 %inputs_back.1 = (f32[16,3200]{1,0:T(8,128)S(1)}, f32[16,3200]{1,0:T(8,128)S(1)}, bf16[16,3200]{1,0:T(8,128)(2,1)S(1)}, bf16[16,3200]{1,0:T(8,128)(2,1)S(1)}) custom-call(bf16[96,1024]{1,0:T(8,128)(2,1)S(1)} %get-tuple-element.34.left_ref, bf16[6144,256]{1,0:T(8,128)(2,1)S(1)} %get-tuple-element.28.refs_8_.own_ref, ...), custom_call_target="tpu_custom_call" | custom-call | tf_op jit(solution)/shard_map/inputs_back/pallas_call | solution.py:296
  26.5 0.7 %collective-permute-done.9.part_ref = bf16[16,128]{1,0:T(8,128)(2,1)S(1)} collective-permute-done((bf16[16,128]{1,0:T(8,128)(2,1)S(1)}, bf16[16,128]{1,0:T(8,128)(2,1)S(1)}, u32[]{:S(2)}, u32[]{:S(2)}) %collective-permute-start.9) | collective-permute-done | bytes 4128 | tf_op jit(solution)/shard_map/ppermute | solution.py:242
  27.2 1.6 %collective-permute-start.10 = (bf16[16,3200]{1,0:T(8,128)(2,1)S(1)}, bf16[16,3200]{1,0:T(8,128)(2,1)S(1)}, u32[]{:S(2)}, u32[]{:S(2)}) collective-permute-start(bf16[16,3200]{1,0:T(8,128)(2,1)S(1)} %get-tuple-element.40), channel_id=1, source_target_pairs={{0,2},{1,3},{2,0},{3,1},{4,6},{5,7},{6,4},{7,5},{8,10},{9,11},{10,... | collective-permute-start | bytes 307208 | tf_op jit(solution)/shard_map/ppermute | solution.py:242
  29.3 2.6 %collective-permute-done.10.got_ref = bf16[16,3200]{1,0:T(8,128)(2,1)S(1)} collective-permute-done((bf16[16,3200]{1,0:T(8,128)(2,1)S(1)}, bf16[16,3200]{1,0:T(8,128)(2,1)S(1)}, u32[]{:S(2)}, u32[]{:S(2)}) %collective-permute-start.10) | collective-permute-done | bytes 102432 | tf_op jit(solution)/shard_map/ppermute | solution.py:242
  32.0 3.0 %collective-permute-start.11 = (bf16[16,3200]{1,0:T(8,128)(2,1)S(1)}, bf16[16,3200]{1,0:T(8,128)(2,1)S(1)}, u32[]{:S(2)}, u32[]{:S(2)}) collective-permute-start(bf16[16,3200]{1,0:T(8,128)(2,1)S(1)} %add_inputs_back.2), channel_id=1, source_target_pairs={{0,24},{1,29},{2,26},{3,31},{4,28},{5,25},{6,30},{7,27},{8,16},{9,... | collective-permute-start | bytes 307208 | tf_op jit(solution)/shard_map/ppermute | solution.py:242
  35.1 0.7 %collective-permute-start.14 = (bf16[16,3200]{1,0:T(8,128)(2,1)S(1)}, bf16[16,3200]{1,0:T(8,128)(2,1)S(1)}, u32[]{:S(2)}, u32[]{:S(2)}) collective-permute-start(bf16[16,3200]{1,0:T(8,128)(2,1)S(1)} %add_inputs_back.3), channel_id=1, source_target_pairs={{0,16},{1,21},{2,18},{3,23},{4,20},{5,17},{6,22},{7,19},{8,24},{9,... | collective-permute-start | bytes 307208 | tf_op jit(solution)/shard_map/ppermute | solution.py:242
  35.8 1.3 %collective-permute-start.12 = (bf16[16,1024]{1,0:T(8,128)(2,1)S(1)}, bf16[16,1024]{1,0:T(8,128)(2,1)S(1)}, u32[]{:S(2)}, u32[]{:S(2)}) collective-permute-start(bf16[16,1024]{1,0:T(8,128)(2,1)S(1)} %get-tuple-element.41), channel_id=1, source_target_pairs={{0,16},{1,17},{2,18},{3,19},{4,20},{5,21},{6,22},{7,23},{8,24},{9,... | collective-permute-start | bytes 98312 | tf_op jit(solution)/shard_map/ppermute | solution.py:242
  37.1 3.0 %collective-permute-done.12.mix_ref = bf16[16,1024]{1,0:T(8,128)(2,1)S(1)} collective-permute-done((bf16[16,1024]{1,0:T(8,128)(2,1)S(1)}, bf16[16,1024]{1,0:T(8,128)(2,1)S(1)}, u32[]{:S(2)}, u32[]{:S(2)}) %collective-permute-start.12) | collective-permute-done | bytes 32800 | tf_op jit(solution)/shard_map/ppermute | solution.py:242
  40.2 1.3 %collective-permute-done.15.near_ref = bf16[32,1664]{1,0:T(8,128)(2,1)S(1)} collective-permute-done((bf16[32,1664]{1,0:T(8,128)(2,1)S(1)}, bf16[32,1664]{1,0:T(8,128)(2,1)S(1)}, u32[]{:S(2)}, u32[]{:S(2)}) %collective-permute-start.15) | collective-permute-done | bytes 106528 | tf_op jit(solution)/shard_map/ppermute | solution.py:242
  41.5 1.1 %mix.1 = (bf16[128,2048]{1,0:T(8,128)(2,1)}, f32[8,128]{1,0:T(8,128)}) custom-call(s32[8,128]{1,0:T(8,128)S(1)} %bitcast.16, f32[64,128]{1,0:T(8,128)S(1)} %get-tuple-element.25.place_ref, bf16[16,1024]{1,0:T(8,128)(2,1)S(1)} %collective-permute-done.12.mix_ref, bf16[32,1664]{1,0:T(8,128)(2,1)S(1)} %collective-permute-done.15.near_ref, ...), custom_call_target="tpu_custom_call" | custom-call | tf_op jit(solution)/shard_map/mix/pallas_call | solution.py:328
  (18 shorter events, 1.5 us)
Async XLA Ops:
  2.9 14.4 %collective-permute-start.2 = (bf16[6144,256]{1,0:T(8,128)(2,1)S(1)}, bf16[6144,256]{1,0:T(8,128)(2,1)S(1)}, u32[]{:S(2)}, u32[]{:S(2)}) collective-permute-start(bf16[6144,256]{1,0:T(8,128)(2,1)S(1)} %get-tuple-element.28.refs_8_.own_ref), channel_id=1, source_target_pairs={{0,1},{1,0},{2,3},{3,2},{4,5},{5,4},{6,7},{7,6},{8,9},{9,8},{10,11... | collective-permute-start | bytes 9437192 | tf_op jit(solution)/shard_map/ppermute | solution.py:242
  3.4 7.1 %collective-permute-start = (bf16[24,2048]{1,0:T(8,128)(2,1)S(1)}, bf16[24,2048]{1,0:T(8,128)(2,1)S(1)}, u32[]{:S(2)}, u32[]{:S(2)}) collective-permute-start(bf16[24,2048]{1,0:T(8,128)(2,1)S(1)} %get-tuple-element.26), channel_id=1, source_target_pairs={{0,5},{1,0},{2,7},{3,2},{4,1},{5,4},{6,3},{7,6},{8,13},{9,8},{10,1... | collective-permute-start | bytes 294920 | tf_op jit(solution)/shard_map/ppermute | solution.py:242
  6.1 6.1 %collective-permute-start.3 = (bf16[24,2048]{1,0:T(8,128)(2,1)S(1)}, bf16[24,2048]{1,0:T(8,128)(2,1)S(1)}, u32[]{:S(2)}, u32[]{:S(2)}) collective-permute-start(bf16[24,2048]{1,0:T(8,128)(2,1)S(1)} %get-tuple-element.30), channel_id=1, source_target_pairs={{0,8},{1,13},{2,10},{3,15},{4,12},{5,9},{6,14},{7,11},{8,0},{9,5},... | collective-permute-start | bytes 294920 | tf_op jit(solution)/shard_map/ppermute | solution.py:242
  8.7 5.0 %collective-permute-start.4 = (bf16[24,2048]{1,0:T(8,128)(2,1)S(1)}, bf16[24,2048]{1,0:T(8,128)(2,1)S(1)}, u32[]{:S(2)}, u32[]{:S(2)}) collective-permute-start(bf16[24,2048]{1,0:T(8,128)(2,1)S(1)} %get-tuple-element.31), channel_id=1, source_target_pairs={{0,0},{1,5},{2,2},{3,7},{4,4},{5,1},{6,6},{7,3},{8,8},{9,13},{10,1... | collective-permute-start | bytes 294920 | tf_op jit(solution)/shard_map/ppermute | solution.py:242
  9.4 8.0 %collective-permute-start.1 = (bf16[24,2048]{1,0:T(8,128)(2,1)S(1)}, bf16[24,2048]{1,0:T(8,128)(2,1)S(1)}, u32[]{:S(2)}, u32[]{:S(2)}) collective-permute-start(bf16[24,2048]{1,0:T(8,128)(2,1)S(1)} %get-tuple-element.27), channel_id=1, source_target_pairs={{0,13},{1,8},{2,15},{3,10},{4,9},{5,12},{6,11},{7,14},{8,5},{9,0},... | collective-permute-start | bytes 294920 | tf_op jit(solution)/shard_map/ppermute | solution.py:242
  10.5 8.4 %collective-permute-start.5 = (bf16[24,2048]{1,0:T(8,128)(2,1)S(1)}, bf16[24,2048]{1,0:T(8,128)(2,1)S(1)}, u32[]{:S(2)}, u32[]{:S(2)}) collective-permute-start(bf16[24,2048]{1,0:T(8,128)(2,1)S(1)} %collective-permute-done.refs_0_), channel_id=1, source_target_pairs={{0,2},{1,3},{2,0},{3,1},{4,6},{5,7},{6,4},{7,5},{8,10},{9,11},{10,... | collective-permute-start | bytes 294920 | tf_op jit(solution)/shard_map/ppermute | solution.py:242
  12.2 6.6 %collective-permute-start.8 = (bf16[24,2048]{1,0:T(8,128)(2,1)S(1)}, bf16[24,2048]{1,0:T(8,128)(2,1)S(1)}, u32[]{:S(2)}, u32[]{:S(2)}) collective-permute-start(bf16[24,2048]{1,0:T(8,128)(2,1)S(1)} %collective-permute-done.3.refs_2_), channel_id=1, source_target_pairs={{0,2},{1,3},{2,0},{3,1},{4,6},{5,7},{6,4},{7,5},{8,10},{9,11},{10,... | collective-permute-start | bytes 294920 | tf_op jit(solution)/shard_map/ppermute | solution.py:242
  13.8 5.9 %collective-permute-start.6 = (bf16[24,2048]{1,0:T(8,128)(2,1)S(1)}, bf16[24,2048]{1,0:T(8,128)(2,1)S(1)}, u32[]{:S(2)}, u32[]{:S(2)}) collective-permute-start(bf16[24,2048]{1,0:T(8,128)(2,1)S(1)} %collective-permute-done.4.refs_3_), channel_id=1, source_target_pairs={{0,2},{1,3},{2,0},{3,1},{4,6},{5,7},{6,4},{7,5},{8,10},{9,11},{10,... | collective-permute-start | bytes 294920 | tf_op jit(solution)/shard_map/ppermute | solution.py:242
  17.4 4.6 %collective-permute-start.7 = (bf16[24,2048]{1,0:T(8,128)(2,1)S(1)}, bf16[24,2048]{1,0:T(8,128)(2,1)S(1)}, u32[]{:S(2)}, u32[]{:S(2)}) collective-permute-start(bf16[24,2048]{1,0:T(8,128)(2,1)S(1)} %collective-permute-done.1.refs_1_), channel_id=1, source_target_pairs={{0,2},{1,3},{2,0},{3,1},{4,6},{5,7},{6,4},{7,5},{8,10},{9,11},{10,... | collective-permute-start | bytes 294920 | tf_op jit(solution)/shard_map/ppermute | solution.py:242
  23.5 3.7 %collective-permute-start.9 = (bf16[16,128]{1,0:T(8,128)(2,1)S(1)}, bf16[16,128]{1,0:T(8,128)(2,1)S(1)}, u32[]{:S(2)}, u32[]{:S(2)}) collective-permute-start(bf16[16,128]{1,0:T(8,128)(2,1)S(1)} %get-tuple-element.33), channel_id=1, source_target_pairs={{0,16},{1,17},{2,18},{3,19},{4,20},{5,21},{6,22},{7,23},{8,24},{9,... | collective-permute-start | bytes 12296 | tf_op jit(solution)/shard_map/ppermute | solution.py:242
  25.1 16.5 %copy-start = (s32[1,128,8]{1,2,0:T(8,128)S(1)}, s32[1,128,8]{1,2,0:T(8,128)}, u32[]{:S(2)}) copy-start(s32[1,128,8]{1,2,0:T(8,128)} %param.9) | copy-start | bytes 12292
  27.2 4.7 %collective-permute-start.10 = (bf16[16,3200]{1,0:T(8,128)(2,1)S(1)}, bf16[16,3200]{1,0:T(8,128)(2,1)S(1)}, u32[]{:S(2)}, u32[]{:S(2)}) collective-permute-start(bf16[16,3200]{1,0:T(8,128)(2,1)S(1)} %get-tuple-element.40), channel_id=1, source_target_pairs={{0,2},{1,3},{2,0},{3,1},{4,6},{5,7},{6,4},{7,5},{8,10},{9,11},{10,... | collective-permute-start | bytes 307208 | tf_op jit(solution)/shard_map/ppermute | solution.py:242
  28.8 6.2 %collective-permute-start.13 = (bf16[16,3200]{1,0:T(8,128)(2,1)S(1)}, bf16[16,3200]{1,0:T(8,128)(2,1)S(1)}, u32[]{:S(2)}, u32[]{:S(2)}) collective-permute-start(bf16[16,3200]{1,0:T(8,128)(2,1)S(1)} %get-tuple-element.45), channel_id=1, source_target_pairs={{0,2},{1,3},{2,0},{3,1},{4,6},{5,7},{6,4},{7,5},{8,10},{9,11},{10,... | collective-permute-start | bytes 307208 | tf_op jit(solution)/shard_map/ppermute | solution.py:242
  32.0 8.1 %collective-permute-start.11 = (bf16[16,3200]{1,0:T(8,128)(2,1)S(1)}, bf16[16,3200]{1,0:T(8,128)(2,1)S(1)}, u32[]{:S(2)}, u32[]{:S(2)}) collective-permute-start(bf16[16,3200]{1,0:T(8,128)(2,1)S(1)} %add_inputs_back.2), channel_id=1, source_target_pairs={{0,24},{1,29},{2,26},{3,31},{4,28},{5,25},{6,30},{7,27},{8,16},{9,... | collective-permute-start | bytes 307208 | tf_op jit(solution)/shard_map/ppermute | solution.py:242
  35.1 5.0 %collective-permute-start.14 = (bf16[16,3200]{1,0:T(8,128)(2,1)S(1)}, bf16[16,3200]{1,0:T(8,128)(2,1)S(1)}, u32[]{:S(2)}, u32[]{:S(2)}) collective-permute-start(bf16[16,3200]{1,0:T(8,128)(2,1)S(1)} %add_inputs_back.3), channel_id=1, source_target_pairs={{0,16},{1,21},{2,18},{3,23},{4,20},{5,17},{6,22},{7,19},{8,24},{9,... | collective-permute-start | bytes 307208 | tf_op jit(solution)/shard_map/ppermute | solution.py:242
  35.8 4.3 %collective-permute-start.12 = (bf16[16,1024]{1,0:T(8,128)(2,1)S(1)}, bf16[16,1024]{1,0:T(8,128)(2,1)S(1)}, u32[]{:S(2)}, u32[]{:S(2)}) collective-permute-start(bf16[16,1024]{1,0:T(8,128)(2,1)S(1)} %get-tuple-element.41), channel_id=1, source_target_pairs={{0,16},{1,17},{2,18},{3,19},{4,20},{5,21},{6,22},{7,23},{8,24},{9,... | collective-permute-start | bytes 98312 | tf_op jit(solution)/shard_map/ppermute | solution.py:242
  40.1 1.4 %collective-permute-start.15 = (bf16[32,1664]{1,0:T(8,128)(2,1)S(1)}, bf16[32,1664]{1,0:T(8,128)(2,1)S(1)}, u32[]{:S(2)}, u32[]{:S(2)}) collective-permute-start(bf16[32,1664]{1,0:T(8,128)(2,1)S(1)} %other_core.1), channel_id=1, source_target_pairs={{0,1},{1,0},{2,3},{3,2},{4,5},{5,4},{6,7},{7,6},{8,9},{9,8},{10,11... | collective-permute-start | bytes 319496 | tf_op jit(solution)/shard_map/ppermute | solution.py:242

commit v7 on v6

--- a/solution.py
+++ b/solution.py
@@ -189,7 +189,7 @@
 
 def mix_kernel(flight, ids_ref, place_ref, mix_ref, near_ref, *refs):
     half = flight // 2
-    home, (out_ref, gates_ref) = refs[:half], refs[half:]
+    home, (out_hbm, gates_ref, out_ref, sems) = refs[:half], refs[half:]
     home = home[::-1]
     blocks, tails = [], []
     count, width = out_ref.shape
@@ -214,14 +214,23 @@
         right = jnp.concatenate([rows, rows], axis=0)
         return lax.dot_general(left, right, tn, preferred_element_type=F32).astype(BF)
 
-    out_ref[:, :main] = blend(jnp.concatenate([b[:, :main] for b in blocks], axis=0))
+    copies = []
+
+    def store(rows, at):
+        cols = pl.ds(at, step)
+        out_ref[:, cols] = blend(rows)
+        copies.append(pltpu.make_async_copy(out_ref.at[:, cols], out_hbm.at[:, cols], sems.at[at // step]))
+        copies[-1].start()
+
+    for c in range(0, main, step):
+        store(jnp.concatenate([b[:, c : c + step] for b in blocks], axis=0), c)
     zero = jnp.zeros((PAD - CAP, step), BF)
     folded = []
     for s in range(flight):
         for j in range(main // step):
             folded.append(blocks[s][CAP:, j * step : (j + 1) * step])
         folded.append(zero)
-    out_ref[:, main:] = blend(jnp.concatenate(folded, axis=0))
+    store(jnp.concatenate(folded, axis=0), main)
     own = lax.axis_index("expert") // SLICES
     parity = lax.axis_index("expert") % 2
     ids = ids_ref[...]
@@ -231,6 +240,8 @@
         back = jnp.sum(place_ref[s * PAD : (s + 1) * PAD] * q, axis=0, keepdims=True)
         total = total + jnp.where(ids == (own ^ s ^ parity), back, 0.0)
     gates_ref[...] = total
+    for copy in copies:
+        copy.wait()
 
 
 def moved(value, sections, devices, stage, flip, bits, along=0):
@@ -328,6 +339,11 @@
     moe, d_gates = pl.pallas_call(
         functools.partial(mix_kernel, flight),
         out_shape=[shape((count, width), BF), shape(ids.shape, F32)],
+        out_specs=[*hbm, pl.BlockSpec(memory_space=pltpu.VMEM)],
+        scratch_shapes=[
+            pltpu.VMEM((count, width), BF),
+            pltpu.SemaphoreType.DMA((width // (width - main),)),
+        ],
         compiler_params=PARAMS,
         name="mix",
     )(ids, place, far_mix, r_near, *r_home[::-1])

time: 42.9 us -> 43.4 us (1.012)
  Pallas kernels: 6.53 us -> 7.04 us
    pallas_call x1, Pallas kernels: 1.13 us -> 1.64 us  [per_device(): pl.pallas_call(functools.partial(mix_kernel, flight), out_shape=[shape((c...]
where the time goes in v7:
time: 43.4 us; the launch traced here: 43.1 us
  starting transfers between devices  21.4 us (49%)
  waiting for transfers between devices  14 us (32%)
  Pallas kernels  7.04 us (16%)
  between operations  0.69 us (2%)
    ppermute x16, starting transfers between devices, moved(): return lax.ppermute(value, stage, route)  21.4 us
    ppermute x16, waiting for transfers between devices, moved(): return lax.ppermute(value, stage, route)  14 us
    pallas_call x1, Pallas kernels, per_device(): pl.pallas_call(functools.partial(select_kernel, flight), out_shape=[shape...  2.28 us
    pallas_call x1, Pallas kernels, per_device(): pl.pallas_call(functools.partial(mix_kernel, flight), out_shape=[shape((c...  1.64 us
    pallas_call x1, Pallas kernels, per_device(): pl.pallas_call(functools.partial(hidden_kernel, order), out_shape=[shape(...  1.52 us
    pallas_call x1, Pallas kernels, per_device(): pl.pallas_call(inputs_kernel, out_shape=r_shapes, compiler_params=PARAMS,...  1.39 us
  transfers between devices with their start and end apart: 16, of which 8 were waited for; matrix products, arithmetic and copies ran while one was open for 0% of the time, Pallas kernels for 4%

profile of v7, /device:TPU:0, one launch (start us, length us, event | category | flops | bytes accessed | tf_op | source)
XLA Modules:
  0.0 43.1 jit_solution(9517313024629963379)
XLA Ops:
  0.6 2.3 %select.1 = (bf16[24,2048]{1,0:T(8,128)(2,1)S(1)}, bf16[24,2048]{1,0:T(8,128)(2,1)S(1)}, bf16[24,2048]{1,0:T(8,128)(2,1)S(1)}, bf16[24,2048]{1,0:T(8,128)(2,1)S(...) custom-call(s32[8,128]{1,0:T(8,128)} %bitcast.15, f32[8,128]{1,0:T(8,128)} %bitcast.22, ...), custom_call_target="tpu_custom_call" | custom-call | tf_op jit(solution)/shard_map/select/pallas_call | solution.py:270
  2.9 0.5 %collective-permute-start.2 = (bf16[6144,256]{1,0:T(8,128)(2,1)S(1)}, bf16[6144,256]{1,0:T(8,128)(2,1)S(1)}, u32[]{:S(2)}, u32[]{:S(2)}) collective-permute-start(bf16[6144,256]{1,0:T(8,128)(2,1)S(1)} %get-tuple-element.28.refs_8_.own_ref), channel_id=1, source_target_pairs={{0,1},{1,0},{2,3},{3,2},{4,5},{5,4},{6,7},{7,6},{8,9},{9,8},{10,11... | collective-permute-start | bytes 9437192 | tf_op jit(solution)/shard_map/ppermute | solution.py:253
  3.4 2.7 %collective-permute-start = (bf16[24,2048]{1,0:T(8,128)(2,1)S(1)}, bf16[24,2048]{1,0:T(8,128)(2,1)S(1)}, u32[]{:S(2)}, u32[]{:S(2)}) collective-permute-start(bf16[24,2048]{1,0:T(8,128)(2,1)S(1)} %get-tuple-element.26), channel_id=1, source_target_pairs={{0,5},{1,0},{2,7},{3,2},{4,1},{5,4},{6,3},{7,6},{8,13},{9,8},{10,1... | collective-permute-start | bytes 294920 | tf_op jit(solution)/shard_map/ppermute | solution.py:253
  6.1 2.6 %collective-permute-start.3 = (bf16[24,2048]{1,0:T(8,128)(2,1)S(1)}, bf16[24,2048]{1,0:T(8,128)(2,1)S(1)}, u32[]{:S(2)}, u32[]{:S(2)}) collective-permute-start(bf16[24,2048]{1,0:T(8,128)(2,1)S(1)} %get-tuple-element.30), channel_id=1, source_target_pairs={{0,8},{1,13},{2,10},{3,15},{4,12},{5,9},{6,14},{7,11},{8,0},{9,5},... | collective-permute-start | bytes 294920 | tf_op jit(solution)/shard_map/ppermute | solution.py:253
  8.7 0.7 %collective-permute-start.4 = (bf16[24,2048]{1,0:T(8,128)(2,1)S(1)}, bf16[24,2048]{1,0:T(8,128)(2,1)S(1)}, u32[]{:S(2)}, u32[]{:S(2)}) collective-permute-start(bf16[24,2048]{1,0:T(8,128)(2,1)S(1)} %get-tuple-element.31), channel_id=1, source_target_pairs={{0,0},{1,5},{2,2},{3,7},{4,4},{5,1},{6,6},{7,3},{8,8},{9,13},{10,1... | collective-permute-start | bytes 294920 | tf_op jit(solution)/shard_map/ppermute | solution.py:253
  9.4 1.1 %collective-permute-start.1 = (bf16[24,2048]{1,0:T(8,128)(2,1)S(1)}, bf16[24,2048]{1,0:T(8,128)(2,1)S(1)}, u32[]{:S(2)}, u32[]{:S(2)}) collective-permute-start(bf16[24,2048]{1,0:T(8,128)(2,1)S(1)} %get-tuple-element.27), channel_id=1, source_target_pairs={{0,13},{1,8},{2,15},{3,10},{4,9},{5,12},{6,11},{7,14},{8,5},{9,0},... | collective-permute-start | bytes 294920 | tf_op jit(solution)/shard_map/ppermute | solution.py:253
  10.5 1.5 %collective-permute-start.5 = (bf16[24,2048]{1,0:T(8,128)(2,1)S(1)}, bf16[24,2048]{1,0:T(8,128)(2,1)S(1)}, u32[]{:S(2)}, u32[]{:S(2)}) collective-permute-start(bf16[24,2048]{1,0:T(8,128)(2,1)S(1)} %collective-permute-done.refs_0_), channel_id=1, source_target_pairs={{0,2},{1,3},{2,0},{3,1},{4,6},{5,7},{6,4},{7,5},{8,10},{9,11},{10,... | collective-permute-start | bytes 294920 | tf_op jit(solution)/shard_map/ppermute | solution.py:253
  12.2 1.5 %collective-permute-start.8 = (bf16[24,2048]{1,0:T(8,128)(2,1)S(1)}, bf16[24,2048]{1,0:T(8,128)(2,1)S(1)}, u32[]{:S(2)}, u32[]{:S(2)}) collective-permute-start(bf16[24,2048]{1,0:T(8,128)(2,1)S(1)} %collective-permute-done.3.refs_2_), channel_id=1, source_target_pairs={{0,2},{1,3},{2,0},{3,1},{4,6},{5,7},{6,4},{7,5},{8,10},{9,11},{10,... | collective-permute-start | bytes 294920 | tf_op jit(solution)/shard_map/ppermute | solution.py:253
  14.3 3.1 %collective-permute-done.1.refs_1_ = bf16[24,2048]{1,0:T(8,128)(2,1)S(1)} collective-permute-done((bf16[24,2048]{1,0:T(8,128)(2,1)S(1)}, bf16[24,2048]{1,0:T(8,128)(2,1)S(1)}, u32[]{:S(2)}, u32[]{:S(2)}) %collective-permute-start.1) | collective-permute-done | bytes 98336 | tf_op jit(solution)/shard_map/ppermute | solution.py:253
  17.4 1.5 %collective-permute-start.7 = (bf16[24,2048]{1,0:T(8,128)(2,1)S(1)}, bf16[24,2048]{1,0:T(8,128)(2,1)S(1)}, u32[]{:S(2)}, u32[]{:S(2)}) collective-permute-start(bf16[24,2048]{1,0:T(8,128)(2,1)S(1)} %collective-permute-done.1.refs_1_), channel_id=1, source_target_pairs={{0,2},{1,3},{2,0},{3,1},{4,6},{5,7},{6,4},{7,5},{8,10},{9,11},{10,... | collective-permute-start | bytes 294920 | tf_op jit(solution)/shard_map/ppermute | solution.py:253
  18.9 0.8 %collective-permute-done.6.refs_5_ = bf16[24,2048]{1,0:T(8,128)(2,1)S(1)} collective-permute-done((bf16[24,2048]{1,0:T(8,128)(2,1)S(1)}, bf16[24,2048]{1,0:T(8,128)(2,1)S(1)}, u32[]{:S(2)}, u32[]{:S(2)}) %collective-permute-start.6) | collective-permute-done | bytes 98336 | tf_op jit(solution)/shard_map/ppermute | solution.py:253
  19.7 2.3 %collective-permute-done.7.refs_6_ = bf16[24,2048]{1,0:T(8,128)(2,1)S(1)} collective-permute-done((bf16[24,2048]{1,0:T(8,128)(2,1)S(1)}, bf16[24,2048]{1,0:T(8,128)(2,1)S(1)}, u32[]{:S(2)}, u32[]{:S(2)}) %collective-permute-start.7) | collective-permute-done | bytes 98336 | tf_op jit(solution)/shard_map/ppermute | solution.py:253
  22.0 1.5 %hidden.1 = (bf16[96,1024]{1,0:T(8,128)(2,1)S(1)}, bf16[16,128]{1,0:T(8,128)(2,1)S(1)}) custom-call(bf16[24,2048]{1,0:T(8,128)(2,1)S(1)} %collective-permute-done.refs_0_, bf16[24,2048]{1,0:T(8,128)(2,1)S(1)} %collective-permute-done.1.refs_1_, bf16[24,2048]{1,0:T(8,128)(2,1)S(1)} %collective-permute-done.3.refs_2_, ...), custom_call_target="tpu_custom_call" | custom-call | tf_op jit(solution)/shard_map/hidden/pallas_call | solution.py:299
  23.5 1.6 %collective-permute-start.9 = (bf16[16,128]{1,0:T(8,128)(2,1)S(1)}, bf16[16,128]{1,0:T(8,128)(2,1)S(1)}, u32[]{:S(2)}, u32[]{:S(2)}) collective-permute-start(bf16[16,128]{1,0:T(8,128)(2,1)S(1)} %get-tuple-element.33), channel_id=1, source_target_pairs={{0,16},{1,17},{2,18},{3,19},{4,20},{5,21},{6,22},{7,23},{8,24},{9,... | collective-permute-start | bytes 12296 | tf_op jit(solution)/shard_map/ppermute | solution.py:253
  25.1 1.4 %inputs_back.1 = (f32[16,3200]{1,0:T(8,128)S(1)}, f32[16,3200]{1,0:T(8,128)S(1)}, bf16[16,3200]{1,0:T(8,128)(2,1)S(1)}, bf16[16,3200]{1,0:T(8,128)(2,1)S(1)}) custom-call(bf16[96,1024]{1,0:T(8,128)(2,1)S(1)} %get-tuple-element.34.left_ref, bf16[6144,256]{1,0:T(8,128)(2,1)S(1)} %get-tuple-element.28.refs_8_.own_ref, ...), custom_call_target="tpu_custom_call" | custom-call | tf_op jit(solution)/shard_map/inputs_back/pallas_call | solution.py:307
  26.5 0.7 %collective-permute-done.9.part_ref = bf16[16,128]{1,0:T(8,128)(2,1)S(1)} collective-permute-done((bf16[16,128]{1,0:T(8,128)(2,1)S(1)}, bf16[16,128]{1,0:T(8,128)(2,1)S(1)}, u32[]{:S(2)}, u32[]{:S(2)}) %collective-permute-start.9) | collective-permute-done | bytes 4128 | tf_op jit(solution)/shard_map/ppermute | solution.py:253
  27.2 1.6 %collective-permute-start.10 = (bf16[16,3200]{1,0:T(8,128)(2,1)S(1)}, bf16[16,3200]{1,0:T(8,128)(2,1)S(1)}, u32[]{:S(2)}, u32[]{:S(2)}) collective-permute-start(bf16[16,3200]{1,0:T(8,128)(2,1)S(1)} %get-tuple-element.40), channel_id=1, source_target_pairs={{0,2},{1,3},{2,0},{3,1},{4,6},{5,7},{6,4},{7,5},{8,10},{9,11},{10,... | collective-permute-start | bytes 307208 | tf_op jit(solution)/shard_map/ppermute | solution.py:253
  29.3 2.6 %collective-permute-done.10.got_ref = bf16[16,3200]{1,0:T(8,128)(2,1)S(1)} collective-permute-done((bf16[16,3200]{1,0:T(8,128)(2,1)S(1)}, bf16[16,3200]{1,0:T(8,128)(2,1)S(1)}, u32[]{:S(2)}, u32[]{:S(2)}) %collective-permute-start.10) | collective-permute-done | bytes 102432 | tf_op jit(solution)/shard_map/ppermute | solution.py:253
  32.0 3.0 %collective-permute-start.11 = (bf16[16,3200]{1,0:T(8,128)(2,1)S(1)}, bf16[16,3200]{1,0:T(8,128)(2,1)S(1)}, u32[]{:S(2)}, u32[]{:S(2)}) collective-permute-start(bf16[16,3200]{1,0:T(8,128)(2,1)S(1)} %add_inputs_back.2), channel_id=1, source_target_pairs={{0,24},{1,29},{2,26},{3,31},{4,28},{5,25},{6,30},{7,27},{8,16},{9,... | collective-permute-start | bytes 307208 | tf_op jit(solution)/shard_map/ppermute | solution.py:253
  35.1 0.7 %collective-permute-start.14 = (bf16[16,3200]{1,0:T(8,128)(2,1)S(1)}, bf16[16,3200]{1,0:T(8,128)(2,1)S(1)}, u32[]{:S(2)}, u32[]{:S(2)}) collective-permute-start(bf16[16,3200]{1,0:T(8,128)(2,1)S(1)} %add_inputs_back.3), channel_id=1, source_target_pairs={{0,16},{1,21},{2,18},{3,23},{4,20},{5,17},{6,22},{7,19},{8,24},{9,... | collective-permute-start | bytes 307208 | tf_op jit(solution)/shard_map/ppermute | solution.py:253
  35.8 1.3 %collective-permute-start.12 = (bf16[16,1024]{1,0:T(8,128)(2,1)S(1)}, bf16[16,1024]{1,0:T(8,128)(2,1)S(1)}, u32[]{:S(2)}, u32[]{:S(2)}) collective-permute-start(bf16[16,1024]{1,0:T(8,128)(2,1)S(1)} %get-tuple-element.41), channel_id=1, source_target_pairs={{0,16},{1,17},{2,18},{3,19},{4,20},{5,21},{6,22},{7,23},{8,24},{9,... | collective-permute-start | bytes 98312 | tf_op jit(solution)/shard_map/ppermute | solution.py:253
  37.1 3.0 %collective-permute-done.12.mix_ref = bf16[16,1024]{1,0:T(8,128)(2,1)S(1)} collective-permute-done((bf16[16,1024]{1,0:T(8,128)(2,1)S(1)}, bf16[16,1024]{1,0:T(8,128)(2,1)S(1)}, u32[]{:S(2)}, u32[]{:S(2)}) %collective-permute-start.12) | collective-permute-done | bytes 32800 | tf_op jit(solution)/shard_map/ppermute | solution.py:253
  40.2 1.3 %collective-permute-done.15.near_ref = bf16[32,1664]{1,0:T(8,128)(2,1)S(1)} collective-permute-done((bf16[32,1664]{1,0:T(8,128)(2,1)S(1)}, bf16[32,1664]{1,0:T(8,128)(2,1)S(1)}, u32[]{:S(2)}, u32[]{:S(2)}) %collective-permute-start.15) | collective-permute-done | bytes 106528 | tf_op jit(solution)/shard_map/ppermute | solution.py:253
  41.5 1.6 %mix.1 = (bf16[128,2048]{1,0:T(8,128)(2,1)}, f32[8,128]{1,0:T(8,128)}) custom-call(s32[8,128]{1,0:T(8,128)S(1)} %bitcast.16, f32[64,128]{1,0:T(8,128)S(1)} %get-tuple-element.25.place_ref, bf16[16,1024]{1,0:T(8,128)(2,1)S(1)} %collective-permute-done.12.mix_ref, bf16[32,1664]{1,0:T(8,128)(2,1)S(1)} %collective-permute-done.15.near_ref, ...), custom_call_target="tpu_custom_call" | custom-call | tf_op jit(solution)/shard_map/mix/pallas_call | solution.py:339
  (18 shorter events, 1.5 us)
Async XLA Ops:
  2.9 14.4 %collective-permute-start.2 = (bf16[6144,256]{1,0:T(8,128)(2,1)S(1)}, bf16[6144,256]{1,0:T(8,128)(2,1)S(1)}, u32[]{:S(2)}, u32[]{:S(2)}) collective-permute-start(bf16[6144,256]{1,0:T(8,128)(2,1)S(1)} %get-tuple-element.28.refs_8_.own_ref), channel_id=1, source_target_pairs={{0,1},{1,0},{2,3},{3,2},{4,5},{5,4},{6,7},{7,6},{8,9},{9,8},{10,11... | collective-permute-start | bytes 9437192 | tf_op jit(solution)/shard_map/ppermute | solution.py:253
  3.4 7.1 %collective-permute-start = (bf16[24,2048]{1,0:T(8,128)(2,1)S(1)}, bf16[24,2048]{1,0:T(8,128)(2,1)S(1)}, u32[]{:S(2)}, u32[]{:S(2)}) collective-permute-start(bf16[24,2048]{1,0:T(8,128)(2,1)S(1)} %get-tuple-element.26), channel_id=1, source_target_pairs={{0,5},{1,0},{2,7},{3,2},{4,1},{5,4},{6,3},{7,6},{8,13},{9,8},{10,1... | collective-permute-start | bytes 294920 | tf_op jit(solution)/shard_map/ppermute | solution.py:253
  6.1 6.1 %collective-permute-start.3 = (bf16[24,2048]{1,0:T(8,128)(2,1)S(1)}, bf16[24,2048]{1,0:T(8,128)(2,1)S(1)}, u32[]{:S(2)}, u32[]{:S(2)}) collective-permute-start(bf16[24,2048]{1,0:T(8,128)(2,1)S(1)} %get-tuple-element.30), channel_id=1, source_target_pairs={{0,8},{1,13},{2,10},{3,15},{4,12},{5,9},{6,14},{7,11},{8,0},{9,5},... | collective-permute-start | bytes 294920 | tf_op jit(solution)/shard_map/ppermute | solution.py:253
  8.7 5.0 %collective-permute-start.4 = (bf16[24,2048]{1,0:T(8,128)(2,1)S(1)}, bf16[24,2048]{1,0:T(8,128)(2,1)S(1)}, u32[]{:S(2)}, u32[]{:S(2)}) collective-permute-start(bf16[24,2048]{1,0:T(8,128)(2,1)S(1)} %get-tuple-element.31), channel_id=1, source_target_pairs={{0,0},{1,5},{2,2},{3,7},{4,4},{5,1},{6,6},{7,3},{8,8},{9,13},{10,1... | collective-permute-start | bytes 294920 | tf_op jit(solution)/shard_map/ppermute | solution.py:253
  9.4 8.0 %collective-permute-start.1 = (bf16[24,2048]{1,0:T(8,128)(2,1)S(1)}, bf16[24,2048]{1,0:T(8,128)(2,1)S(1)}, u32[]{:S(2)}, u32[]{:S(2)}) collective-permute-start(bf16[24,2048]{1,0:T(8,128)(2,1)S(1)} %get-tuple-element.27), channel_id=1, source_target_pairs={{0,13},{1,8},{2,15},{3,10},{4,9},{5,12},{6,11},{7,14},{8,5},{9,0},... | collective-permute-start | bytes 294920 | tf_op jit(solution)/shard_map/ppermute | solution.py:253
  10.5 8.4 %collective-permute-start.5 = (bf16[24,2048]{1,0:T(8,128)(2,1)S(1)}, bf16[24,2048]{1,0:T(8,128)(2,1)S(1)}, u32[]{:S(2)}, u32[]{:S(2)}) collective-permute-start(bf16[24,2048]{1,0:T(8,128)(2,1)S(1)} %collective-permute-done.refs_0_), channel_id=1, source_target_pairs={{0,2},{1,3},{2,0},{3,1},{4,6},{5,7},{6,4},{7,5},{8,10},{9,11},{10,... | collective-permute-start | bytes 294920 | tf_op jit(solution)/shard_map/ppermute | solution.py:253
  12.2 6.6 %collective-permute-start.8 = (bf16[24,2048]{1,0:T(8,128)(2,1)S(1)}, bf16[24,2048]{1,0:T(8,128)(2,1)S(1)}, u32[]{:S(2)}, u32[]{:S(2)}) collective-permute-start(bf16[24,2048]{1,0:T(8,128)(2,1)S(1)} %collective-permute-done.3.refs_2_), channel_id=1, source_target_pairs={{0,2},{1,3},{2,0},{3,1},{4,6},{5,7},{6,4},{7,5},{8,10},{9,11},{10,... | collective-permute-start | bytes 294920 | tf_op jit(solution)/shard_map/ppermute | solution.py:253
  13.8 5.9 %collective-permute-start.6 = (bf16[24,2048]{1,0:T(8,128)(2,1)S(1)}, bf16[24,2048]{1,0:T(8,128)(2,1)S(1)}, u32[]{:S(2)}, u32[]{:S(2)}) collective-permute-start(bf16[24,2048]{1,0:T(8,128)(2,1)S(1)} %collective-permute-done.4.refs_3_), channel_id=1, source_target_pairs={{0,2},{1,3},{2,0},{3,1},{4,6},{5,7},{6,4},{7,5},{8,10},{9,11},{10,... | collective-permute-start | bytes 294920 | tf_op jit(solution)/shard_map/ppermute | solution.py:253
  17.4 4.6 %collective-permute-start.7 = (bf16[24,2048]{1,0:T(8,128)(2,1)S(1)}, bf16[24,2048]{1,0:T(8,128)(2,1)S(1)}, u32[]{:S(2)}, u32[]{:S(2)}) collective-permute-start(bf16[24,2048]{1,0:T(8,128)(2,1)S(1)} %collective-permute-done.1.refs_1_), channel_id=1, source_target_pairs={{0,2},{1,3},{2,0},{3,1},{4,6},{5,7},{6,4},{7,5},{8,10},{9,11},{10,... | collective-permute-start | bytes 294920 | tf_op jit(solution)/shard_map/ppermute | solution.py:253
  23.5 3.7 %collective-permute-start.9 = (bf16[16,128]{1,0:T(8,128)(2,1)S(1)}, bf16[16,128]{1,0:T(8,128)(2,1)S(1)}, u32[]{:S(2)}, u32[]{:S(2)}) collective-permute-start(bf16[16,128]{1,0:T(8,128)(2,1)S(1)} %get-tuple-element.33), channel_id=1, source_target_pairs={{0,16},{1,17},{2,18},{3,19},{4,20},{5,21},{6,22},{7,23},{8,24},{9,... | collective-permute-start | bytes 12296 | tf_op jit(solution)/shard_map/ppermute | solution.py:253
  25.1 16.5 %copy-start = (s32[1,128,8]{1,2,0:T(8,128)S(1)}, s32[1,128,8]{1,2,0:T(8,128)}, u32[]{:S(2)}) copy-start(s32[1,128,8]{1,2,0:T(8,128)} %param.9) | copy-start | bytes 12292
  27.2 4.7 %collective-permute-start.10 = (bf16[16,3200]{1,0:T(8,128)(2,1)S(1)}, bf16[16,3200]{1,0:T(8,128)(2,1)S(1)}, u32[]{:S(2)}, u32[]{:S(2)}) collective-permute-start(bf16[16,3200]{1,0:T(8,128)(2,1)S(1)} %get-tuple-element.40), channel_id=1, source_target_pairs={{0,2},{1,3},{2,0},{3,1},{4,6},{5,7},{6,4},{7,5},{8,10},{9,11},{10,... | collective-permute-start | bytes 307208 | tf_op jit(solution)/shard_map/ppermute | solution.py:253
  28.8 6.2 %collective-permute-start.13 = (bf16[16,3200]{1,0:T(8,128)(2,1)S(1)}, bf16[16,3200]{1,0:T(8,128)(2,1)S(1)}, u32[]{:S(2)}, u32[]{:S(2)}) collective-permute-start(bf16[16,3200]{1,0:T(8,128)(2,1)S(1)} %get-tuple-element.45), channel_id=1, source_target_pairs={{0,2},{1,3},{2,0},{3,1},{4,6},{5,7},{6,4},{7,5},{8,10},{9,11},{10,... | collective-permute-start | bytes 307208 | tf_op jit(solution)/shard_map/ppermute | solution.py:253
  32.0 8.1 %collective-permute-start.11 = (bf16[16,3200]{1,0:T(8,128)(2,1)S(1)}, bf16[16,3200]{1,0:T(8,128)(2,1)S(1)}, u32[]{:S(2)}, u32[]{:S(2)}) collective-permute-start(bf16[16,3200]{1,0:T(8,128)(2,1)S(1)} %add_inputs_back.2), channel_id=1, source_target_pairs={{0,24},{1,29},{2,26},{3,31},{4,28},{5,25},{6,30},{7,27},{8,16},{9,... | collective-permute-start | bytes 307208 | tf_op jit(solution)/shard_map/ppermute | solution.py:253
  35.1 5.0 %collective-permute-start.14 = (bf16[16,3200]{1,0:T(8,128)(2,1)S(1)}, bf16[16,3200]{1,0:T(8,128)(2,1)S(1)}, u32[]{:S(2)}, u32[]{:S(2)}) collective-permute-start(bf16[16,3200]{1,0:T(8,128)(2,1)S(1)} %add_inputs_back.3), channel_id=1, source_target_pairs={{0,16},{1,21},{2,18},{3,23},{4,20},{5,17},{6,22},{7,19},{8,24},{9,... | collective-permute-start | bytes 307208 | tf_op jit(solution)/shard_map/ppermute | solution.py:253
  35.8 4.3 %collective-permute-start.12 = (bf16[16,1024]{1,0:T(8,128)(2,1)S(1)}, bf16[16,1024]{1,0:T(8,128)(2,1)S(1)}, u32[]{:S(2)}, u32[]{:S(2)}) collective-permute-start(bf16[16,1024]{1,0:T(8,128)(2,1)S(1)} %get-tuple-element.41), channel_id=1, source_target_pairs={{0,16},{1,17},{2,18},{3,19},{4,20},{5,21},{6,22},{7,23},{8,24},{9,... | collective-permute-start | bytes 98312 | tf_op jit(solution)/shard_map/ppermute | solution.py:253
  40.1 1.4 %collective-permute-start.15 = (bf16[32,1664]{1,0:T(8,128)(2,1)S(1)}, bf16[32,1664]{1,0:T(8,128)(2,1)S(1)}, u32[]{:S(2)}, u32[]{:S(2)}) collective-permute-start(bf16[32,1664]{1,0:T(8,128)(2,1)S(1)} %other_core.1), channel_id=1, source_target_pairs={{0,1},{1,0},{2,3},{3,2},{4,5},{5,4},{6,7},{7,6},{8,9},{9,8},{10,11... | collective-permute-start | bytes 319496 | tf_op jit(solution)/shard_map/ppermute | solution.py:253
